TPU v7x, 512 devices: a whole 4x8x8 slice. The times are simulated.
512 devices in a mesh: freq: 128 (over y, x_lo, z), tile: 4 (over x_hi, core).
Axes of the slice: x: 4 (x_hi: 2, x_lo: 2; x = x_hi * 2 + x_lo), y: 8, z: 8, core: 2. Of those that a mesh axis runs over, the one named last changes fastest.
Arguments:
- wavefield: bfloat16 [2, 128, 512, 512], P(None, None, 'freq', 'tile'), may hold values from -6 to 6
- slowness: bfloat16 [128, 512, 512], P('freq', 'tile'), may hold values from 0.69921875 to 1.3984375
- freq_ids: int32 [128], replicated, may hold values from 0 to 127, each once
- depth_owner: int32 [1], replicated, may hold values from 0 to 127
Outputs:
- wave_next: bfloat16 [2, 128, 512, 512], P(None, 'freq', 'tile')
- image: float32 [512, 512], P('tile', 'freq')
Inputs may be any that keep to these rules, and one draw needn't show every extreme that they name: `freq_ids`: each frequency number appears in exactly one slot.
All inputs are finite; a program needn't handle non-finite values.
Results may differ from a plain program's by a relative error of at most 0.0097.
Values may be sent and summed in bfloat16 or wider, within the bound.
No kernel may reach another device: no remote copies, remote signals or barrier semaphores. Data moves between devices by JAX's collectives and lax.ppermute only.
A program may use at most 64 MiB of HBM per device.

v0:
```python
import math

import jax
import jax.numpy as jnp
from jax import lax
from jax.sharding import PartitionSpec as P

depth_step = 0.5
omega_top = 2.8


def spread(x, axis, root):
    mine = lax.axis_index(axis) == root
    return lax.psum(jnp.where(mine, x, jnp.zeros_like(x)), axis)


def dft_table(length):
    places = jnp.arange(length, dtype=jnp.int32)
    product = places[:, None] * places[None, :] % length
    angles = 2.0 * math.pi / length * product.astype(jnp.float32)
    factor = 1.0 / math.sqrt(length)
    return (
        (jnp.cos(angles) * factor).astype(jnp.bfloat16),
        (jnp.sin(angles) * factor).astype(jnp.bfloat16),
    )


def wavenumbers(length):
    places = jnp.arange(length, dtype=jnp.int32)
    signed = jnp.where(places < length // 2, places, places - length)
    return 2.0 * math.pi / length * signed.astype(jnp.float32)


def right_product(field, table):
    return jnp.dot(field, table, preferred_element_type=jnp.float32)


def left_product(table, field):
    return jnp.einsum("px,fxq->fpq", table, field, preferred_element_type=jnp.float32)


def local(wavefield, slowness, freq_ids, depth_owner):
    tiles = lax.all_to_all(wavefield, "freq", split_axis=1, concat_axis=2, tiled=True)
    rows = lax.all_to_all(tiles, "tile", split_axis=2, concat_axis=3, tiled=True)
    slot_count = rows.shape[1]
    total_slots = freq_ids.shape[0]
    own_ids = lax.dynamic_slice_in_dim(freq_ids, lax.axis_index("freq") * slot_count, slot_count)
    angular = omega_top * (own_ids + 1).astype(jnp.float32) / total_slots
    slowness_now = spread(slowness, "freq", depth_owner[0])[0].astype(jnp.float32)
    phase = angular[:, None, None] * depth_step * (slowness_now[None] - 1.0)
    lens_cos = jnp.cos(phase)
    lens_sin = jnp.sin(phase)
    wave_real = rows[0].astype(jnp.float32)
    wave_imag = rows[1].astype(jnp.float32)
    lensed_real = (wave_real * lens_cos - wave_imag * lens_sin).astype(jnp.bfloat16)
    lensed_imag = (wave_real * lens_sin + wave_imag * lens_cos).astype(jnp.bfloat16)
    width_y = rows.shape[3]
    ycos, ysin = dft_table(width_y)
    half_real = right_product(lensed_real, ycos) + right_product(lensed_imag, ysin)
    half_imag = right_product(lensed_imag, ycos) - right_product(lensed_real, ysin)
    half = jnp.stack([half_real, half_imag]).astype(jnp.bfloat16)
    columns = lax.all_to_all(half, "tile", split_axis=3, concat_axis=2, tiled=True)
    width_x = columns.shape[2]
    quarter = columns.shape[3]
    xcos, xsin = dft_table(width_x)
    spec_real = left_product(xcos, columns[0]) + left_product(xsin, columns[1])
    spec_imag = left_product(xcos, columns[1]) - left_product(xsin, columns[0])
    ky_values = lax.dynamic_slice_in_dim(
        wavenumbers(width_y), lax.axis_index("tile") * quarter, quarter
    )
    kx_square = (wavenumbers(width_x) ** 2)[None, :, None]
    ky_square = (ky_values**2)[None, None, :]
    vertical = (angular * angular)[:, None, None] - kx_square - ky_square
    travel = depth_step * jnp.sqrt(jnp.maximum(vertical, 0.0))
    damping = jnp.exp(-depth_step * jnp.sqrt(jnp.maximum(-vertical, 0.0)))
    shift_real = damping * jnp.cos(travel)
    shift_imag = damping * jnp.sin(travel)
    shifted_real = (spec_real * shift_real - spec_imag * shift_imag).astype(jnp.bfloat16)
    shifted_imag = (spec_real * shift_imag + spec_imag * shift_real).astype(jnp.bfloat16)
    back_real = left_product(xcos, shifted_real) - left_product(xsin, shifted_imag)
    back_imag = left_product(xcos, shifted_imag) + left_product(xsin, shifted_real)
    back = jnp.stack([back_real, back_imag]).astype(jnp.bfloat16)
    returned = lax.all_to_all(back, "tile", split_axis=2, concat_axis=3, tiled=True)
    field_real = right_product(returned[0], ycos) - right_product(returned[1], ysin)
    field_imag = right_product(returned[1], ycos) + right_product(returned[0], ysin)
    wave_next = jnp.stack([field_real, field_imag]).astype(jnp.bfloat16)
    partial_image = jnp.sum(field_real, axis=0) / math.sqrt(total_slots)
    summed = lax.psum(partial_image, "freq")
    columns_each = summed.shape[1] // lax.axis_size("freq")
    image = lax.dynamic_slice_in_dim(summed, lax.axis_index("freq") * columns_each, columns_each, 1)
    return (wave_next, image)


def solution(mesh):
    return jax.shard_map(
        local,
        mesh=mesh,
        in_specs=(P(None, None, "freq", "tile"), P("freq", "tile", None), P(), P()),
        out_specs=(P(None, "freq", "tile", None), P("tile", "freq")),
        check_vma=False,
    )
```

profile of v0, /device:TPU:20, one launch (start us, length us, event | category | flops | bytes accessed | tf_op | source)
XLA Modules:
  0.0 2225.8 jit_solution(11892665381434698050)
XLA Ops:
  7.2 1.7 copy.40
  8.9 18.1 all-to-all-start
  27.8 13.1 all-to-all-done
  41.0 1.0 copy.42
  42.0 4.8 all-to-all-start.1
  49.4 1.7 all-to-all-done.1
  51.5 1016.5 %all-reduce.3.cloned.1.call-done = bf16[1,128,512]{1,2,0:T(8,128)(2,1)} async-done(((bf16[1,128,512]{1,2,0:T(8,128)(2,1)}), bf16[1,128,512]{1,2,0:T(8,128)(2,1)}) %all-reduce.3.cloned.1.call-update) | async-done | bytes 131088 | tf_op jit(solution)/shard_map/psum | solution.py:14
  1068.0 1.9 fusion.37
  1069.9 4.2 fusion.25
  1074.1 4.2 fusion.24
  1078.3 4.6 fusion.11
  1083.0 4.6 fusion.10
  1087.6 0.9 copy.47
  1088.5 5.0 all-to-all-start.2
  1093.6 4.3 all-to-all-done.2
  1098.1 4.2 fusion.23
  1102.4 4.2 fusion.22
  1106.7 4.2 fusion.1
  1110.9 5.1 subtract_convert_fusion
  1116.0 4.7 fusion.21
  1120.7 4.2 fusion.20
  1124.9 4.6 fusion.9
  1129.5 4.6 fusion.8
  1134.1 0.9 copy.51
  1135.0 6.5 all-to-all-start.3
  1141.6 4.4 all-to-all-done.3
  1146.1 4.4 fusion.19
  1150.7 4.2 fusion.18
  1154.9 5.3 broadcast_multiply_fusion
  1160.2 4.6 fusion.7
  1165.5 1051.7 %all-reduce.5.cloned.1.call-done = f32[128,512]{1,0:T(8,128)} async-done(((f32[128,512]{1,0:T(8,128)}), f32[128,512]{1,0:T(8,128)}) %all-reduce.5.cloned.1.call-update) | async-done | bytes 262160 | tf_op jit(solution)/shard_map/psum | solution.py:88
  2217.2 0.9 constant_dynamic-slice_fusion
  (31 shorter events, 4.7 us)
Async XLA Ops:
  8.9 18.8 copy-start
  8.9 32.0 %all-to-all-start = ((bf16[2,128,4,128]{3,2,0,1:T(4,128)(2,1)}), bf16[2,128,4,128]{3,2,0,1:T(4,128)(2,1)S(1)}, u32[]{:S(2)}, u32[]{:S(2)}) async-start(bf16[2,128,4,128]{3,2,0,1:T(4,128)(2,1)} %copy.40), calls=%async_computation | async-start | bytes 524288 | tf_op jit(solution)/shard_map/all_to_all | solution.py:43
  42.0 9.2 all-to-all-start.1
  46.8 1021.2 %all-reduce.3.cloned.1.call-start = ((), (), s32[]{:S(2)}) async-start(), calls=%async_computation.4 | async-start | bytes 262144 | tf_op jit(solution)/shard_map/psum | solution.py:14
  47.5 0.7 copy-start.1
  1088.5 9.4 all-to-all-start.2
  1135.0 10.9 all-to-all-start.3
  1141.5 1075.7 %all-reduce.5.cloned.1.call-start = ((), (), s32[]{:S(2)}) async-start(), calls=%async_computation.5 | async-start | bytes 524288 | tf_op jit(solution)/shard_map/psum | solution.py:88
Sparse Core Ops, SparseCore 0:
  50.5 1017.4 all-reduce.2
  1160.3 1056.9 all-reduce.4
where the time goes:
time: 2230 us
  waiting for transfers between devices  2090 us (94%)
  matrix products  71.9 us (3%)
  starting transfers between devices  34.5 us (2%)
    psum x1, waiting for transfers between devices, local(): summed = lax.psum(partial_image, 'freq')  1050 us
    psum x1, waiting for transfers between devices, spread(): return lax.psum(jnp.where(mine, x, jnp.zeros_like(x)), axis)  1020 us
  transfers between devices with their start and end apart: 6, of which 6 were waited for; matrix products, arithmetic and copies ran while one was open for 0% of the time, Pallas kernels for 0%

commit v1 on v0

v1 whole, which is shorter than its diff:
```python
import math

import jax
import jax.numpy as jnp
import numpy as np
from jax import lax
from jax.experimental import pallas as pl
from jax.experimental.pallas import tpu as pltpu
from jax.sharding import Mesh
from jax.sharding import PartitionSpec as P

depth_step = 0.5
omega_top = 2.8
slots = 128
size = 512
tile_size = 128
freq = ("u", "v", "w", "z", "l")


def dft_table(length):
    places = np.arange(length)
    angles = 2.0 * np.pi / length * (places[:, None] * places[None, :] % length)
    factor = 1.0 / math.sqrt(length)
    return (
        (np.cos(angles) * factor).astype(jnp.bfloat16),
        (np.sin(angles) * factor).astype(jnp.bfloat16),
    )


def dot(left, right):
    return jnp.dot(left, right, preferred_element_type=jnp.float32)


def series(square, first, last):
    total = (-1.0) ** ((last - first) // 2) / math.factorial(last)
    for order in range(last - 2, first - 1, -2):
        total = (-1.0) ** ((order - first) // 2) / math.factorial(order) + square * total
    return total


def pick_kernel(owner_ref, rows_ref, out_ref):
    rows = rows_ref[owner_ref[0] // 2 % 16].astype(jnp.float32)
    for l in range(2):
        for c in range(2):
            lanes = (c * tile_size, (2 + c) * tile_size)
            piece = jnp.concatenate([rows[4 * l : 4 * l + 4, lane : lane + tile_size] for lane in lanes], axis=0)
            piece = piece.astype(jnp.bfloat16)
            for u in range(4):
                for h in range(2):
                    out_ref[((u * 2 + l) * 2 + h) * 2 + c] = piece


def shift_kernel(slot_ref, ids_ref, shift_ref):
    angular = omega_top * (ids_ref[slot_ref[0]] + 1).astype(jnp.float32) / slots

    def square(start, shape, axis):
        places = lax.broadcasted_iota(jnp.int32, shape, axis) + start
        signed = jnp.where(places < size // 2, places, places - size)
        return (2.0 * math.pi / size * signed.astype(jnp.float32)) ** 2

    ky_square = square(0, (16, size), 1)

    @pl.loop(0, size, step=16)
    def _(start):
        start = pl.multiple_of(start, 16)
        vertical = angular * angular - square(start, (16, size), 0) - ky_square
        root = depth_step * jnp.sqrt(jnp.abs(vertical))
        travel = jnp.where(vertical > 0.0, root, 0.0)
        damping = jnp.exp(jnp.where(vertical < 0.0, -root, 0.0))
        travel_square = travel * travel
        shift_ref[0, pl.ds(start, 16), :] = (damping * series(travel_square, 0, 12)).astype(jnp.bfloat16)
        shift_ref[1, pl.ds(start, 16), :] = (damping * travel * series(travel_square, 1, 13)).astype(jnp.bfloat16)


def pack_kernel(ids_ref, own_ref, other_ref, own_out, other_out, factor_ref):
    own_out[...] = own_ref[...]
    other_out[...] = other_ref[...]
    first = lax.broadcasted_iota(jnp.int32, (8, tile_size), 0) < 4
    for pair in range(slots // 2):
        low, high = (
            depth_step * (omega_top * (ids_ref[2 * pair + at] + 1).astype(jnp.float32) / slots) for at in range(2)
        )
        factor_ref[pair] = jnp.where(first, low, high)


def lens_kernel(place_ref, slow_ref, own_ref, other_ref, factor_ref, out_ref):
    slow = slow_ref[place_ref[0]].astype(jnp.float32) - 1.0
    halves = (jnp.concatenate([slow[:4]] * 2, axis=0), jnp.concatenate([slow[4:]] * 2, axis=0))
    low = place_ref[1] == 0
    depths = (jnp.where(low, halves[0], halves[1]), jnp.where(low, halves[1], halves[0]))
    for pair in range(slots // 2):
        factor = factor_ref[pair]
        for block, (ref, depth) in enumerate(zip((own_ref, other_ref), depths)):
            phase = factor * depth
            square = phase * phase
            lens_cos = series(square, 0, 8)
            lens_sin = phase * series(square, 1, 9)
            wave_real = ref[0, pair].astype(jnp.float32)
            wave_imag = ref[1, pair].astype(jnp.float32)
            real = wave_real * lens_cos - wave_imag * lens_sin
            imag = wave_real * lens_sin + wave_imag * lens_cos
            lanes = slice(block * tile_size, (block + 1) * tile_size)
            out_ref[2 * pair, :, lanes] = jnp.concatenate([real[:4], imag[:4]], axis=0).astype(jnp.bfloat16)
            out_ref[2 * pair + 1, :, lanes] = jnp.concatenate([real[4:], imag[4:]], axis=0).astype(jnp.bfloat16)


def column_kernel(cos_ref, sin_ref, wave_ref, out_ref, both):
    for at in range(0, size // 4, 4):
        tiles = [wave_ref[at + k].astype(jnp.float32) for k in range(4)]
        for part in range(2):
            rows = jnp.concatenate([tile[4 * part : 4 * part + 4] for tile in tiles], axis=0)
            both[4 * at : 4 * at + 16, part * 2 * tile_size : (part + 1) * 2 * tile_size] = rows.astype(jnp.bfloat16)
    by_cos = dot(cos_ref[...], both[...])
    by_sin = dot(sin_ref[...], both[...])
    real = (by_cos[:, : 2 * tile_size] + by_sin[:, 2 * tile_size :]).astype(jnp.bfloat16)
    imag = (by_cos[:, 2 * tile_size :] - by_sin[:, : 2 * tile_size]).astype(jnp.bfloat16)
    for block in range(2):
        lanes = slice(block * tile_size, (block + 1) * tile_size)
        out_ref[block, 0] = real[:, lanes]
        out_ref[block, 1] = imag[:, lanes]


def step_kernel(tile_ref, own_ref, other_ref, cos_ref, sin_ref, shift_ref, wave_ref, image_ref, field, back):
    tile = tile_ref[0]
    for flip in range(4):
        block = (own_ref, other_ref)[flip % 2]
        start = pl.multiple_of((tile ^ flip) * tile_size, tile_size)
        field[:, :, pl.ds(start, tile_size)] = block[flip // 2]
    rows = pl.ds(pl.multiple_of(tile * tile_size, tile_size), tile_size)
    inverse = jnp.concatenate([cos_ref[rows, :], sin_ref[rows, :]], axis=0)
    width = 256
    for at in range(0, size, width):
        part = slice(at, at + width)
        spec_real = dot(field[0], cos_ref[:, part]) + dot(field[1], sin_ref[:, part])
        spec_imag = dot(field[1], cos_ref[:, part]) - dot(field[0], sin_ref[:, part])
        shift_real = shift_ref[0, :, part].astype(jnp.float32)
        shift_imag = shift_ref[1, :, part].astype(jnp.float32)
        shifted_real = (spec_real * shift_real - spec_imag * shift_imag).astype(jnp.bfloat16)
        shifted_imag = (spec_real * shift_imag + spec_imag * shift_real).astype(jnp.bfloat16)
        from_real = dot(inverse, shifted_real)
        from_imag = dot(inverse, shifted_imag)
        back[:tile_size, part] = (from_real[:tile_size] - from_imag[tile_size:]).astype(jnp.bfloat16)
        back[tile_size:, part] = (from_imag[:tile_size] + from_real[tile_size:]).astype(jnp.bfloat16)
    for at in range(0, size, width):
        part = slice(at, at + width)
        by_cos = dot(back[...], cos_ref[:, part])
        by_sin = dot(back[...], sin_ref[:, part])
        field_real = by_cos[:tile_size] - by_sin[tile_size:]
        wave_ref[0, :, part] = field_real.astype(jnp.bfloat16)
        wave_ref[1, :, part] = (by_cos[tile_size:] + by_sin[:tile_size]).astype(jnp.bfloat16)
        image_ref[part, :] = (field_real * (1.0 / math.sqrt(slots))).T.astype(jnp.bfloat16)


def whole(memory=pltpu.VMEM):
    return pl.BlockSpec(memory_space=memory)


def exchange(x, axes):
    return lax.all_to_all(x, axes, split_axis=0, concat_axis=0, tiled=True)


def local(wavefield, slowness, freq_ids, depth_owner):
    owner = depth_owner[0]
    swap = [(0, 1), (1, 0)]
    side = lax.axis_index("h").astype(jnp.int32)
    tile = 2 * side + lax.axis_index("c").astype(jnp.int32)
    wavefield = wavefield.reshape(2, slots // 2, 8, tile_size)
    pieces = exchange(slowness.reshape(16, 8, size), ("v", "w", "z"))
    other = lax.ppermute(wavefield, "h", swap)
    pieces = pl.pallas_call(
        pick_kernel,
        out_shape=jax.ShapeDtypeStruct((32, 8, tile_size), jnp.bfloat16),
        in_specs=[whole(pltpu.SMEM), whole()],
        out_specs=whole(),
        compiler_params=pltpu.CompilerParams(vmem_limit_bytes=8 << 20),
        cost_estimate=pl.CostEstimate(flops=10_000, bytes_accessed=100_000, transcendentals=0),
    )(depth_owner, pieces)
    pieces = exchange(pieces, ("u", "l", "h", "c"))
    half = jax.ShapeDtypeStruct((2, slots // 2, 8, tile_size), jnp.bfloat16)
    own, other, factors = pl.pallas_call(
        pack_kernel,
        out_shape=(half, half, jax.ShapeDtypeStruct((slots // 2, 8, tile_size), jnp.float32)),
        in_specs=[whole(pltpu.SMEM)] + [whole()] * 2,
        out_specs=(whole(), whole(), whole()),
        compiler_params=pltpu.CompilerParams(vmem_limit_bytes=8 << 20),
        cost_estimate=pl.CostEstimate(flops=300_000, bytes_accessed=1_300_000, transcendentals=0),
    )(freq_ids, wavefield, other)
    place = (owner // 32 * 2 + owner % 2) * 4 + lax.axis_index("u").astype(jnp.int32)
    lensed = pl.pallas_call(
        lens_kernel,
        out_shape=jax.ShapeDtypeStruct((slots, 8, 2 * tile_size), jnp.bfloat16),
        in_specs=[whole(pltpu.SMEM)] + [whole()] * 4,
        out_specs=whole(),
        compiler_params=pltpu.CompilerParams(vmem_limit_bytes=8 << 20),
        cost_estimate=pl.CostEstimate(flops=6_000_000, bytes_accessed=1_300_000, transcendentals=0),
    )(jnp.stack([place, side]), pieces, own, other, factors)
    columns = exchange(lensed, freq)

    table_cos, table_sin = dft_table(size)
    shift = pl.pallas_call(
        shift_kernel,
        out_shape=jax.ShapeDtypeStruct((2, size, size), jnp.bfloat16),
        in_specs=[whole(pltpu.SMEM)] * 2,
        out_specs=whole(),
        compiler_params=pltpu.CompilerParams(vmem_limit_bytes=16 << 20),
        cost_estimate=pl.CostEstimate(flops=10_000_000, bytes_accessed=2_100_000, transcendentals=500_000),
    )(lax.axis_index(freq).astype(jnp.int32)[None], freq_ids)
    columns, shift = lax.optimization_barrier((columns, shift))

    table_cos, table_sin = jnp.asarray(table_cos), jnp.asarray(table_sin)
    own = pl.pallas_call(
        column_kernel,
        out_shape=jax.ShapeDtypeStruct((2, 2, size, tile_size), jnp.bfloat16),
        in_specs=[whole()] * 3,
        out_specs=whole(),
        scratch_shapes=[pltpu.VMEM((size, 4 * tile_size), jnp.bfloat16)],
        compiler_params=pltpu.CompilerParams(vmem_limit_bytes=8 << 20),
        cost_estimate=pl.CostEstimate(flops=540_000_000, bytes_accessed=2_100_000, transcendentals=0),
    )(table_cos, table_sin, columns)
    beside = lax.ppermute(own, "c", swap)
    wave_next, parts = pl.pallas_call(
        step_kernel,
        out_shape=(
            jax.ShapeDtypeStruct((2, tile_size, size), jnp.bfloat16),
            jax.ShapeDtypeStruct((size, tile_size), jnp.bfloat16),
        ),
        in_specs=[whole(pltpu.SMEM)] + [whole()] * 5,
        out_specs=(whole(), whole()),
        scratch_shapes=[
            pltpu.VMEM((2, size, size), jnp.bfloat16),
            pltpu.VMEM((2 * tile_size, size), jnp.bfloat16),
        ],
        compiler_params=pltpu.CompilerParams(vmem_limit_bytes=20 << 20),
        cost_estimate=pl.CostEstimate(flops=1_620_000_000, bytes_accessed=4_600_000, transcendentals=0),
    )(tile[None], own, beside, table_cos, table_sin, shift)
    parts = exchange(parts.reshape(slots, size // slots, tile_size), freq)
    image = jnp.sum(parts.astype(jnp.float32), axis=0).T
    return (wave_next[:, None], image)


def solution(mesh):
    grid = Mesh(mesh.devices.reshape(4, 2, 2, 4, 2, 2, 2), freq + ("h", "c"))
    tile = ("h", "c")
    return jax.shard_map(
        local,
        mesh=grid,
        in_specs=(P(None, None, freq, tile), P(freq, tile, None), P(), P()),
        out_specs=(P(None, freq, tile, None), P(tile, freq)),
        check_vma=False,
    )
```

time: 2230 us -> 100 us (0.04)
  the two profiles are of different devices: /device:TPU:20 before, /device:TPU:1 now
where the time goes in v1:
time: 100 us; the launch traced here: 99.8 us
  starting transfers between devices  40.3 us (40%)
  waiting for transfers between devices  29.3 us (29%)
  blocking collectives  17.3 us (17%)
  Pallas kernels  10.1 us (10%)
  between operations  1.45 us (1%)
    all_to_all x3, starting transfers between devices, exchange(): return lax.all_to_all(x, axes, split_axis=0, concat_axis=0, tiled=True)  30.6 us
    all_to_all x3, waiting for transfers between devices, exchange(): return lax.all_to_all(x, axes, split_axis=0, concat_axis=0, tiled=True)  27.8 us
    all_to_all x1, blocking collectives, exchange(): return lax.all_to_all(x, axes, split_axis=0, concat_axis=0, tiled=True)  17.3 us
    ppermute x1, starting transfers between devices, local(): beside = lax.ppermute(own, 'c', swap)  5.34 us
    ppermute x1, starting transfers between devices, local(): other = lax.ppermute(wavefield, 'h', swap)  4.36 us
    pallas_call x1, Pallas kernels, local(): pl.pallas_call(step_kernel, out_shape=(jax.ShapeDtypeStruct((2, tile_size...  3.28 us
    pallas_call x1, Pallas kernels, local(): pl.pallas_call(shift_kernel, out_shape=jax.ShapeDtypeStruct((2, size, siz...  2.74 us
  transfers between devices with their start and end apart: 5, of which 4 were waited for; matrix products, arithmetic and copies ran while one was open for 0% of the time, Pallas kernels for 4%

profile of v1, /device:TPU:1, one launch (start us, length us, event | category | flops | bytes accessed | tf_op | source)
XLA Modules:
  0.0 99.8 jit_solution(13726438382777848510)
XLA Ops:
  0.6 0.0 copy-start.2
  0.6 13.0 %all-to-all-start = ((bf16[16,8,512]{2,1,0:T(8,128)(2,1)}), bf16[16,8,512]{2,1,0:T(8,128)(2,1)S(1)}, u32[]{:S(2)}, u32[]{:S(2)}) async-start(bf16[16,8,512]{2,1,0:T(8,128)(2,1)} %bitcast.19), calls=%async_computation | async-start | bytes 262144 | tf_op jit(solution)/shard_map/all_to_all | solution.py:159
  13.7 0.0 copy-done.2
  13.7 4.4 %collective-permute-start = (bf16[2,64,8,128]{3,2,1,0:T(8,128)(2,1)S(1)}, bf16[2,64,8,128]{3,2,1,0:T(8,128)(2,1)S(1)}, u32[]{:S(2)}, u32[]{:S(2)}) collective-permute-start(bf16[2,64,8,128]{3,2,1,0:T(8,128)(2,1)S(1)} %bitcast.16), channel_id=1, source_target_pairs={{0,2},{2,0},{1,3},{3,1},{4,6},{6,4},{5,7},{7,5},{8,10},{10,8},{9,1... | collective-permute-start | bytes 786440 | tf_op jit(solution)/shard_map/ppermute | solution.py:169
  18.7 4.1 %all-to-all-done.rows_ref = bf16[16,8,512]{2,1,0:T(8,128)(2,1)S(1)} async-done(((bf16[16,8,512]{2,1,0:T(8,128)(2,1)}), bf16[16,8,512]{2,1,0:T(8,128)(2,1)S(1)}, u32[]{:S(2)}, u32[]{:S(2)}) %all-to-all-start) | async-done | bytes 131104 | tf_op jit(solution)/shard_map/all_to_all | solution.py:159
  22.9 0.6 shard_map.77
  23.5 11.4 %all-to-all-start.1 = ((bf16[32,8,128]{2,1,0:T(8,128)(2,1)}), bf16[32,8,128]{2,1,0:T(8,128)(2,1)S(1)}, u32[]{:S(2)}, u32[]{:S(2)}) async-start(bf16[32,8,128]{2,1,0:T(8,128)(2,1)} %shard_map.77), calls=%async_computation.1 | async-start | bytes 131072 | tf_op jit(solution)/shard_map/all_to_all | solution.py:159
  34.9 0.0 copy-start.3
  34.9 0.1 pad_add_fusion.place_ref
  35.0 0.0 collective-permute-done.other_ref
  35.0 0.6 copy-done.3
  35.6 0.8 shard_map.78
  36.4 8.8 %all-to-all-done.1.slow_ref = bf16[32,8,128]{2,1,0:T(8,128)(2,1)S(1)} async-done(((bf16[32,8,128]{2,1,0:T(8,128)(2,1)}), bf16[32,8,128]{2,1,0:T(8,128)(2,1)S(1)}, u32[]{:S(2)}, u32[]{:S(2)}) %all-to-all-start.1) | async-done | bytes 65568 | tf_op jit(solution)/shard_map/all_to_all | solution.py:159
  45.1 1.9 %shard_map.79 = bf16[128,8,256]{2,1,0:T(8,128)(2,1)} custom-call(s32[2]{0:T(128)S(1)} %pad_add_fusion.place_ref, bf16[32,8,128]{2,1,0:T(8,128)(2,1)S(1)} %all-to-all-done.1.slow_ref, bf16[2,64,8,128]{3,2,1,0:T(8,128)(2,1)S(1)} %get-tuple-element.9.own_ref, bf16[2,64,8,128]{3,2,1,0:T(8,128)(2,1)S(1)} %get-tuple-element.10.other_ref, ...), custom_call_target="tpu_custom_call" | custom-call | flops 6000000 | bytes 1300000 | tf_op jit(solution)/shard_map/pallas_call | solution.py:189
  47.0 6.2 %all-to-all-start.2 = ((bf16[128,8,256]{2,1,0:T(8,128)(2,1)}), bf16[128,8,256]{2,1,0:T(8,128)(2,1)S(1)}, u32[]{:S(2)}, u32[]{:S(2)}) async-start(bf16[128,8,256]{2,1,0:T(8,128)(2,1)} %shard_map.79), calls=%async_computation.2 | async-start | bytes 1048576 | tf_op jit(solution)/shard_map/all_to_all | solution.py:159
  53.2 0.0 copy-start
  53.2 0.0 copy-start.1
  53.3 2.7 %shard_map.80.shift_ref = bf16[2,512,512]{2,1,0:T(8,128)(2,1)S(1)} custom-call(s32[1]{0:T(128)} %bitcast.6.slot_ref, s32[128]{0:T(128)S(1)} %copy-done.3), custom_call_target="tpu_custom_call" | custom-call | flops 10000000 | bytes 2100000 | tf_op jit(solution)/shard_map/pallas_call | solution.py:200
  56.0 14.8 %all-to-all-done.2.wave_ref = bf16[128,8,256]{2,1,0:T(8,128)(2,1)S(1)} async-done(((bf16[128,8,256]{2,1,0:T(8,128)(2,1)}), bf16[128,8,256]{2,1,0:T(8,128)(2,1)S(1)}, u32[]{:S(2)}, u32[]{:S(2)}) %all-to-all-start.2) | async-done | bytes 524320 | tf_op jit(solution)/shard_map/all_to_all | solution.py:159
  70.8 0.0 copy-done
  70.8 0.0 copy-done.1
  70.8 0.7 shard_map.81.own_ref
  71.6 5.3 %collective-permute-start.1 = (bf16[2,2,512,128]{3,2,1,0:T(8,128)(2,1)S(1)}, bf16[2,2,512,128]{3,2,1,0:T(8,128)(2,1)S(1)}, u32[]{:S(2)}, u32[]{:S(2)}) collective-permute-start(bf16[2,2,512,128]{3,2,1,0:T(8,128)(2,1)S(1)} %shard_map.81.own_ref), channel_id=1, source_target_pairs={{0,1},{1,0},{2,3},{3,2},{4,5},{5,4},{6,7},{7,6},{8,9},{9,8},{10,11... | collective-permute-start | bytes 1572872 | tf_op jit(solution)/shard_map/ppermute | solution.py:220
  76.9 1.5 %collective-permute-done.1.other_ref = bf16[2,2,512,128]{3,2,1,0:T(8,128)(2,1)S(1)} collective-permute-done((bf16[2,2,512,128]{3,2,1,0:T(8,128)(2,1)S(1)}, bf16[2,2,512,128]{3,2,1,0:T(8,128)(2,1)S(1)}, u32[]{:S(2)}, u32[]{:S(2)}) %collective-permute-start.1) | collective-permute-done | bytes 524320 | tf_op jit(solution)/shard_map/ppermute | solution.py:220
  78.4 3.3 %shard_map.82 = (bf16[2,128,512]{2,1,0:T(8,128)(2,1)}, bf16[512,128]{1,0:T(8,128)(2,1)S(1)}) custom-call(s32[1]{0:T(128)} %bitcast.tile_ref, bf16[2,2,512,128]{3,2,1,0:T(8,128)(2,1)S(1)} %shard_map.81.own_ref, bf16[2,2,512,128]{3,2,1,0:T(8,128)(2,1)S(1)} %collective-permute-done.1.other_ref, bf16[512,512]{1,0:T(8,128)(2,1)S(1)} %copy-done.1, ...), custom_call_target="tpu_custom_call" | custom-call | flops 1620000000 | bytes 4600000 | tf_op jit(solution)/shard_map/pallas_call | solution.py:221
  81.7 17.3 %all_to_all.20 = bf16[128,4,128]{2,1,0:T(4,128)(2,1)S(1)} all-to-all(bf16[128,4,128]{2,1,0:T(4,128)(2,1)S(1)} %bitcast.18), channel_id=1, replica_groups=mesh['u'=4,'v'=2,'w'=2,'z'=4,'l'=2,'h'=2,'c'=2] {'u','v','w','z','l'}, dimensions={0} | all-to-all | bytes 262144 | tf_op jit(solution)/shard_map/all_to_all | solution.py:159
  99.0 0.7 convert_reduce_fusion
Async XLA Ops:
  0.6 13.1 %copy-start.2 = (bf16[2,128,4,128]{3,2,1,0:T(4,128)(2,1)S(1)}, bf16[2,128,4,128]{3,2,1,0:T(4,128)(2,1)}, u32[]{:S(2)}) copy-start(bf16[2,128,4,128]{3,2,1,0:T(4,128)(2,1)} %param.6) | copy-start | bytes 786436
  0.6 22.2 %all-to-all-start = ((bf16[16,8,512]{2,1,0:T(8,128)(2,1)}), bf16[16,8,512]{2,1,0:T(8,128)(2,1)S(1)}, u32[]{:S(2)}, u32[]{:S(2)}) async-start(bf16[16,8,512]{2,1,0:T(8,128)(2,1)} %bitcast.19), calls=%async_computation | async-start | bytes 262144 | tf_op jit(solution)/shard_map/all_to_all | solution.py:159
  13.7 21.3 %collective-permute-start = (bf16[2,64,8,128]{3,2,1,0:T(8,128)(2,1)S(1)}, bf16[2,64,8,128]{3,2,1,0:T(8,128)(2,1)S(1)}, u32[]{:S(2)}, u32[]{:S(2)}) collective-permute-start(bf16[2,64,8,128]{3,2,1,0:T(8,128)(2,1)S(1)} %bitcast.16), channel_id=1, source_target_pairs={{0,2},{2,0},{1,3},{3,1},{4,6},{6,4},{5,7},{7,5},{8,10},{10,8},{9,1... | collective-permute-start | bytes 786440 | tf_op jit(solution)/shard_map/ppermute | solution.py:169
  23.5 21.6 %all-to-all-start.1 = ((bf16[32,8,128]{2,1,0:T(8,128)(2,1)}), bf16[32,8,128]{2,1,0:T(8,128)(2,1)S(1)}, u32[]{:S(2)}, u32[]{:S(2)}) async-start(bf16[32,8,128]{2,1,0:T(8,128)(2,1)} %shard_map.77), calls=%async_computation.1 | async-start | bytes 131072 | tf_op jit(solution)/shard_map/all_to_all | solution.py:159
  34.9 0.7 copy-start.3
  47.0 23.8 %all-to-all-start.2 = ((bf16[128,8,256]{2,1,0:T(8,128)(2,1)}), bf16[128,8,256]{2,1,0:T(8,128)(2,1)S(1)}, u32[]{:S(2)}, u32[]{:S(2)}) async-start(bf16[128,8,256]{2,1,0:T(8,128)(2,1)} %shard_map.79), calls=%async_computation.2 | async-start | bytes 1048576 | tf_op jit(solution)/shard_map/all_to_all | solution.py:159
  53.2 17.6 %copy-start = (bf16[512,512]{1,0:T(8,128)(2,1)S(1)}, bf16[512,512]{1,0:T(8,128)(2,1)}, u32[]{:S(2)}) copy-start(bf16[512,512]{1,0:T(8,128)(2,1)} %constant.67.clone.sin_ref) | copy-start | bytes 1572868
  53.2 17.6 %copy-start.1 = (bf16[512,512]{1,0:T(8,128)(2,1)S(1)}, bf16[512,512]{1,0:T(8,128)(2,1)}, u32[]{:S(2)}) copy-start(bf16[512,512]{1,0:T(8,128)(2,1)} %constant.66.clone.cos_ref) | copy-start | bytes 1572868
  71.6 6.9 %collective-permute-start.1 = (bf16[2,2,512,128]{3,2,1,0:T(8,128)(2,1)S(1)}, bf16[2,2,512,128]{3,2,1,0:T(8,128)(2,1)S(1)}, u32[]{:S(2)}, u32[]{:S(2)}) collective-permute-start(bf16[2,2,512,128]{3,2,1,0:T(8,128)(2,1)S(1)} %shard_map.81.own_ref), channel_id=1, source_target_pairs={{0,1},{1,0},{2,3},{3,2},{4,5},{5,4},{6,7},{7,6},{8,9},{9,8},{10,11... | collective-permute-start | bytes 1572872 | tf_op jit(solution)/shard_map/ppermute | solution.py:220

commit v2 on v1

--- a/solution.py
+++ b/solution.py
@@ -39,15 +39,14 @@
 
 
 def pick_kernel(owner_ref, rows_ref, out_ref):
-    rows = rows_ref[owner_ref[0] // 2 % 16].astype(jnp.float32)
-    for l in range(2):
-        for c in range(2):
-            lanes = (c * tile_size, (2 + c) * tile_size)
-            piece = jnp.concatenate([rows[4 * l : 4 * l + 4, lane : lane + tile_size] for lane in lanes], axis=0)
-            piece = piece.astype(jnp.bfloat16)
-            for u in range(4):
+    source = owner_ref[0] // 2 % 16
+    for core in range(2):
+        low, high = (rows_ref[source, core, half].astype(jnp.float32) for half in range(2))
+        for l in range(2):
+            piece = jnp.concatenate([low[4 * l : 4 * l + 4], high[4 * l : 4 * l + 4]], axis=0).astype(jnp.bfloat16)
+            for u in (core, core + 2):
                 for h in range(2):
-                    out_ref[((u * 2 + l) * 2 + h) * 2 + c] = piece
+                    out_ref[(u * 2 + l) * 2 + h] = piece
 
 
 def shift_kernel(slot_ref, ids_ref, shift_ref):
@@ -72,36 +71,38 @@
         shift_ref[1, pl.ds(start, 16), :] = (damping * travel * series(travel_square, 1, 13)).astype(jnp.bfloat16)
 
 
-def pack_kernel(ids_ref, own_ref, other_ref, own_out, other_out, factor_ref):
-    own_out[...] = own_ref[...]
-    other_out[...] = other_ref[...]
-    first = lax.broadcasted_iota(jnp.int32, (8, tile_size), 0) < 4
-    for pair in range(slots // 2):
-        low, high = (
-            depth_step * (omega_top * (ids_ref[2 * pair + at] + 1).astype(jnp.float32) / slots) for at in range(2)
-        )
-        factor_ref[pair] = jnp.where(first, low, high)
-
-
-def lens_kernel(place_ref, slow_ref, own_ref, other_ref, factor_ref, out_ref):
-    slow = slow_ref[place_ref[0]].astype(jnp.float32) - 1.0
-    halves = (jnp.concatenate([slow[:4]] * 2, axis=0), jnp.concatenate([slow[4:]] * 2, axis=0))
-    low = place_ref[1] == 0
-    depths = (jnp.where(low, halves[0], halves[1]), jnp.where(low, halves[1], halves[0]))
-    for pair in range(slots // 2):
-        factor = factor_ref[pair]
-        for block, (ref, depth) in enumerate(zip((own_ref, other_ref), depths)):
-            phase = factor * depth
-            square = phase * phase
-            lens_cos = series(square, 0, 8)
-            lens_sin = phase * series(square, 1, 9)
-            wave_real = ref[0, pair].astype(jnp.float32)
-            wave_imag = ref[1, pair].astype(jnp.float32)
-            real = wave_real * lens_cos - wave_imag * lens_sin
-            imag = wave_real * lens_sin + wave_imag * lens_cos
-            lanes = slice(block * tile_size, (block + 1) * tile_size)
-            out_ref[2 * pair, :, lanes] = jnp.concatenate([real[:4], imag[:4]], axis=0).astype(jnp.bfloat16)
-            out_ref[2 * pair + 1, :, lanes] = jnp.concatenate([real[4:], imag[4:]], axis=0).astype(jnp.bfloat16)
+def pack_kernel(own_ref, other_ref, wave_ref):
+    for slot in range(slots):
+        for part in range(2):
+            both = jnp.concatenate([own_ref[part, slot].astype(jnp.float32), other_ref[part, slot].astype(jnp.float32)], axis=0)
+            wave_ref[slot, part] = both.astype(jnp.bfloat16)
+
+
+def lens_kernel(place_ref, slow_ref, wave_ref, out_ref, turn):
+    slow = slow_ref[place_ref[0]].astype(jnp.float32)
+    swapped = jnp.concatenate([slow[4:], slow[:4]], axis=0)
+    unit = (depth_step * omega_top / slots) * (jnp.where(place_ref[1] == 0, slow, swapped) - 1.0)
+
+    def turned(count):
+        phase = unit * float(count)
+        square = phase * phase
+        return series(square, 0, 8), phase * series(square, 1, 9)
+
+    fine = [turned(count) for count in range(1, 17)]
+    for group in range(slots // 16):
+        group_cos, group_sin = turned(16 * group)
+        for at, (fine_cos, fine_sin) in enumerate(fine):
+            turn[16 * group + at, 0] = group_cos * fine_cos - group_sin * fine_sin
+            turn[16 * group + at, 1] = group_cos * fine_sin + group_sin * fine_cos
+    for slot in range(slots):
+        number = place_ref[2 + slot]
+        lens_cos, lens_sin = turn[number, 0], turn[number, 1]
+        wave_real = wave_ref[slot, 0].astype(jnp.float32)
+        wave_imag = wave_ref[slot, 1].astype(jnp.float32)
+        real = wave_real * lens_cos - wave_imag * lens_sin
+        imag = wave_real * lens_sin + wave_imag * lens_cos
+        out_ref[slot, :, :tile_size] = jnp.concatenate([real[:4], imag[:4]], axis=0).astype(jnp.bfloat16)
+        out_ref[slot, :, tile_size:] = jnp.concatenate([real[4:], imag[4:]], axis=0).astype(jnp.bfloat16)
 
 
 def column_kernel(cos_ref, sin_ref, wave_ref, out_ref, both):
@@ -164,36 +165,36 @@
     swap = [(0, 1), (1, 0)]
     side = lax.axis_index("h").astype(jnp.int32)
     tile = 2 * side + lax.axis_index("c").astype(jnp.int32)
-    wavefield = wavefield.reshape(2, slots // 2, 8, tile_size)
-    pieces = exchange(slowness.reshape(16, 8, size), ("v", "w", "z"))
+    pieces = slowness.reshape(16, 8, 2, 2, tile_size).transpose(0, 3, 2, 1, 4)
+    pieces = exchange(pieces.reshape(32, 2, 8, tile_size), ("v", "w", "z", "c"))
     other = lax.ppermute(wavefield, "h", swap)
     pieces = pl.pallas_call(
         pick_kernel,
-        out_shape=jax.ShapeDtypeStruct((32, 8, tile_size), jnp.bfloat16),
+        out_shape=jax.ShapeDtypeStruct((16, 8, tile_size), jnp.bfloat16),
         in_specs=[whole(pltpu.SMEM), whole()],
         out_specs=whole(),
         compiler_params=pltpu.CompilerParams(vmem_limit_bytes=8 << 20),
         cost_estimate=pl.CostEstimate(flops=10_000, bytes_accessed=100_000, transcendentals=0),
-    )(depth_owner, pieces)
-    pieces = exchange(pieces, ("u", "l", "h", "c"))
-    half = jax.ShapeDtypeStruct((2, slots // 2, 8, tile_size), jnp.bfloat16)
-    own, other, factors = pl.pallas_call(
+    )(depth_owner, pieces.reshape(16, 2, 2, 8, tile_size))
+    pieces = exchange(pieces, ("u", "l", "h"))
+    waves = pl.pallas_call(
         pack_kernel,
-        out_shape=(half, half, jax.ShapeDtypeStruct((slots // 2, 8, tile_size), jnp.float32)),
-        in_specs=[whole(pltpu.SMEM)] + [whole()] * 2,
-        out_specs=(whole(), whole(), whole()),
-        compiler_params=pltpu.CompilerParams(vmem_limit_bytes=8 << 20),
-        cost_estimate=pl.CostEstimate(flops=300_000, bytes_accessed=1_300_000, transcendentals=0),
-    )(freq_ids, wavefield, other)
-    place = (owner // 32 * 2 + owner % 2) * 4 + lax.axis_index("u").astype(jnp.int32)
+        out_shape=jax.ShapeDtypeStruct((slots, 2, 8, tile_size), jnp.bfloat16),
+        in_specs=[whole()] * 2,
+        out_specs=whole(),
+        compiler_params=pltpu.CompilerParams(vmem_limit_bytes=8 << 20),
+        cost_estimate=pl.CostEstimate(flops=300_000, bytes_accessed=1_000_000, transcendentals=0),
+    )(wavefield, other)
+    place = (owner // 32 * 2 + owner % 2) * 2 + lax.axis_index("u").astype(jnp.int32) // 2
     lensed = pl.pallas_call(
         lens_kernel,
         out_shape=jax.ShapeDtypeStruct((slots, 8, 2 * tile_size), jnp.bfloat16),
-        in_specs=[whole(pltpu.SMEM)] + [whole()] * 4,
-        out_specs=whole(),
-        compiler_params=pltpu.CompilerParams(vmem_limit_bytes=8 << 20),
-        cost_estimate=pl.CostEstimate(flops=6_000_000, bytes_accessed=1_300_000, transcendentals=0),
-    )(jnp.stack([place, side]), pieces, own, other, factors)
+        in_specs=[whole(pltpu.SMEM)] + [whole()] * 2,
+        out_specs=whole(),
+        scratch_shapes=[pltpu.VMEM((slots, 2, 8, tile_size), jnp.float32)],
+        compiler_params=pltpu.CompilerParams(vmem_limit_bytes=8 << 20),
+        cost_estimate=pl.CostEstimate(flops=3_000_000, bytes_accessed=1_100_000, transcendentals=0),
+    )(jnp.concatenate([jnp.stack([place, side]), freq_ids]), pieces, waves)
     columns = exchange(lensed, freq)
 
     table_cos, table_sin = dft_table(size)

time: 100 us -> 100 us (level)
  local copies, waits for them, and re-layouts: 0.59 us -> 2.29 us
    all_to_all x3, starting transfers between devices: 30.6 us -> 28.8 us  [exchange(): return lax.all_to_all(x, axes, split_axis=0, concat_axis=0, tiled=True)]
    transpose x0 -> x1, local copies, waits for them, and re-layouts: none -> 1.62 us  [local(): pieces = slowness.reshape(16, 8, 2, 2, tile_size).transpose(0, 3, 2, 1, 4)]
where the time goes in v2:
time: 100 us
  starting transfers between devices  39.4 us (39%)
  waiting for transfers between devices  29.4 us (29%)
  blocking collectives  17.3 us (17%)
  Pallas kernels  9.27 us (9%)
  local copies, waits for them, and re-layouts  2.29 us (2%)
  between operations  1.45 us (1%)
    all_to_all x3, starting transfers between devices, exchange(): return lax.all_to_all(x, axes, split_axis=0, concat_axis=0, tiled=True)  28.8 us
    all_to_all x3, waiting for transfers between devices, exchange(): return lax.all_to_all(x, axes, split_axis=0, concat_axis=0, tiled=True)  27.9 us
    all_to_all x1, blocking collectives, exchange(): return lax.all_to_all(x, axes, split_axis=0, concat_axis=0, tiled=True)  17.3 us
    ppermute x1, starting transfers between devices, local(): beside = lax.ppermute(own, 'c', swap)  6.26 us
    ppermute x1, starting transfers between devices, local(): other = lax.ppermute(wavefield, 'h', swap)  4.36 us
    pallas_call x1, Pallas kernels, local(): pl.pallas_call(step_kernel, out_shape=(jax.ShapeDtypeStruct((2, tile_size...  3.22 us
    pallas_call x1, Pallas kernels, local(): pl.pallas_call(shift_kernel, out_shape=jax.ShapeDtypeStruct((2, size, siz...  2.74 us
  transfers between devices with their start and end apart: 5, of which 4 were waited for; matrix products, arithmetic and copies ran while one was open for 0% of the time, Pallas kernels for 4%

profile of v2, /device:TPU:1, one launch (start us, length us, event | category | flops | bytes accessed | tf_op | source)
XLA Modules:
  0.0 100.0 jit_solution(106300622833956507)
XLA Ops:
  0.6 0.0 copy-start.2
  0.6 1.6 %copy.8 = bf16[16,2,2,8,128]{4,3,2,1,0:T(8,128)(2,1)} copy(bf16[16,2,2,8,128]{4,3,1,2,0:T(8,128)(2,1)} %bitcast.21) | data formatting | bytes 262144 | tf_op jit(solution)/shard_map/transpose | solution.py:168
  2.3 13.9 %all-to-all-start = ((bf16[32,2,8,128]{3,2,1,0:T(8,128)(2,1)}), bf16[32,2,8,128]{3,2,1,0:T(8,128)(2,1)S(1)}, u32[]{:S(2)}, u32[]{:S(2)}) async-start(bf16[32,2,8,128]{3,2,1,0:T(8,128)(2,1)} %bitcast.6), calls=%async_computation | async-start | bytes 262144 | tf_op jit(solution)/shard_map/all_to_all | solution.py:160
  16.2 0.0 copy-done.2
  16.2 4.4 %collective-permute-start = (bf16[2,128,4,128]{3,2,1,0:T(4,128)(2,1)S(1)}, bf16[2,128,4,128]{3,2,1,0:T(4,128)(2,1)S(1)}, u32[]{:S(2)}, u32[]{:S(2)}) collective-permute-start(bf16[2,128,4,128]{3,2,1,0:T(4,128)(2,1)S(1)} %copy-done.2), channel_id=1, source_target_pairs={{0,2},{2,0},{1,3},{3,1},{4,6},{6,4},{5,7},{7,5},{8,10},{10,8},{9,1... | collective-permute-start | bytes 786440 | tf_op jit(solution)/shard_map/ppermute | solution.py:170
  21.2 4.9 %all-to-all-done = bf16[32,2,8,128]{3,2,1,0:T(8,128)(2,1)S(1)} async-done(((bf16[32,2,8,128]{3,2,1,0:T(8,128)(2,1)}), bf16[32,2,8,128]{3,2,1,0:T(8,128)(2,1)S(1)}, u32[]{:S(2)}, u32[]{:S(2)}) %all-to-all-start) | async-done | bytes 131104 | tf_op jit(solution)/shard_map/all_to_all | solution.py:160
  26.2 0.6 shard_map.77
  26.8 8.7 %all-to-all-start.1 = ((bf16[16,8,128]{2,1,0:T(8,128)(2,1)}), bf16[16,8,128]{2,1,0:T(8,128)(2,1)S(1)}, u32[]{:S(2)}, u32[]{:S(2)}) async-start(bf16[16,8,128]{2,1,0:T(8,128)(2,1)} %shard_map.77), calls=%async_computation.1 | async-start | bytes 65536 | tf_op jit(solution)/shard_map/all_to_all | solution.py:160
  35.6 0.0 copy-start.3
  35.6 0.6 copy-done.3
  36.2 0.1 pad_add_fusion.place_ref
  36.3 0.0 collective-permute-done.other_ref
  36.3 0.2 shard_map.78.wave_ref
  36.5 9.0 %all-to-all-done.1.slow_ref = bf16[16,8,128]{2,1,0:T(8,128)(2,1)S(1)} async-done(((bf16[16,8,128]{2,1,0:T(8,128)(2,1)}), bf16[16,8,128]{2,1,0:T(8,128)(2,1)S(1)}, u32[]{:S(2)}, u32[]{:S(2)}) %all-to-all-start.1) | async-done | bytes 32800 | tf_op jit(solution)/shard_map/all_to_all | solution.py:160
  45.4 1.8 %shard_map.79 = bf16[128,8,256]{2,1,0:T(8,128)(2,1)} custom-call(s32[130]{0:T(256)S(1)} %pad_add_fusion.place_ref, bf16[16,8,128]{2,1,0:T(8,128)(2,1)S(1)} %all-to-all-done.1.slow_ref, bf16[128,2,8,128]{3,2,1,0:T(8,128)(2,1)S(1)} %shard_map.78.wave_ref), custom_call_target="tpu_custom_call" | custom-call | flops 3000000 | bytes 1100000 | tf_op jit(solution)/shard_map/pallas_call | solution.py:189
  47.2 6.2 %all-to-all-start.2 = ((bf16[128,8,256]{2,1,0:T(8,128)(2,1)}), bf16[128,8,256]{2,1,0:T(8,128)(2,1)S(1)}, u32[]{:S(2)}, u32[]{:S(2)}) async-start(bf16[128,8,256]{2,1,0:T(8,128)(2,1)} %shard_map.79), calls=%async_computation.2 | async-start | bytes 1048576 | tf_op jit(solution)/shard_map/all_to_all | solution.py:160
  53.4 0.0 copy-start
  53.4 0.0 copy-start.1
  53.4 2.7 %shard_map.80.shift_ref = bf16[2,512,512]{2,1,0:T(8,128)(2,1)S(1)} custom-call(s32[1]{0:T(128)} %bitcast.8.slot_ref, s32[128]{0:T(128)S(1)} %copy-done.3), custom_call_target="tpu_custom_call" | custom-call | flops 10000000 | bytes 2100000 | tf_op jit(solution)/shard_map/pallas_call | solution.py:201
  56.2 14.0 %all-to-all-done.2.wave_ref = bf16[128,8,256]{2,1,0:T(8,128)(2,1)S(1)} async-done(((bf16[128,8,256]{2,1,0:T(8,128)(2,1)}), bf16[128,8,256]{2,1,0:T(8,128)(2,1)S(1)}, u32[]{:S(2)}, u32[]{:S(2)}) %all-to-all-start.2) | async-done | bytes 524320 | tf_op jit(solution)/shard_map/all_to_all | solution.py:160
  70.2 0.0 copy-done
  70.2 0.0 copy-done.1
  70.2 0.7 shard_map.81.own_ref
  71.0 6.3 %collective-permute-start.1 = (bf16[2,2,512,128]{3,2,1,0:T(8,128)(2,1)S(1)}, bf16[2,2,512,128]{3,2,1,0:T(8,128)(2,1)S(1)}, u32[]{:S(2)}, u32[]{:S(2)}) collective-permute-start(bf16[2,2,512,128]{3,2,1,0:T(8,128)(2,1)S(1)} %shard_map.81.own_ref), channel_id=1, source_target_pairs={{0,1},{1,0},{2,3},{3,2},{4,5},{5,4},{6,7},{7,6},{8,9},{9,8},{10,11... | collective-permute-start | bytes 1572872 | tf_op jit(solution)/shard_map/ppermute | solution.py:221
  77.2 1.5 %collective-permute-done.1.other_ref = bf16[2,2,512,128]{3,2,1,0:T(8,128)(2,1)S(1)} collective-permute-done((bf16[2,2,512,128]{3,2,1,0:T(8,128)(2,1)S(1)}, bf16[2,2,512,128]{3,2,1,0:T(8,128)(2,1)S(1)}, u32[]{:S(2)}, u32[]{:S(2)}) %collective-permute-start.1) | collective-permute-done | bytes 524320 | tf_op jit(solution)/shard_map/ppermute | solution.py:221
  78.7 3.2 %shard_map.82 = (bf16[2,128,512]{2,1,0:T(8,128)(2,1)}, bf16[512,128]{1,0:T(8,128)(2,1)S(1)}) custom-call(s32[1]{0:T(128)} %bitcast.tile_ref, bf16[2,2,512,128]{3,2,1,0:T(8,128)(2,1)S(1)} %shard_map.81.own_ref, bf16[2,2,512,128]{3,2,1,0:T(8,128)(2,1)S(1)} %collective-permute-done.1.other_ref, bf16[512,512]{1,0:T(8,128)(2,1)S(1)} %copy-done.1, ...), custom_call_target="tpu_custom_call" | custom-call | flops 1620000000 | bytes 4600000 | tf_op jit(solution)/shard_map/pallas_call | solution.py:222
  82.0 17.3 %all_to_all.20 = bf16[128,4,128]{2,1,0:T(4,128)(2,1)S(1)} all-to-all(bf16[128,4,128]{2,1,0:T(4,128)(2,1)S(1)} %bitcast.20), channel_id=1, replica_groups=mesh['u'=4,'v'=2,'w'=2,'z'=4,'l'=2,'h'=2,'c'=2] {'u','v','w','z','l'}, dimensions={0} | all-to-all | bytes 262144 | tf_op jit(solution)/shard_map/all_to_all | solution.py:160
  99.3 0.7 convert_reduce_fusion
Async XLA Ops:
  0.6 15.5 %copy-start.2 = (bf16[2,128,4,128]{3,2,1,0:T(4,128)(2,1)S(1)}, bf16[2,128,4,128]{3,2,1,0:T(4,128)(2,1)}, u32[]{:S(2)}) copy-start(bf16[2,128,4,128]{3,2,1,0:T(4,128)(2,1)} %own_ref.1) | copy-start | bytes 786436
  2.3 23.9 %all-to-all-start = ((bf16[32,2,8,128]{3,2,1,0:T(8,128)(2,1)}), bf16[32,2,8,128]{3,2,1,0:T(8,128)(2,1)S(1)}, u32[]{:S(2)}, u32[]{:S(2)}) async-start(bf16[32,2,8,128]{3,2,1,0:T(8,128)(2,1)} %bitcast.6), calls=%async_computation | async-start | bytes 262144 | tf_op jit(solution)/shard_map/all_to_all | solution.py:160
  16.2 20.1 %collective-permute-start = (bf16[2,128,4,128]{3,2,1,0:T(4,128)(2,1)S(1)}, bf16[2,128,4,128]{3,2,1,0:T(4,128)(2,1)S(1)}, u32[]{:S(2)}, u32[]{:S(2)}) collective-permute-start(bf16[2,128,4,128]{3,2,1,0:T(4,128)(2,1)S(1)} %copy-done.2), channel_id=1, source_target_pairs={{0,2},{2,0},{1,3},{3,1},{4,6},{6,4},{5,7},{7,5},{8,10},{10,8},{9,1... | collective-permute-start | bytes 786440 | tf_op jit(solution)/shard_map/ppermute | solution.py:170
  26.8 18.6 %all-to-all-start.1 = ((bf16[16,8,128]{2,1,0:T(8,128)(2,1)}), bf16[16,8,128]{2,1,0:T(8,128)(2,1)S(1)}, u32[]{:S(2)}, u32[]{:S(2)}) async-start(bf16[16,8,128]{2,1,0:T(8,128)(2,1)} %shard_map.77), calls=%async_computation.1 | async-start | bytes 65536 | tf_op jit(solution)/shard_map/all_to_all | solution.py:160
  35.6 0.7 copy-start.3
  47.2 23.0 %all-to-all-start.2 = ((bf16[128,8,256]{2,1,0:T(8,128)(2,1)}), bf16[128,8,256]{2,1,0:T(8,128)(2,1)S(1)}, u32[]{:S(2)}, u32[]{:S(2)}) async-start(bf16[128,8,256]{2,1,0:T(8,128)(2,1)} %shard_map.79), calls=%async_computation.2 | async-start | bytes 1048576 | tf_op jit(solution)/shard_map/all_to_all | solution.py:160
  53.4 16.8 %copy-start = (bf16[512,512]{1,0:T(8,128)(2,1)S(1)}, bf16[512,512]{1,0:T(8,128)(2,1)}, u32[]{:S(2)}) copy-start(bf16[512,512]{1,0:T(8,128)(2,1)} %constant.73.clone.sin_ref) | copy-start | bytes 1572868
  53.4 16.8 %copy-start.1 = (bf16[512,512]{1,0:T(8,128)(2,1)S(1)}, bf16[512,512]{1,0:T(8,128)(2,1)}, u32[]{:S(2)}) copy-start(bf16[512,512]{1,0:T(8,128)(2,1)} %constant.72.clone.cos_ref) | copy-start | bytes 1572868
  71.0 7.8 %collective-permute-start.1 = (bf16[2,2,512,128]{3,2,1,0:T(8,128)(2,1)S(1)}, bf16[2,2,512,128]{3,2,1,0:T(8,128)(2,1)S(1)}, u32[]{:S(2)}, u32[]{:S(2)}) collective-permute-start(bf16[2,2,512,128]{3,2,1,0:T(8,128)(2,1)S(1)} %shard_map.81.own_ref), channel_id=1, source_target_pairs={{0,1},{1,0},{2,3},{3,2},{4,5},{5,4},{6,7},{7,6},{8,9},{9,8},{10,11... | collective-permute-start | bytes 1572872 | tf_op jit(solution)/shard_map/ppermute | solution.py:221

commit v3 on v1

--- a/solution.py
+++ b/solution.py
@@ -14,7 +14,13 @@
 slots = 128
 size = 512
 tile_size = 128
-freq = ("u", "v", "w", "z", "l")
+freq = ("y4", "y2", "y1", "w", "z4", "z2", "z1")
+mixed = ("z1", "y1", "w", "z2", "y2", "z4", "y4")
+
+
+def place_of(slot):
+    bits = {axis: slot >> (len(freq) - 1 - at) & 1 for at, axis in enumerate(freq)}
+    return sum(bits[axis] << (len(mixed) - 1 - at) for at, axis in enumerate(mixed))
 
 
 def dft_table(length):
@@ -100,13 +106,13 @@
             real = wave_real * lens_cos - wave_imag * lens_sin
             imag = wave_real * lens_sin + wave_imag * lens_cos
             lanes = slice(block * tile_size, (block + 1) * tile_size)
-            out_ref[2 * pair, :, lanes] = jnp.concatenate([real[:4], imag[:4]], axis=0).astype(jnp.bfloat16)
-            out_ref[2 * pair + 1, :, lanes] = jnp.concatenate([real[4:], imag[4:]], axis=0).astype(jnp.bfloat16)
+            out_ref[place_of(2 * pair), :, lanes] = jnp.concatenate([real[:4], imag[:4]], axis=0).astype(jnp.bfloat16)
+            out_ref[place_of(2 * pair + 1), :, lanes] = jnp.concatenate([real[4:], imag[4:]], axis=0).astype(jnp.bfloat16)
 
 
 def column_kernel(cos_ref, sin_ref, wave_ref, out_ref, both):
     for at in range(0, size // 4, 4):
-        tiles = [wave_ref[at + k].astype(jnp.float32) for k in range(4)]
+        tiles = [wave_ref[place_of(at + k)].astype(jnp.float32) for k in range(4)]
         for part in range(2):
             rows = jnp.concatenate([tile[4 * part : 4 * part + 4] for tile in tiles], axis=0)
             both[4 * at : 4 * at + 16, part * 2 * tile_size : (part + 1) * 2 * tile_size] = rows.astype(jnp.bfloat16)
@@ -148,7 +154,9 @@
         field_real = by_cos[:tile_size] - by_sin[tile_size:]
         wave_ref[0, :, part] = field_real.astype(jnp.bfloat16)
         wave_ref[1, :, part] = (by_cos[tile_size:] + by_sin[:tile_size]).astype(jnp.bfloat16)
-        image_ref[part, :] = (field_real * (1.0 / math.sqrt(slots))).T.astype(jnp.bfloat16)
+        image = (field_real * (1.0 / math.sqrt(slots))).T.astype(jnp.bfloat16)
+        for slot in range(at // 4, (at + width) // 4):
+            image_ref[place_of(slot)] = image[4 * slot - at : 4 * slot - at + 4]
 
 
 def whole(memory=pltpu.VMEM):
@@ -165,7 +173,7 @@
     side = lax.axis_index("h").astype(jnp.int32)
     tile = 2 * side + lax.axis_index("c").astype(jnp.int32)
     wavefield = wavefield.reshape(2, slots // 2, 8, tile_size)
-    pieces = exchange(slowness.reshape(16, 8, size), ("v", "w", "z"))
+    pieces = exchange(slowness.reshape(16, 8, size), ("y1", "w", "z4", "z2"))
     other = lax.ppermute(wavefield, "h", swap)
     pieces = pl.pallas_call(
         pick_kernel,
@@ -175,7 +183,7 @@
         compiler_params=pltpu.CompilerParams(vmem_limit_bytes=8 << 20),
         cost_estimate=pl.CostEstimate(flops=10_000, bytes_accessed=100_000, transcendentals=0),
     )(depth_owner, pieces)
-    pieces = exchange(pieces, ("u", "l", "h", "c"))
+    pieces = exchange(pieces, ("y4", "y2", "z1", "h", "c"))
     half = jax.ShapeDtypeStruct((2, slots // 2, 8, tile_size), jnp.bfloat16)
     own, other, factors = pl.pallas_call(
         pack_kernel,
@@ -185,7 +193,7 @@
         compiler_params=pltpu.CompilerParams(vmem_limit_bytes=8 << 20),
         cost_estimate=pl.CostEstimate(flops=300_000, bytes_accessed=1_300_000, transcendentals=0),
     )(freq_ids, wavefield, other)
-    place = (owner // 32 * 2 + owner % 2) * 4 + lax.axis_index("u").astype(jnp.int32)
+    place = (owner // 32 * 2 + owner % 2) * 4 + lax.axis_index(("y4", "y2")).astype(jnp.int32)
     lensed = pl.pallas_call(
         lens_kernel,
         out_shape=jax.ShapeDtypeStruct((slots, 8, 2 * tile_size), jnp.bfloat16),
@@ -194,7 +202,7 @@
         compiler_params=pltpu.CompilerParams(vmem_limit_bytes=8 << 20),
         cost_estimate=pl.CostEstimate(flops=6_000_000, bytes_accessed=1_300_000, transcendentals=0),
     )(jnp.stack([place, side]), pieces, own, other, factors)
-    columns = exchange(lensed, freq)
+    columns = exchange(lensed, mixed)
 
     table_cos, table_sin = dft_table(size)
     shift = pl.pallas_call(
@@ -222,7 +230,7 @@
         step_kernel,
         out_shape=(
             jax.ShapeDtypeStruct((2, tile_size, size), jnp.bfloat16),
-            jax.ShapeDtypeStruct((size, tile_size), jnp.bfloat16),
+            jax.ShapeDtypeStruct((slots, size // slots, tile_size), jnp.bfloat16),
         ),
         in_specs=[whole(pltpu.SMEM)] + [whole()] * 5,
         out_specs=(whole(), whole()),
@@ -233,13 +241,13 @@
         compiler_params=pltpu.CompilerParams(vmem_limit_bytes=20 << 20),
         cost_estimate=pl.CostEstimate(flops=1_620_000_000, bytes_accessed=4_600_000, transcendentals=0),
     )(tile[None], own, beside, table_cos, table_sin, shift)
-    parts = exchange(parts.reshape(slots, size // slots, tile_size), freq)
+    parts = exchange(parts, mixed)
     image = jnp.sum(parts.astype(jnp.float32), axis=0).T
     return (wave_next[:, None], image)
 
 
 def solution(mesh):
-    grid = Mesh(mesh.devices.reshape(4, 2, 2, 4, 2, 2, 2), freq + ("h", "c"))
+    grid = Mesh(mesh.devices.reshape((2,) * 9), freq + ("h", "c"))
     tile = ("h", "c")
     return jax.shard_map(
         local,

time: 100 us -> 99.5 us (level)
  waiting for transfers between devices: 29.3 us -> 28.1 us
    all_to_all x3, waiting for transfers between devices: 27.8 us -> 26.5 us  [exchange(): return lax.all_to_all(x, axes, split_axis=0, concat_axis=0, tiled=True)]
where the time goes in v3:
time: 99.5 us; the launch traced here: 98.8 us
  starting transfers between devices  40.3 us (41%)
  waiting for transfers between devices  28.1 us (28%)
  blocking collectives  17.5 us (18%)
  Pallas kernels  10.1 us (10%)
  between operations  1.46 us (1%)
    all_to_all x3, starting transfers between devices, exchange(): return lax.all_to_all(x, axes, split_axis=0, concat_axis=0, tiled=True)  30.6 us
    all_to_all x3, waiting for transfers between devices, exchange(): return lax.all_to_all(x, axes, split_axis=0, concat_axis=0, tiled=True)  26.5 us
    all_to_all x1, blocking collectives, exchange(): return lax.all_to_all(x, axes, split_axis=0, concat_axis=0, tiled=True)  17.5 us
    ppermute x1, starting transfers between devices, local(): beside = lax.ppermute(own, 'c', swap)  5.33 us
    ppermute x1, starting transfers between devices, local(): other = lax.ppermute(wavefield, 'h', swap)  4.36 us
    pallas_call x1, Pallas kernels, local(): pl.pallas_call(step_kernel, out_shape=(jax.ShapeDtypeStruct((2, tile_size...  3.28 us
    pallas_call x1, Pallas kernels, local(): pl.pallas_call(shift_kernel, out_shape=jax.ShapeDtypeStruct((2, size, siz...  2.74 us
  transfers between devices with their start and end apart: 5, of which 4 were waited for; matrix products, arithmetic and copies ran while one was open for 0% of the time, Pallas kernels for 4%

profile of v3, /device:TPU:1, one launch (start us, length us, event | category | flops | bytes accessed | tf_op | source)
XLA Modules:
  0.0 98.8 jit_solution(17084330303482027032)
XLA Ops:
  0.6 0.0 copy-start.2
  0.6 13.0 %all-to-all-start = ((bf16[16,8,512]{2,1,0:T(8,128)(2,1)}), bf16[16,8,512]{2,1,0:T(8,128)(2,1)S(1)}, u32[]{:S(2)}, u32[]{:S(2)}) async-start(bf16[16,8,512]{2,1,0:T(8,128)(2,1)} %bitcast.17), calls=%async_computation | async-start | bytes 262144 | tf_op jit(solution)/shard_map/all_to_all | solution.py:167
  13.7 0.0 copy-done.2
  13.7 4.4 %collective-permute-start = (bf16[2,64,8,128]{3,2,1,0:T(8,128)(2,1)S(1)}, bf16[2,64,8,128]{3,2,1,0:T(8,128)(2,1)S(1)}, u32[]{:S(2)}, u32[]{:S(2)}) collective-permute-start(bf16[2,64,8,128]{3,2,1,0:T(8,128)(2,1)S(1)} %bitcast.15), channel_id=1, source_target_pairs={{0,2},{2,0},{1,3},{3,1},{4,6},{6,4},{5,7},{7,5},{8,10},{10,8},{9,1... | collective-permute-start | bytes 786440 | tf_op jit(solution)/shard_map/ppermute | solution.py:177
  18.7 4.1 %all-to-all-done.rows_ref = bf16[16,8,512]{2,1,0:T(8,128)(2,1)S(1)} async-done(((bf16[16,8,512]{2,1,0:T(8,128)(2,1)}), bf16[16,8,512]{2,1,0:T(8,128)(2,1)S(1)}, u32[]{:S(2)}, u32[]{:S(2)}) %all-to-all-start) | async-done | bytes 131104 | tf_op jit(solution)/shard_map/all_to_all | solution.py:167
  22.9 0.6 shard_map.77
  23.5 11.4 %all-to-all-start.1 = ((bf16[32,8,128]{2,1,0:T(8,128)(2,1)}), bf16[32,8,128]{2,1,0:T(8,128)(2,1)S(1)}, u32[]{:S(2)}, u32[]{:S(2)}) async-start(bf16[32,8,128]{2,1,0:T(8,128)(2,1)} %shard_map.77), calls=%async_computation.1 | async-start | bytes 131072 | tf_op jit(solution)/shard_map/all_to_all | solution.py:167
  34.9 0.0 copy-start.3
  35.0 0.1 pad_add_fusion.place_ref
  35.0 0.0 collective-permute-done.other_ref
  35.0 0.6 copy-done.3
  35.6 0.8 shard_map.78
  36.4 8.8 %all-to-all-done.1.slow_ref = bf16[32,8,128]{2,1,0:T(8,128)(2,1)S(1)} async-done(((bf16[32,8,128]{2,1,0:T(8,128)(2,1)}), bf16[32,8,128]{2,1,0:T(8,128)(2,1)S(1)}, u32[]{:S(2)}, u32[]{:S(2)}) %all-to-all-start.1) | async-done | bytes 65568 | tf_op jit(solution)/shard_map/all_to_all | solution.py:167
  45.1 1.9 %shard_map.79 = bf16[128,8,256]{2,1,0:T(8,128)(2,1)} custom-call(s32[2]{0:T(128)S(1)} %pad_add_fusion.place_ref, bf16[32,8,128]{2,1,0:T(8,128)(2,1)S(1)} %all-to-all-done.1.slow_ref, bf16[2,64,8,128]{3,2,1,0:T(8,128)(2,1)S(1)} %get-tuple-element.9.own_ref, bf16[2,64,8,128]{3,2,1,0:T(8,128)(2,1)S(1)} %get-tuple-element.10.other_ref, ...), custom_call_target="tpu_custom_call" | custom-call | flops 6000000 | bytes 1300000 | tf_op jit(solution)/shard_map/pallas_call | solution.py:197
  47.0 6.2 %all-to-all-start.2 = ((bf16[128,8,256]{2,1,0:T(8,128)(2,1)}), bf16[128,8,256]{2,1,0:T(8,128)(2,1)S(1)}, u32[]{:S(2)}, u32[]{:S(2)}) async-start(bf16[128,8,256]{2,1,0:T(8,128)(2,1)} %shard_map.79), calls=%async_computation.2 | async-start | bytes 1048576 | tf_op jit(solution)/shard_map/all_to_all | solution.py:167
  53.2 0.0 copy-start
  53.3 0.0 copy-start.1
  53.3 2.7 %shard_map.80.shift_ref = bf16[2,512,512]{2,1,0:T(8,128)(2,1)S(1)} custom-call(s32[1]{0:T(128)} %bitcast.6.slot_ref, s32[128]{0:T(128)S(1)} %copy-done.3), custom_call_target="tpu_custom_call" | custom-call | flops 10000000 | bytes 2100000 | tf_op jit(solution)/shard_map/pallas_call | solution.py:208
  56.0 13.6 %all-to-all-done.2.wave_ref = bf16[128,8,256]{2,1,0:T(8,128)(2,1)S(1)} async-done(((bf16[128,8,256]{2,1,0:T(8,128)(2,1)}), bf16[128,8,256]{2,1,0:T(8,128)(2,1)S(1)}, u32[]{:S(2)}, u32[]{:S(2)}) %all-to-all-start.2) | async-done | bytes 524320 | tf_op jit(solution)/shard_map/all_to_all | solution.py:167
  69.6 0.0 copy-done
  69.6 0.0 copy-done.1
  69.6 0.7 shard_map.81.own_ref
  70.4 5.3 %collective-permute-start.1 = (bf16[2,2,512,128]{3,2,1,0:T(8,128)(2,1)S(1)}, bf16[2,2,512,128]{3,2,1,0:T(8,128)(2,1)S(1)}, u32[]{:S(2)}, u32[]{:S(2)}) collective-permute-start(bf16[2,2,512,128]{3,2,1,0:T(8,128)(2,1)S(1)} %shard_map.81.own_ref), channel_id=1, source_target_pairs={{0,1},{1,0},{2,3},{3,2},{4,5},{5,4},{6,7},{7,6},{8,9},{9,8},{10,11... | collective-permute-start | bytes 1572872 | tf_op jit(solution)/shard_map/ppermute | solution.py:228
  75.7 1.5 %collective-permute-done.1.other_ref = bf16[2,2,512,128]{3,2,1,0:T(8,128)(2,1)S(1)} collective-permute-done((bf16[2,2,512,128]{3,2,1,0:T(8,128)(2,1)S(1)}, bf16[2,2,512,128]{3,2,1,0:T(8,128)(2,1)S(1)}, u32[]{:S(2)}, u32[]{:S(2)}) %collective-permute-start.1) | collective-permute-done | bytes 524320 | tf_op jit(solution)/shard_map/ppermute | solution.py:228
  77.2 3.3 %shard_map.82 = (bf16[2,128,512]{2,1,0:T(8,128)(2,1)}, bf16[128,4,128]{2,1,0:T(4,128)(2,1)S(1)}) custom-call(s32[1]{0:T(128)} %bitcast.tile_ref, bf16[2,2,512,128]{3,2,1,0:T(8,128)(2,1)S(1)} %shard_map.81.own_ref, bf16[2,2,512,128]{3,2,1,0:T(8,128)(2,1)S(1)} %collective-permute-done.1.other_ref, bf16[512,512]{1,0:T(8,128)(2,1)S(1)} %copy-done.1, ...), custom_call_target="tpu_custom_call" | custom-call | flops 1620000000 | bytes 4600000 | tf_op jit(solution)/shard_map/pallas_call | solution.py:229
  80.5 17.5 %all_to_all.20 = bf16[128,4,128]{2,1,0:T(4,128)(2,1)S(1)} all-to-all(bf16[128,4,128]{2,1,0:T(4,128)(2,1)S(1)} %get-tuple-element.15), channel_id=1, replica_groups=mesh['y4'=2,'y2'=2,'y1'=2,'w'=2,'z4'=2,'z2'=2,'z1'=2,'h'=2,'c'=2] {'z1',..., dimensions={0} | all-to-all | bytes 262144 | tf_op jit(solution)/shard_map/all_to_all | solution.py:167
  98.1 0.7 convert_reduce_fusion
Async XLA Ops:
  0.6 13.1 %copy-start.2 = (bf16[2,128,4,128]{3,2,1,0:T(4,128)(2,1)S(1)}, bf16[2,128,4,128]{3,2,1,0:T(4,128)(2,1)}, u32[]{:S(2)}) copy-start(bf16[2,128,4,128]{3,2,1,0:T(4,128)(2,1)} %param.6) | copy-start | bytes 786436
  0.6 22.2 %all-to-all-start = ((bf16[16,8,512]{2,1,0:T(8,128)(2,1)}), bf16[16,8,512]{2,1,0:T(8,128)(2,1)S(1)}, u32[]{:S(2)}, u32[]{:S(2)}) async-start(bf16[16,8,512]{2,1,0:T(8,128)(2,1)} %bitcast.17), calls=%async_computation | async-start | bytes 262144 | tf_op jit(solution)/shard_map/all_to_all | solution.py:167
  13.7 21.3 %collective-permute-start = (bf16[2,64,8,128]{3,2,1,0:T(8,128)(2,1)S(1)}, bf16[2,64,8,128]{3,2,1,0:T(8,128)(2,1)S(1)}, u32[]{:S(2)}, u32[]{:S(2)}) collective-permute-start(bf16[2,64,8,128]{3,2,1,0:T(8,128)(2,1)S(1)} %bitcast.15), channel_id=1, source_target_pairs={{0,2},{2,0},{1,3},{3,1},{4,6},{6,4},{5,7},{7,5},{8,10},{10,8},{9,1... | collective-permute-start | bytes 786440 | tf_op jit(solution)/shard_map/ppermute | solution.py:177
  23.5 21.6 %all-to-all-start.1 = ((bf16[32,8,128]{2,1,0:T(8,128)(2,1)}), bf16[32,8,128]{2,1,0:T(8,128)(2,1)S(1)}, u32[]{:S(2)}, u32[]{:S(2)}) async-start(bf16[32,8,128]{2,1,0:T(8,128)(2,1)} %shard_map.77), calls=%async_computation.1 | async-start | bytes 131072 | tf_op jit(solution)/shard_map/all_to_all | solution.py:167
  34.9 0.7 copy-start.3
  47.0 22.6 %all-to-all-start.2 = ((bf16[128,8,256]{2,1,0:T(8,128)(2,1)}), bf16[128,8,256]{2,1,0:T(8,128)(2,1)S(1)}, u32[]{:S(2)}, u32[]{:S(2)}) async-start(bf16[128,8,256]{2,1,0:T(8,128)(2,1)} %shard_map.79), calls=%async_computation.2 | async-start | bytes 1048576 | tf_op jit(solution)/shard_map/all_to_all | solution.py:167
  53.2 16.4 %copy-start = (bf16[512,512]{1,0:T(8,128)(2,1)S(1)}, bf16[512,512]{1,0:T(8,128)(2,1)}, u32[]{:S(2)}) copy-start(bf16[512,512]{1,0:T(8,128)(2,1)} %constant.77.clone.sin_ref) | copy-start | bytes 1572868
  53.3 16.4 %copy-start.1 = (bf16[512,512]{1,0:T(8,128)(2,1)S(1)}, bf16[512,512]{1,0:T(8,128)(2,1)}, u32[]{:S(2)}) copy-start(bf16[512,512]{1,0:T(8,128)(2,1)} %constant.76.clone.cos_ref) | copy-start | bytes 1572868
  70.4 6.9 %collective-permute-start.1 = (bf16[2,2,512,128]{3,2,1,0:T(8,128)(2,1)S(1)}, bf16[2,2,512,128]{3,2,1,0:T(8,128)(2,1)S(1)}, u32[]{:S(2)}, u32[]{:S(2)}) collective-permute-start(bf16[2,2,512,128]{3,2,1,0:T(8,128)(2,1)S(1)} %shard_map.81.own_ref), channel_id=1, source_target_pairs={{0,1},{1,0},{2,3},{3,2},{4,5},{5,4},{6,7},{7,6},{8,9},{9,8},{10,11... | collective-permute-start | bytes 1572872 | tf_op jit(solution)/shard_map/ppermute | solution.py:228

commit v4 on v1

--- a/solution.py
+++ b/solution.py
@@ -38,16 +38,16 @@
     return total
 
 
-def pick_kernel(owner_ref, rows_ref, out_ref):
-    rows = rows_ref[owner_ref[0] // 2 % 16].astype(jnp.float32)
-    for l in range(2):
+def scatter_kernel(slow_ref, out_ref):
+    for at in range(0, 32, 4):
+        slow = slow_ref[0, 4 * at : 4 * at + 16, :].astype(jnp.float32)
         for c in range(2):
-            lanes = (c * tile_size, (2 + c) * tile_size)
-            piece = jnp.concatenate([rows[4 * l : 4 * l + 4, lane : lane + tile_size] for lane in lanes], axis=0)
-            piece = piece.astype(jnp.bfloat16)
-            for u in range(4):
+            for k in range(4):
+                rows = slow[4 * k : 4 * k + 4]
+                pieces = [rows[:, lane : lane + tile_size] for lane in (c * tile_size, (2 + c) * tile_size)]
+                piece = jnp.concatenate(pieces, axis=0).astype(jnp.bfloat16)
                 for h in range(2):
-                    out_ref[((u * 2 + l) * 2 + h) * 2 + c] = piece
+                    out_ref[(at + k) * 4 + h * 2 + c] = piece
 
 
 def shift_kernel(slot_ref, ids_ref, shift_ref):
@@ -99,9 +99,8 @@
             wave_imag = ref[1, pair].astype(jnp.float32)
             real = wave_real * lens_cos - wave_imag * lens_sin
             imag = wave_real * lens_sin + wave_imag * lens_cos
-            lanes = slice(block * tile_size, (block + 1) * tile_size)
-            out_ref[2 * pair, :, lanes] = jnp.concatenate([real[:4], imag[:4]], axis=0).astype(jnp.bfloat16)
-            out_ref[2 * pair + 1, :, lanes] = jnp.concatenate([real[4:], imag[4:]], axis=0).astype(jnp.bfloat16)
+            both = jnp.concatenate([real[:4], imag[:4], real[4:], imag[4:]], axis=0).astype(jnp.bfloat16)
+            out_ref[pair, :, block * tile_size : (block + 1) * tile_size] = both
 
 
 def column_kernel(cos_ref, sin_ref, wave_ref, out_ref, both):
@@ -165,17 +164,18 @@
     side = lax.axis_index("h").astype(jnp.int32)
     tile = 2 * side + lax.axis_index("c").astype(jnp.int32)
     wavefield = wavefield.reshape(2, slots // 2, 8, tile_size)
-    pieces = exchange(slowness.reshape(16, 8, size), ("v", "w", "z"))
+    pieces = pl.pallas_call(
+        scatter_kernel,
+        out_shape=jax.ShapeDtypeStruct((slots, 8, tile_size), jnp.bfloat16),
+        in_specs=[whole()],
+        out_specs=whole(),
+        compiler_params=pltpu.CompilerParams(vmem_limit_bytes=8 << 20),
+        cost_estimate=pl.CostEstimate(flops=10_000, bytes_accessed=400_000, transcendentals=0),
+    )(slowness)
+    pieces = exchange(pieces, ("v", "w", "z", "l", "h", "c")).reshape(32, 4, 8, tile_size)
     other = lax.ppermute(wavefield, "h", swap)
-    pieces = pl.pallas_call(
-        pick_kernel,
-        out_shape=jax.ShapeDtypeStruct((32, 8, tile_size), jnp.bfloat16),
-        in_specs=[whole(pltpu.SMEM), whole()],
-        out_specs=whole(),
-        compiler_params=pltpu.CompilerParams(vmem_limit_bytes=8 << 20),
-        cost_estimate=pl.CostEstimate(flops=10_000, bytes_accessed=100_000, transcendentals=0),
-    )(depth_owner, pieces)
-    pieces = exchange(pieces, ("u", "l", "h", "c"))
+    pieces = lax.dynamic_index_in_dim(pieces, owner % 32, 0, keepdims=False)
+    pieces = exchange(pieces, "u")
     half = jax.ShapeDtypeStruct((2, slots // 2, 8, tile_size), jnp.bfloat16)
     own, other, factors = pl.pallas_call(
         pack_kernel,
@@ -185,16 +185,16 @@
         compiler_params=pltpu.CompilerParams(vmem_limit_bytes=8 << 20),
         cost_estimate=pl.CostEstimate(flops=300_000, bytes_accessed=1_300_000, transcendentals=0),
     )(freq_ids, wavefield, other)
-    place = (owner // 32 * 2 + owner % 2) * 4 + lax.axis_index("u").astype(jnp.int32)
+    place = owner // 32
     lensed = pl.pallas_call(
         lens_kernel,
-        out_shape=jax.ShapeDtypeStruct((slots, 8, 2 * tile_size), jnp.bfloat16),
+        out_shape=jax.ShapeDtypeStruct((slots // 2, 16, 2 * tile_size), jnp.bfloat16),
         in_specs=[whole(pltpu.SMEM)] + [whole()] * 4,
         out_specs=whole(),
         compiler_params=pltpu.CompilerParams(vmem_limit_bytes=8 << 20),
         cost_estimate=pl.CostEstimate(flops=6_000_000, bytes_accessed=1_300_000, transcendentals=0),
     )(jnp.stack([place, side]), pieces, own, other, factors)
-    columns = exchange(lensed, freq)
+    columns = exchange(lensed.reshape(slots, 8, 2 * tile_size), freq)
 
     table_cos, table_sin = dft_table(size)
     shift = pl.pallas_call(

time: 100 us -> 101 us (1.010)
  local copies, waits for them, and re-layouts: 0.59 us -> 2.09 us
    all_to_all x3, starting transfers between devices: 30.6 us -> 28.8 us  [exchange(): return lax.all_to_all(x, axes, split_axis=0, concat_axis=0, tiled=True)]
    ppermute x1, starting transfers between devices: 5.34 us -> 6.4 us  [local(): beside = lax.ppermute(own, 'c', swap)]
  transfers between devices with their start and end apart: 5 -> 5, of which waited for: 4 -> 4; matrix products, arithmetic and copies ran while one was open for 0% -> 1% of each run, Pallas kernels for 4% -> 3%
where the time goes in v4:
time: 101 us; the launch traced here: 100 us
  starting transfers between devices  40 us (40%)
  waiting for transfers between devices  28.5 us (28%)
  blocking collectives  17.3 us (17%)
  Pallas kernels  10.1 us (10%)
  local copies, waits for them, and re-layouts  2.09 us (2%)
  between operations  1.43 us (1%)
    all_to_all x3, starting transfers between devices, exchange(): return lax.all_to_all(x, axes, split_axis=0, concat_axis=0, tiled=True)  28.8 us
    all_to_all x3, waiting for transfers between devices, exchange(): return lax.all_to_all(x, axes, split_axis=0, concat_axis=0, tiled=True)  27 us
    all_to_all x1, blocking collectives, exchange(): return lax.all_to_all(x, axes, split_axis=0, concat_axis=0, tiled=True)  17.3 us
    ppermute x1, starting transfers between devices, local(): beside = lax.ppermute(own, 'c', swap)  6.4 us
    ppermute x1, starting transfers between devices, local(): other = lax.ppermute(wavefield, 'h', swap)  4.8 us
    pallas_call x1, Pallas kernels, local(): pl.pallas_call(step_kernel, out_shape=(jax.ShapeDtypeStruct((2, tile_size...  3.22 us
    pallas_call x1, Pallas kernels, local(): pl.pallas_call(shift_kernel, out_shape=jax.ShapeDtypeStruct((2, size, siz...  2.74 us
  transfers between devices with their start and end apart: 5, of which 4 were waited for; matrix products, arithmetic and copies ran while one was open for 1% of the time, Pallas kernels for 3%

profile of v4, /device:TPU:1, one launch (start us, length us, event | category | flops | bytes accessed | tf_op | source)
XLA Modules:
  0.0 100.3 jit_solution(14726798384513080711)
XLA Ops:
  0.6 0.0 copy-start.3
  0.6 0.9 copy-done.3
  1.5 0.7 shard_map.77
  2.3 0.0 copy-start.2
  2.3 16.8 %all-to-all-start = ((bf16[128,8,128]{2,1,0:T(8,128)(2,1)}), bf16[128,8,128]{2,1,0:T(8,128)(2,1)S(1)}, u32[]{:S(2)}, u32[]{:S(2)}) async-start(bf16[128,8,128]{2,1,0:T(8,128)(2,1)} %shard_map.77), calls=%async_computation | async-start | bytes 524288 | tf_op jit(solution)/shard_map/all_to_all | solution.py:158
  19.1 0.0 copy-done.2
  19.1 4.8 %collective-permute-start = (bf16[2,64,8,128]{3,2,1,0:T(8,128)(2,1)S(1)}, bf16[2,64,8,128]{3,2,1,0:T(8,128)(2,1)S(1)}, u32[]{:S(2)}, u32[]{:S(2)}) collective-permute-start(bf16[2,64,8,128]{3,2,1,0:T(8,128)(2,1)S(1)} %bitcast.19), channel_id=1, source_target_pairs={{0,2},{2,0},{1,3},{3,1},{4,6},{6,4},{5,7},{7,5},{8,10},{10,8},{9,1... | collective-permute-start | bytes 786440 | tf_op jit(solution)/shard_map/ppermute | solution.py:176
  24.5 7.9 %all-to-all-done = bf16[128,8,128]{2,1,0:T(8,128)(2,1)S(1)} async-done(((bf16[128,8,128]{2,1,0:T(8,128)(2,1)}), bf16[128,8,128]{2,1,0:T(8,128)(2,1)S(1)}, u32[]{:S(2)}, u32[]{:S(2)}) %all-to-all-start) | async-done | bytes 262176 | tf_op jit(solution)/shard_map/all_to_all | solution.py:158
  32.5 0.6 dynamic-slice_bitcast_fusion
  33.1 5.9 %all-to-all-start.1 = ((bf16[4,8,128]{2,1,0:T(8,128)(2,1)}), bf16[4,8,128]{2,1,0:T(8,128)(2,1)S(1)}, u32[]{:S(2)}, u32[]{:S(2)}) async-start(bf16[4,8,128]{2,1,0:T(8,128)(2,1)} %dynamic-slice_bitcast_fusion), calls=%async_computation.1 | async-start | bytes 16384 | tf_op jit(solution)/shard_map/all_to_all | solution.py:158
  39.0 0.0 copy-start.4
  39.0 0.1 pad_add_fusion.place_ref
  39.1 0.0 collective-permute-done.other_ref
  39.1 0.6 copy-done.4
  39.7 0.8 shard_map.78
  40.4 5.2 %all-to-all-done.1.slow_ref = bf16[4,8,128]{2,1,0:T(8,128)(2,1)S(1)} async-done(((bf16[4,8,128]{2,1,0:T(8,128)(2,1)}), bf16[4,8,128]{2,1,0:T(8,128)(2,1)S(1)}, u32[]{:S(2)}, u32[]{:S(2)}) %all-to-all-start.1) | async-done | bytes 8224 | tf_op jit(solution)/shard_map/all_to_all | solution.py:158
  45.6 1.9 %shard_map.79 = bf16[64,16,256]{2,1,0:T(8,128)(2,1)} custom-call(s32[2]{0:T(128)S(1)} %pad_add_fusion.place_ref, bf16[4,8,128]{2,1,0:T(8,128)(2,1)S(1)} %all-to-all-done.1.slow_ref, bf16[2,64,8,128]{3,2,1,0:T(8,128)(2,1)S(1)} %get-tuple-element.9.own_ref, bf16[2,64,8,128]{3,2,1,0:T(8,128)(2,1)S(1)} %get-tuple-element.10.other_ref, ...), custom_call_target="tpu_custom_call" | custom-call | flops 6000000 | bytes 1300000 | tf_op jit(solution)/shard_map/pallas_call | solution.py:189
  47.5 6.2 %all-to-all-start.2 = ((bf16[128,8,256]{2,1,0:T(8,128)(2,1)}), bf16[128,8,256]{2,1,0:T(8,128)(2,1)S(1)}, u32[]{:S(2)}, u32[]{:S(2)}) async-start(bf16[128,8,256]{2,1,0:T(8,128)(2,1)} %bitcast.7), calls=%async_computation.2 | async-start | bytes 1048576 | tf_op jit(solution)/shard_map/all_to_all | solution.py:158
  53.7 0.0 copy-start
  53.7 0.0 copy-start.1
  53.7 2.7 %shard_map.80.shift_ref = bf16[2,512,512]{2,1,0:T(8,128)(2,1)S(1)} custom-call(s32[1]{0:T(128)} %bitcast.8.slot_ref, s32[128]{0:T(128)S(1)} %copy-done.4), custom_call_target="tpu_custom_call" | custom-call | flops 10000000 | bytes 2100000 | tf_op jit(solution)/shard_map/pallas_call | solution.py:200
  56.5 13.9 %all-to-all-done.2.wave_ref = bf16[128,8,256]{2,1,0:T(8,128)(2,1)S(1)} async-done(((bf16[128,8,256]{2,1,0:T(8,128)(2,1)}), bf16[128,8,256]{2,1,0:T(8,128)(2,1)S(1)}, u32[]{:S(2)}, u32[]{:S(2)}) %all-to-all-start.2) | async-done | bytes 524320 | tf_op jit(solution)/shard_map/all_to_all | solution.py:158
  70.4 0.0 copy-done
  70.4 0.0 copy-done.1
  70.4 0.7 shard_map.81.own_ref
  71.1 6.4 %collective-permute-start.1 = (bf16[2,2,512,128]{3,2,1,0:T(8,128)(2,1)S(1)}, bf16[2,2,512,128]{3,2,1,0:T(8,128)(2,1)S(1)}, u32[]{:S(2)}, u32[]{:S(2)}) collective-permute-start(bf16[2,2,512,128]{3,2,1,0:T(8,128)(2,1)S(1)} %shard_map.81.own_ref), channel_id=1, source_target_pairs={{0,1},{1,0},{2,3},{3,2},{4,5},{5,4},{6,7},{7,6},{8,9},{9,8},{10,11... | collective-permute-start | bytes 1572872 | tf_op jit(solution)/shard_map/ppermute | solution.py:220
  77.5 1.5 %collective-permute-done.1.other_ref = bf16[2,2,512,128]{3,2,1,0:T(8,128)(2,1)S(1)} collective-permute-done((bf16[2,2,512,128]{3,2,1,0:T(8,128)(2,1)S(1)}, bf16[2,2,512,128]{3,2,1,0:T(8,128)(2,1)S(1)}, u32[]{:S(2)}, u32[]{:S(2)}) %collective-permute-start.1) | collective-permute-done | bytes 524320 | tf_op jit(solution)/shard_map/ppermute | solution.py:220
  79.0 3.2 %shard_map.82 = (bf16[2,128,512]{2,1,0:T(8,128)(2,1)}, bf16[512,128]{1,0:T(8,128)(2,1)S(1)}) custom-call(s32[1]{0:T(128)} %bitcast.tile_ref, bf16[2,2,512,128]{3,2,1,0:T(8,128)(2,1)S(1)} %shard_map.81.own_ref, bf16[2,2,512,128]{3,2,1,0:T(8,128)(2,1)S(1)} %collective-permute-done.1.other_ref, bf16[512,512]{1,0:T(8,128)(2,1)S(1)} %copy-done.1, ...), custom_call_target="tpu_custom_call" | custom-call | flops 1620000000 | bytes 4600000 | tf_op jit(solution)/shard_map/pallas_call | solution.py:221
  82.2 17.3 %all_to_all.20 = bf16[128,4,128]{2,1,0:T(4,128)(2,1)S(1)} all-to-all(bf16[128,4,128]{2,1,0:T(4,128)(2,1)S(1)} %bitcast.21), channel_id=1, replica_groups=mesh['u'=4,'v'=2,'w'=2,'z'=4,'l'=2,'h'=2,'c'=2] {'u','v','w','z','l'}, dimensions={0} | all-to-all | bytes 262144 | tf_op jit(solution)/shard_map/all_to_all | solution.py:158
  99.5 0.7 convert_reduce_fusion
Async XLA Ops:
  0.6 0.9 copy-start.3
  2.3 16.8 %copy-start.2 = (bf16[2,128,4,128]{3,2,1,0:T(4,128)(2,1)S(1)}, bf16[2,128,4,128]{3,2,1,0:T(4,128)(2,1)}, u32[]{:S(2)}) copy-start(bf16[2,128,4,128]{3,2,1,0:T(4,128)(2,1)} %param.6) | copy-start | bytes 786436
  2.3 30.2 %all-to-all-start = ((bf16[128,8,128]{2,1,0:T(8,128)(2,1)}), bf16[128,8,128]{2,1,0:T(8,128)(2,1)S(1)}, u32[]{:S(2)}, u32[]{:S(2)}) async-start(bf16[128,8,128]{2,1,0:T(8,128)(2,1)} %shard_map.77), calls=%async_computation | async-start | bytes 524288 | tf_op jit(solution)/shard_map/all_to_all | solution.py:158
  19.1 20.0 %collective-permute-start = (bf16[2,64,8,128]{3,2,1,0:T(8,128)(2,1)S(1)}, bf16[2,64,8,128]{3,2,1,0:T(8,128)(2,1)S(1)}, u32[]{:S(2)}, u32[]{:S(2)}) collective-permute-start(bf16[2,64,8,128]{3,2,1,0:T(8,128)(2,1)S(1)} %bitcast.19), channel_id=1, source_target_pairs={{0,2},{2,0},{1,3},{3,1},{4,6},{6,4},{5,7},{7,5},{8,10},{10,8},{9,1... | collective-permute-start | bytes 786440 | tf_op jit(solution)/shard_map/ppermute | solution.py:176
  33.1 12.5 %all-to-all-start.1 = ((bf16[4,8,128]{2,1,0:T(8,128)(2,1)}), bf16[4,8,128]{2,1,0:T(8,128)(2,1)S(1)}, u32[]{:S(2)}, u32[]{:S(2)}) async-start(bf16[4,8,128]{2,1,0:T(8,128)(2,1)} %dynamic-slice_bitcast_fusion), calls=%async_computation.1 | async-start | bytes 16384 | tf_op jit(solution)/shard_map/all_to_all | solution.py:158
  39.0 0.7 copy-start.4
  47.5 22.8 %all-to-all-start.2 = ((bf16[128,8,256]{2,1,0:T(8,128)(2,1)}), bf16[128,8,256]{2,1,0:T(8,128)(2,1)S(1)}, u32[]{:S(2)}, u32[]{:S(2)}) async-start(bf16[128,8,256]{2,1,0:T(8,128)(2,1)} %bitcast.7), calls=%async_computation.2 | async-start | bytes 1048576 | tf_op jit(solution)/shard_map/all_to_all | solution.py:158
  53.7 16.7 %copy-start = (bf16[512,512]{1,0:T(8,128)(2,1)S(1)}, bf16[512,512]{1,0:T(8,128)(2,1)}, u32[]{:S(2)}) copy-start(bf16[512,512]{1,0:T(8,128)(2,1)} %constant.69.clone.sin_ref) | copy-start | bytes 1572868
  53.7 16.6 %copy-start.1 = (bf16[512,512]{1,0:T(8,128)(2,1)S(1)}, bf16[512,512]{1,0:T(8,128)(2,1)}, u32[]{:S(2)}) copy-start(bf16[512,512]{1,0:T(8,128)(2,1)} %constant.68.clone.cos_ref) | copy-start | bytes 1572868
  71.1 7.9 %collective-permute-start.1 = (bf16[2,2,512,128]{3,2,1,0:T(8,128)(2,1)S(1)}, bf16[2,2,512,128]{3,2,1,0:T(8,128)(2,1)S(1)}, u32[]{:S(2)}, u32[]{:S(2)}) collective-permute-start(bf16[2,2,512,128]{3,2,1,0:T(8,128)(2,1)S(1)} %shard_map.81.own_ref), channel_id=1, source_target_pairs={{0,1},{1,0},{2,3},{3,2},{4,5},{5,4},{6,7},{7,6},{8,9},{9,8},{10,11... | collective-permute-start | bytes 1572872 | tf_op jit(solution)/shard_map/ppermute | solution.py:220

commit v5 on v3

--- a/solution.py
+++ b/solution.py
@@ -26,11 +26,8 @@
 def dft_table(length):
     places = np.arange(length)
     angles = 2.0 * np.pi / length * (places[:, None] * places[None, :] % length)
-    factor = 1.0 / math.sqrt(length)
-    return (
-        (np.cos(angles) * factor).astype(jnp.bfloat16),
-        (np.sin(angles) * factor).astype(jnp.bfloat16),
-    )
+    both = np.concatenate([np.cos(angles), np.sin(angles)])
+    return (both * (1.0 / math.sqrt(length))).astype(jnp.bfloat16)
 
 
 def dot(left, right):
@@ -110,14 +107,14 @@
             out_ref[place_of(2 * pair + 1), :, lanes] = jnp.concatenate([real[4:], imag[4:]], axis=0).astype(jnp.bfloat16)
 
 
-def column_kernel(cos_ref, sin_ref, wave_ref, out_ref, both):
+def column_kernel(table_ref, wave_ref, out_ref, both):
     for at in range(0, size // 4, 4):
         tiles = [wave_ref[place_of(at + k)].astype(jnp.float32) for k in range(4)]
         for part in range(2):
             rows = jnp.concatenate([tile[4 * part : 4 * part + 4] for tile in tiles], axis=0)
             both[4 * at : 4 * at + 16, part * 2 * tile_size : (part + 1) * 2 * tile_size] = rows.astype(jnp.bfloat16)
-    by_cos = dot(cos_ref[...], both[...])
-    by_sin = dot(sin_ref[...], both[...])
+    by_cos = dot(table_ref[:size], both[...])
+    by_sin = dot(table_ref[size:], both[...])
     real = (by_cos[:, : 2 * tile_size] + by_sin[:, 2 * tile_size :]).astype(jnp.bfloat16)
     imag = (by_cos[:, 2 * tile_size :] - by_sin[:, : 2 * tile_size]).astype(jnp.bfloat16)
     for block in range(2):
@@ -126,35 +123,43 @@
         out_ref[block, 1] = imag[:, lanes]
 
 
-def step_kernel(tile_ref, own_ref, other_ref, cos_ref, sin_ref, shift_ref, wave_ref, image_ref, field, back):
+def step_kernel(tile_ref, own_ref, other_ref, table_ref, shift_ref, wave_ref, image_ref, field, back):
     tile = tile_ref[0]
     for flip in range(4):
         block = (own_ref, other_ref)[flip % 2]
         start = pl.multiple_of((tile ^ flip) * tile_size, tile_size)
-        field[:, :, pl.ds(start, tile_size)] = block[flip // 2]
-    rows = pl.ds(pl.multiple_of(tile * tile_size, tile_size), tile_size)
-    inverse = jnp.concatenate([cos_ref[rows, :], sin_ref[rows, :]], axis=0)
+        real, imag = block[flip // 2, 0], block[flip // 2, 1]
+        field[:size, pl.ds(start, tile_size)] = real
+        field[size:, pl.ds(start, tile_size)] = imag
+        start = pl.multiple_of(start + size, tile_size)
+        field[:size, pl.ds(start, tile_size)] = imag
+        field[size:, pl.ds(start, tile_size)] = -real
+    start = pl.multiple_of(tile * tile_size, tile_size)
+    cos_rows = table_ref[pl.ds(start, tile_size), :]
+    sin_rows = table_ref[pl.ds(pl.multiple_of(start + size, tile_size), tile_size), :]
+    inverse = jnp.concatenate(
+        [jnp.concatenate([cos_rows, -sin_rows], axis=1), jnp.concatenate([sin_rows, cos_rows], axis=1)], axis=0
+    )
     width = 256
     for at in range(0, size, width):
         part = slice(at, at + width)
-        spec_real = dot(field[0], cos_ref[:, part]) + dot(field[1], sin_ref[:, part])
-        spec_imag = dot(field[1], cos_ref[:, part]) - dot(field[0], sin_ref[:, part])
+        far = slice(at + size, at + size + width)
+        spectrum = dot(field[...], table_ref[:, part])
+        spec_real, spec_imag = spectrum[:size], spectrum[size:]
         shift_real = shift_ref[0, :, part].astype(jnp.float32)
         shift_imag = shift_ref[1, :, part].astype(jnp.float32)
         shifted_real = (spec_real * shift_real - spec_imag * shift_imag).astype(jnp.bfloat16)
         shifted_imag = (spec_real * shift_imag + spec_imag * shift_real).astype(jnp.bfloat16)
-        from_real = dot(inverse, shifted_real)
-        from_imag = dot(inverse, shifted_imag)
-        back[:tile_size, part] = (from_real[:tile_size] - from_imag[tile_size:]).astype(jnp.bfloat16)
-        back[tile_size:, part] = (from_imag[:tile_size] + from_real[tile_size:]).astype(jnp.bfloat16)
+        rows = dot(inverse, jnp.concatenate([shifted_real, shifted_imag], axis=0)).astype(jnp.bfloat16)
+        back[:, part] = rows
+        back[:tile_size, far] = -rows[tile_size:]
+        back[tile_size:, far] = rows[:tile_size]
     for at in range(0, size, width):
         part = slice(at, at + width)
-        by_cos = dot(back[...], cos_ref[:, part])
-        by_sin = dot(back[...], sin_ref[:, part])
-        field_real = by_cos[:tile_size] - by_sin[tile_size:]
-        wave_ref[0, :, part] = field_real.astype(jnp.bfloat16)
-        wave_ref[1, :, part] = (by_cos[tile_size:] + by_sin[:tile_size]).astype(jnp.bfloat16)
-        image = (field_real * (1.0 / math.sqrt(slots))).T.astype(jnp.bfloat16)
+        rows = dot(back[...], table_ref[:, part])
+        wave_ref[0, :, part] = rows[:tile_size].astype(jnp.bfloat16)
+        wave_ref[1, :, part] = rows[tile_size:].astype(jnp.bfloat16)
+        image = (rows[:tile_size] * (1.0 / math.sqrt(slots))).T.astype(jnp.bfloat16)
         for slot in range(at // 4, (at + width) // 4):
             image_ref[place_of(slot)] = image[4 * slot - at : 4 * slot - at + 4]
 
@@ -204,7 +209,6 @@
     )(jnp.stack([place, side]), pieces, own, other, factors)
     columns = exchange(lensed, mixed)
 
-    table_cos, table_sin = dft_table(size)
     shift = pl.pallas_call(
         shift_kernel,
         out_shape=jax.ShapeDtypeStruct((2, size, size), jnp.bfloat16),
@@ -215,16 +219,16 @@
     )(lax.axis_index(freq).astype(jnp.int32)[None], freq_ids)
     columns, shift = lax.optimization_barrier((columns, shift))
 
-    table_cos, table_sin = jnp.asarray(table_cos), jnp.asarray(table_sin)
+    table = jnp.asarray(dft_table(size))
     own = pl.pallas_call(
         column_kernel,
         out_shape=jax.ShapeDtypeStruct((2, 2, size, tile_size), jnp.bfloat16),
-        in_specs=[whole()] * 3,
+        in_specs=[whole()] * 2,
         out_specs=whole(),
         scratch_shapes=[pltpu.VMEM((size, 4 * tile_size), jnp.bfloat16)],
         compiler_params=pltpu.CompilerParams(vmem_limit_bytes=8 << 20),
         cost_estimate=pl.CostEstimate(flops=540_000_000, bytes_accessed=2_100_000, transcendentals=0),
-    )(table_cos, table_sin, columns)
+    )(table, columns)
     beside = lax.ppermute(own, "c", swap)
     wave_next, parts = pl.pallas_call(
         step_kernel,
@@ -232,15 +236,15 @@
             jax.ShapeDtypeStruct((2, tile_size, size), jnp.bfloat16),
             jax.ShapeDtypeStruct((slots, size // slots, tile_size), jnp.bfloat16),
         ),
-        in_specs=[whole(pltpu.SMEM)] + [whole()] * 5,
+        in_specs=[whole(pltpu.SMEM)] + [whole()] * 4,
         out_specs=(whole(), whole()),
         scratch_shapes=[
-            pltpu.VMEM((2, size, size), jnp.bfloat16),
-            pltpu.VMEM((2 * tile_size, size), jnp.bfloat16),
+            pltpu.VMEM((2 * size, 2 * size), jnp.bfloat16),
+            pltpu.VMEM((2 * tile_size, 2 * size), jnp.bfloat16),
         ],
         compiler_params=pltpu.CompilerParams(vmem_limit_bytes=20 << 20),
         cost_estimate=pl.CostEstimate(flops=1_620_000_000, bytes_accessed=4_600_000, transcendentals=0),
-    )(tile[None], own, beside, table_cos, table_sin, shift)
+    )(tile[None], own, beside, table, shift)
     parts = exchange(parts, mixed)
     image = jnp.sum(parts.astype(jnp.float32), axis=0).T
     return (wave_next[:, None], image)

time: 99.5 us -> 101 us (1.015)
  Pallas kernels: 10.1 us -> 11.5 us
    pallas_call x1, Pallas kernels: 3.28 us -> 4.67 us  [local(): pl.pallas_call(step_kernel, out_shape=(jax.ShapeDtypeStruct((2, tile_size...]
where the time goes in v5:
time: 101 us; the launch traced here: 100 us
  starting transfers between devices  40.4 us (40%)
  waiting for transfers between devices  28.1 us (28%)
  blocking collectives  17.5 us (17%)
  Pallas kernels  11.5 us (11%)
  between operations  1.44 us (1%)
    all_to_all x3, starting transfers between devices, exchange(): return lax.all_to_all(x, axes, split_axis=0, concat_axis=0, tiled=True)  30.7 us
    all_to_all x3, waiting for transfers between devices, exchange(): return lax.all_to_all(x, axes, split_axis=0, concat_axis=0, tiled=True)  26.6 us
    all_to_all x1, blocking collectives, exchange(): return lax.all_to_all(x, axes, split_axis=0, concat_axis=0, tiled=True)  17.5 us
    ppermute x1, starting transfers between devices, local(): beside = lax.ppermute(own, 'c', swap)  5.33 us
    pallas_call x1, Pallas kernels, local(): pl.pallas_call(step_kernel, out_shape=(jax.ShapeDtypeStruct((2, tile_size...  4.67 us
    ppermute x1, starting transfers between devices, local(): other = lax.ppermute(wavefield, 'h', swap)  4.36 us
    pallas_call x1, Pallas kernels, local(): pl.pallas_call(shift_kernel, out_shape=jax.ShapeDtypeStruct((2, size, siz...  2.74 us
  transfers between devices with their start and end apart: 5, of which 4 were waited for; matrix products, arithmetic and copies ran while one was open for 0% of the time, Pallas kernels for 4%

profile of v5, /device:TPU:1, one launch (start us, length us, event | category | flops | bytes accessed | tf_op | source)
XLA Modules:
  0.0 100.3 jit_solution(4794567438353222636)
XLA Ops:
  0.6 0.0 copy-start.1
  0.6 13.0 %all-to-all-start = ((bf16[16,8,512]{2,1,0:T(8,128)(2,1)}), bf16[16,8,512]{2,1,0:T(8,128)(2,1)S(1)}, u32[]{:S(2)}, u32[]{:S(2)}) async-start(bf16[16,8,512]{2,1,0:T(8,128)(2,1)} %bitcast.17), calls=%async_computation | async-start | bytes 262144 | tf_op jit(solution)/shard_map/all_to_all | solution.py:172
  13.7 0.0 copy-done.1
  13.7 4.4 %collective-permute-start = (bf16[2,64,8,128]{3,2,1,0:T(8,128)(2,1)S(1)}, bf16[2,64,8,128]{3,2,1,0:T(8,128)(2,1)S(1)}, u32[]{:S(2)}, u32[]{:S(2)}) collective-permute-start(bf16[2,64,8,128]{3,2,1,0:T(8,128)(2,1)S(1)} %bitcast.15), channel_id=1, source_target_pairs={{0,2},{2,0},{1,3},{3,1},{4,6},{6,4},{5,7},{7,5},{8,10},{10,8},{9,1... | collective-permute-start | bytes 786440 | tf_op jit(solution)/shard_map/ppermute | solution.py:182
  18.7 4.1 %all-to-all-done.rows_ref = bf16[16,8,512]{2,1,0:T(8,128)(2,1)S(1)} async-done(((bf16[16,8,512]{2,1,0:T(8,128)(2,1)}), bf16[16,8,512]{2,1,0:T(8,128)(2,1)S(1)}, u32[]{:S(2)}, u32[]{:S(2)}) %all-to-all-start) | async-done | bytes 131104 | tf_op jit(solution)/shard_map/all_to_all | solution.py:172
  22.9 0.6 shard_map.68
  23.5 11.4 %all-to-all-start.1 = ((bf16[32,8,128]{2,1,0:T(8,128)(2,1)}), bf16[32,8,128]{2,1,0:T(8,128)(2,1)S(1)}, u32[]{:S(2)}, u32[]{:S(2)}) async-start(bf16[32,8,128]{2,1,0:T(8,128)(2,1)} %shard_map.68), calls=%async_computation.1 | async-start | bytes 131072 | tf_op jit(solution)/shard_map/all_to_all | solution.py:172
  34.9 0.0 copy-start.2
  35.0 0.1 pad_add_fusion.place_ref
  35.0 0.0 collective-permute-done.other_ref
  35.0 0.6 copy-done.2
  35.6 0.8 shard_map.69
  36.4 8.8 %all-to-all-done.1.slow_ref = bf16[32,8,128]{2,1,0:T(8,128)(2,1)S(1)} async-done(((bf16[32,8,128]{2,1,0:T(8,128)(2,1)}), bf16[32,8,128]{2,1,0:T(8,128)(2,1)S(1)}, u32[]{:S(2)}, u32[]{:S(2)}) %all-to-all-start.1) | async-done | bytes 65568 | tf_op jit(solution)/shard_map/all_to_all | solution.py:172
  45.1 1.9 %shard_map.70 = bf16[128,8,256]{2,1,0:T(8,128)(2,1)} custom-call(s32[2]{0:T(128)S(1)} %pad_add_fusion.place_ref, bf16[32,8,128]{2,1,0:T(8,128)(2,1)S(1)} %all-to-all-done.1.slow_ref, bf16[2,64,8,128]{3,2,1,0:T(8,128)(2,1)S(1)} %get-tuple-element.9.own_ref, bf16[2,64,8,128]{3,2,1,0:T(8,128)(2,1)S(1)} %get-tuple-element.10.other_ref, ...), custom_call_target="tpu_custom_call" | custom-call | flops 6000000 | bytes 1300000 | tf_op jit(solution)/shard_map/pallas_call | solution.py:202
  47.1 0.0 copy-start
  47.1 6.3 %all-to-all-start.2 = ((bf16[128,8,256]{2,1,0:T(8,128)(2,1)}), bf16[128,8,256]{2,1,0:T(8,128)(2,1)S(1)}, u32[]{:S(2)}, u32[]{:S(2)}) async-start(bf16[128,8,256]{2,1,0:T(8,128)(2,1)} %shard_map.70), calls=%async_computation.2 | async-start | bytes 1048576 | tf_op jit(solution)/shard_map/all_to_all | solution.py:172
  53.4 2.7 %shard_map.71.shift_ref = bf16[2,512,512]{2,1,0:T(8,128)(2,1)S(1)} custom-call(s32[1]{0:T(128)} %bitcast.6.slot_ref, s32[128]{0:T(128)S(1)} %copy-done.2), custom_call_target="tpu_custom_call" | custom-call | flops 10000000 | bytes 2100000 | tf_op jit(solution)/shard_map/pallas_call | solution.py:212
  56.1 13.6 %all-to-all-done.2.wave_ref = bf16[128,8,256]{2,1,0:T(8,128)(2,1)S(1)} async-done(((bf16[128,8,256]{2,1,0:T(8,128)(2,1)}), bf16[128,8,256]{2,1,0:T(8,128)(2,1)S(1)}, u32[]{:S(2)}, u32[]{:S(2)}) %all-to-all-start.2) | async-done | bytes 524320 | tf_op jit(solution)/shard_map/all_to_all | solution.py:172
  69.8 0.0 copy-done
  69.8 0.7 shard_map.72.own_ref
  70.5 5.3 %collective-permute-start.1 = (bf16[2,2,512,128]{3,2,1,0:T(8,128)(2,1)S(1)}, bf16[2,2,512,128]{3,2,1,0:T(8,128)(2,1)S(1)}, u32[]{:S(2)}, u32[]{:S(2)}) collective-permute-start(bf16[2,2,512,128]{3,2,1,0:T(8,128)(2,1)S(1)} %shard_map.72.own_ref), channel_id=1, source_target_pairs={{0,1},{1,0},{2,3},{3,2},{4,5},{5,4},{6,7},{7,6},{8,9},{9,8},{10,11... | collective-permute-start | bytes 1572872 | tf_op jit(solution)/shard_map/ppermute | solution.py:232
  75.9 1.5 %collective-permute-done.1.other_ref = bf16[2,2,512,128]{3,2,1,0:T(8,128)(2,1)S(1)} collective-permute-done((bf16[2,2,512,128]{3,2,1,0:T(8,128)(2,1)S(1)}, bf16[2,2,512,128]{3,2,1,0:T(8,128)(2,1)S(1)}, u32[]{:S(2)}, u32[]{:S(2)}) %collective-permute-start.1) | collective-permute-done | bytes 524320 | tf_op jit(solution)/shard_map/ppermute | solution.py:232
  77.4 4.7 %shard_map.73 = (bf16[2,128,512]{2,1,0:T(8,128)(2,1)}, bf16[128,4,128]{2,1,0:T(4,128)(2,1)S(1)}) custom-call(s32[1]{0:T(128)} %bitcast.tile_ref, bf16[2,2,512,128]{3,2,1,0:T(8,128)(2,1)S(1)} %shard_map.72.own_ref, bf16[2,2,512,128]{3,2,1,0:T(8,128)(2,1)S(1)} %collective-permute-done.1.other_ref, bf16[1024,512]{1,0:T(8,128)(2,1)S(1)} %copy-done, ...), custom_call_target="tpu_custom_call" | custom-call | flops 1620000000 | bytes 4600000 | tf_op jit(solution)/shard_map/pallas_call | solution.py:233
  82.0 17.5 %all_to_all.20 = bf16[128,4,128]{2,1,0:T(4,128)(2,1)S(1)} all-to-all(bf16[128,4,128]{2,1,0:T(4,128)(2,1)S(1)} %get-tuple-element.15), channel_id=1, replica_groups=mesh['y4'=2,'y2'=2,'y1'=2,'w'=2,'z4'=2,'z2'=2,'z1'=2,'h'=2,'c'=2] {'z1',..., dimensions={0} | all-to-all | bytes 262144 | tf_op jit(solution)/shard_map/all_to_all | solution.py:172
  99.6 0.7 convert_reduce_fusion
Async XLA Ops:
  0.6 13.1 %copy-start.1 = (bf16[2,128,4,128]{3,2,1,0:T(4,128)(2,1)S(1)}, bf16[2,128,4,128]{3,2,1,0:T(4,128)(2,1)}, u32[]{:S(2)}) copy-start(bf16[2,128,4,128]{3,2,1,0:T(4,128)(2,1)} %param.5) | copy-start | bytes 786436
  0.6 22.2 %all-to-all-start = ((bf16[16,8,512]{2,1,0:T(8,128)(2,1)}), bf16[16,8,512]{2,1,0:T(8,128)(2,1)S(1)}, u32[]{:S(2)}, u32[]{:S(2)}) async-start(bf16[16,8,512]{2,1,0:T(8,128)(2,1)} %bitcast.17), calls=%async_computation | async-start | bytes 262144 | tf_op jit(solution)/shard_map/all_to_all | solution.py:172
  13.7 21.3 %collective-permute-start = (bf16[2,64,8,128]{3,2,1,0:T(8,128)(2,1)S(1)}, bf16[2,64,8,128]{3,2,1,0:T(8,128)(2,1)S(1)}, u32[]{:S(2)}, u32[]{:S(2)}) collective-permute-start(bf16[2,64,8,128]{3,2,1,0:T(8,128)(2,1)S(1)} %bitcast.15), channel_id=1, source_target_pairs={{0,2},{2,0},{1,3},{3,1},{4,6},{6,4},{5,7},{7,5},{8,10},{10,8},{9,1... | collective-permute-start | bytes 786440 | tf_op jit(solution)/shard_map/ppermute | solution.py:182
  23.5 21.6 %all-to-all-start.1 = ((bf16[32,8,128]{2,1,0:T(8,128)(2,1)}), bf16[32,8,128]{2,1,0:T(8,128)(2,1)S(1)}, u32[]{:S(2)}, u32[]{:S(2)}) async-start(bf16[32,8,128]{2,1,0:T(8,128)(2,1)} %shard_map.68), calls=%async_computation.1 | async-start | bytes 131072 | tf_op jit(solution)/shard_map/all_to_all | solution.py:172
  34.9 0.7 copy-start.2
  47.1 22.7 %copy-start = (bf16[1024,512]{1,0:T(8,128)(2,1)S(1)}, bf16[1024,512]{1,0:T(8,128)(2,1)}, u32[]{:S(2)}) copy-start(bf16[1024,512]{1,0:T(8,128)(2,1)} %constant.74.clone.table_ref) | copy-start | bytes 3145732
  47.1 22.7 %all-to-all-start.2 = ((bf16[128,8,256]{2,1,0:T(8,128)(2,1)}), bf16[128,8,256]{2,1,0:T(8,128)(2,1)S(1)}, u32[]{:S(2)}, u32[]{:S(2)}) async-start(bf16[128,8,256]{2,1,0:T(8,128)(2,1)} %shard_map.70), calls=%async_computation.2 | async-start | bytes 1048576 | tf_op jit(solution)/shard_map/all_to_all | solution.py:172
  70.5 6.9 %collective-permute-start.1 = (bf16[2,2,512,128]{3,2,1,0:T(8,128)(2,1)S(1)}, bf16[2,2,512,128]{3,2,1,0:T(8,128)(2,1)S(1)}, u32[]{:S(2)}, u32[]{:S(2)}) collective-permute-start(bf16[2,2,512,128]{3,2,1,0:T(8,128)(2,1)S(1)} %shard_map.72.own_ref), channel_id=1, source_target_pairs={{0,1},{1,0},{2,3},{3,2},{4,5},{5,4},{6,7},{7,6},{8,9},{9,8},{10,11... | collective-permute-start | bytes 1572872 | tf_op jit(solution)/shard_map/ppermute | solution.py:232

commit v6 on v3

--- a/solution.py
+++ b/solution.py
@@ -44,16 +44,21 @@
     return total
 
 
+def rows_kernel(slow_ref, out_ref):
+    for at in range(0, 32, 4):
+        slow = slow_ref[0, 4 * at : 4 * at + 16, :].astype(jnp.float32)
+        for k in range(4):
+            out_ref[at + k] = slow[4 * k : 4 * k + 4].astype(jnp.bfloat16)
+
+
 def pick_kernel(owner_ref, rows_ref, out_ref):
-    rows = rows_ref[owner_ref[0] // 2 % 16].astype(jnp.float32)
-    for l in range(2):
-        for c in range(2):
-            lanes = (c * tile_size, (2 + c) * tile_size)
-            piece = jnp.concatenate([rows[4 * l : 4 * l + 4, lane : lane + tile_size] for lane in lanes], axis=0)
-            piece = piece.astype(jnp.bfloat16)
-            for u in range(4):
-                for h in range(2):
-                    out_ref[((u * 2 + l) * 2 + h) * 2 + c] = piece
+    rows = rows_ref[owner_ref[0] % 32].astype(jnp.float32)
+    for c in range(2):
+        lanes = (c * tile_size, (2 + c) * tile_size)
+        piece = jnp.concatenate([rows[:, lane : lane + tile_size] for lane in lanes], axis=0).astype(jnp.bfloat16)
+        for u in range(4):
+            for h in range(2):
+                out_ref[(u * 2 + h) * 2 + c] = piece
 
 
 def shift_kernel(slot_ref, ids_ref, shift_ref):
@@ -173,17 +178,25 @@
     side = lax.axis_index("h").astype(jnp.int32)
     tile = 2 * side + lax.axis_index("c").astype(jnp.int32)
     wavefield = wavefield.reshape(2, slots // 2, 8, tile_size)
-    pieces = exchange(slowness.reshape(16, 8, size), ("y1", "w", "z4", "z2"))
+    pieces = pl.pallas_call(
+        rows_kernel,
+        out_shape=jax.ShapeDtypeStruct((32, 4, size), jnp.bfloat16),
+        in_specs=[whole()],
+        out_specs=whole(),
+        compiler_params=pltpu.CompilerParams(vmem_limit_bytes=8 << 20),
+        cost_estimate=pl.CostEstimate(flops=10_000, bytes_accessed=260_000, transcendentals=0),
+    )(slowness)
+    pieces = exchange(pieces, ("y1", "w", "z4", "z2", "z1"))
     other = lax.ppermute(wavefield, "h", swap)
     pieces = pl.pallas_call(
         pick_kernel,
-        out_shape=jax.ShapeDtypeStruct((32, 8, tile_size), jnp.bfloat16),
+        out_shape=jax.ShapeDtypeStruct((16, 8, tile_size), jnp.bfloat16),
         in_specs=[whole(pltpu.SMEM), whole()],
         out_specs=whole(),
         compiler_params=pltpu.CompilerParams(vmem_limit_bytes=8 << 20),
         cost_estimate=pl.CostEstimate(flops=10_000, bytes_accessed=100_000, transcendentals=0),
     )(depth_owner, pieces)
-    pieces = exchange(pieces, ("y4", "y2", "z1", "h", "c"))
+    pieces = exchange(pieces, ("y4", "y2", "h", "c"))
     half = jax.ShapeDtypeStruct((2, slots // 2, 8, tile_size), jnp.bfloat16)
     own, other, factors = pl.pallas_call(
         pack_kernel,
@@ -193,7 +206,7 @@
         compiler_params=pltpu.CompilerParams(vmem_limit_bytes=8 << 20),
         cost_estimate=pl.CostEstimate(flops=300_000, bytes_accessed=1_300_000, transcendentals=0),
     )(freq_ids, wavefield, other)
-    place = (owner // 32 * 2 + owner % 2) * 4 + lax.axis_index(("y4", "y2")).astype(jnp.int32)
+    place = owner // 32 * 4 + lax.axis_index(("y4", "y2")).astype(jnp.int32)
     lensed = pl.pallas_call(
         lens_kernel,
         out_shape=jax.ShapeDtypeStruct((slots, 8, 2 * tile_size), jnp.bfloat16),

time: 99.5 us -> 99.1 us (level)
  starting transfers between devices: 40.3 us -> 38.3 us
    ppermute x1, starting transfers between devices: 5.33 us -> 4.1 us  [local(): beside = lax.ppermute(own, 'c', swap)]
where the time goes in v6:
time: 99.1 us; the launch traced here: 98.4 us
  starting transfers between devices  38.3 us (39%)
  waiting for transfers between devices  28 us (28%)
  blocking collectives  17.7 us (18%)
  Pallas kernels  10.6 us (11%)
  local copies, waits for them, and re-layouts  1.53 us (2%)
  between operations  1.44 us (1%)
    all_to_all x3, starting transfers between devices, exchange(): return lax.all_to_all(x, axes, split_axis=0, concat_axis=0, tiled=True)  29.8 us
    all_to_all x3, waiting for transfers between devices, exchange(): return lax.all_to_all(x, axes, split_axis=0, concat_axis=0, tiled=True)  26.4 us
    all_to_all x1, blocking collectives, exchange(): return lax.all_to_all(x, axes, split_axis=0, concat_axis=0, tiled=True)  17.7 us
    ppermute x1, starting transfers between devices, local(): other = lax.ppermute(wavefield, 'h', swap)  4.36 us
    ppermute x1, starting transfers between devices, local(): beside = lax.ppermute(own, 'c', swap)  4.1 us
    pallas_call x1, Pallas kernels, local(): pl.pallas_call(step_kernel, out_shape=(jax.ShapeDtypeStruct((2, tile_size...  3.22 us
    pallas_call x1, Pallas kernels, local(): pl.pallas_call(shift_kernel, out_shape=jax.ShapeDtypeStruct((2, size, siz...  2.74 us
  transfers between devices with their start and end apart: 5, of which 4 were waited for; matrix products, arithmetic and copies ran while one was open for 0% of the time, Pallas kernels for 4%

profile of v6, /device:TPU:1, one launch (start us, length us, event | category | flops | bytes accessed | tf_op | source)
XLA Modules:
  0.0 98.4 jit_solution(3004727938596567766)
XLA Ops:
  0.6 0.0 copy-start.2
  0.6 0.0 copy-start.3
  0.6 0.9 copy-done.3
  1.6 0.7 shard_map.77
  2.3 13.2 %all-to-all-start = ((bf16[32,4,512]{2,1,0:T(4,128)(2,1)}), bf16[32,4,512]{2,1,0:T(4,128)(2,1)S(1)}, u32[]{:S(2)}, u32[]{:S(2)}) async-start(bf16[32,4,512]{2,1,0:T(4,128)(2,1)} %shard_map.77), calls=%async_computation | async-start | bytes 262144 | tf_op jit(solution)/shard_map/all_to_all | solution.py:172
  15.5 0.0 copy-done.2
  15.5 4.4 %collective-permute-start = (bf16[2,64,8,128]{3,2,1,0:T(8,128)(2,1)S(1)}, bf16[2,64,8,128]{3,2,1,0:T(8,128)(2,1)S(1)}, u32[]{:S(2)}, u32[]{:S(2)}) collective-permute-start(bf16[2,64,8,128]{3,2,1,0:T(8,128)(2,1)S(1)} %bitcast.14), channel_id=1, source_target_pairs={{0,2},{2,0},{1,3},{3,1},{4,6},{6,4},{5,7},{7,5},{8,10},{10,8},{9,1... | collective-permute-start | bytes 786440 | tf_op jit(solution)/shard_map/ppermute | solution.py:190
  20.5 3.4 %all-to-all-done.rows_ref = bf16[32,4,512]{2,1,0:T(4,128)(2,1)S(1)} async-done(((bf16[32,4,512]{2,1,0:T(4,128)(2,1)}), bf16[32,4,512]{2,1,0:T(4,128)(2,1)S(1)}, u32[]{:S(2)}, u32[]{:S(2)}) %all-to-all-start) | async-done | bytes 131104 | tf_op jit(solution)/shard_map/all_to_all | solution.py:172
  24.0 0.6 shard_map.78
  24.6 10.5 %all-to-all-start.1 = ((bf16[16,8,128]{2,1,0:T(8,128)(2,1)}), bf16[16,8,128]{2,1,0:T(8,128)(2,1)S(1)}, u32[]{:S(2)}, u32[]{:S(2)}) async-start(bf16[16,8,128]{2,1,0:T(8,128)(2,1)} %shard_map.78), calls=%async_computation.1 | async-start | bytes 65536 | tf_op jit(solution)/shard_map/all_to_all | solution.py:172
  35.1 0.0 copy-start.4
  35.1 0.1 pad_add_fusion.place_ref
  35.2 0.0 collective-permute-done.other_ref
  35.2 0.6 copy-done.4
  35.7 0.8 shard_map.79
  36.5 8.3 %all-to-all-done.1.slow_ref = bf16[16,8,128]{2,1,0:T(8,128)(2,1)S(1)} async-done(((bf16[16,8,128]{2,1,0:T(8,128)(2,1)}), bf16[16,8,128]{2,1,0:T(8,128)(2,1)S(1)}, u32[]{:S(2)}, u32[]{:S(2)}) %all-to-all-start.1) | async-done | bytes 32800 | tf_op jit(solution)/shard_map/all_to_all | solution.py:172
  44.8 1.9 %shard_map.80 = bf16[128,8,256]{2,1,0:T(8,128)(2,1)} custom-call(s32[2]{0:T(128)S(1)} %pad_add_fusion.place_ref, bf16[16,8,128]{2,1,0:T(8,128)(2,1)S(1)} %all-to-all-done.1.slow_ref, bf16[2,64,8,128]{3,2,1,0:T(8,128)(2,1)S(1)} %get-tuple-element.9.own_ref, bf16[2,64,8,128]{3,2,1,0:T(8,128)(2,1)S(1)} %get-tuple-element.10.other_ref, ...), custom_call_target="tpu_custom_call" | custom-call | flops 6000000 | bytes 1300000 | tf_op jit(solution)/shard_map/pallas_call | solution.py:210
  46.7 6.2 %all-to-all-start.2 = ((bf16[128,8,256]{2,1,0:T(8,128)(2,1)}), bf16[128,8,256]{2,1,0:T(8,128)(2,1)S(1)}, u32[]{:S(2)}, u32[]{:S(2)}) async-start(bf16[128,8,256]{2,1,0:T(8,128)(2,1)} %shard_map.80), calls=%async_computation.2 | async-start | bytes 1048576 | tf_op jit(solution)/shard_map/all_to_all | solution.py:172
  52.9 0.0 copy-start
  52.9 0.0 copy-start.1
  52.9 2.7 %shard_map.81.shift_ref = bf16[2,512,512]{2,1,0:T(8,128)(2,1)S(1)} custom-call(s32[1]{0:T(128)} %bitcast.5.slot_ref, s32[128]{0:T(128)S(1)} %copy-done.4), custom_call_target="tpu_custom_call" | custom-call | flops 10000000 | bytes 2100000 | tf_op jit(solution)/shard_map/pallas_call | solution.py:221
  55.7 14.7 %all-to-all-done.2.wave_ref = bf16[128,8,256]{2,1,0:T(8,128)(2,1)S(1)} async-done(((bf16[128,8,256]{2,1,0:T(8,128)(2,1)}), bf16[128,8,256]{2,1,0:T(8,128)(2,1)S(1)}, u32[]{:S(2)}, u32[]{:S(2)}) %all-to-all-start.2) | async-done | bytes 524320 | tf_op jit(solution)/shard_map/all_to_all | solution.py:172
  70.4 0.0 copy-done
  70.4 0.0 copy-done.1
  70.4 0.7 shard_map.82.own_ref
  71.1 4.1 %collective-permute-start.1 = (bf16[2,2,512,128]{3,2,1,0:T(8,128)(2,1)S(1)}, bf16[2,2,512,128]{3,2,1,0:T(8,128)(2,1)S(1)}, u32[]{:S(2)}, u32[]{:S(2)}) collective-permute-start(bf16[2,2,512,128]{3,2,1,0:T(8,128)(2,1)S(1)} %shard_map.82.own_ref), channel_id=1, source_target_pairs={{0,1},{1,0},{2,3},{3,2},{4,5},{5,4},{6,7},{7,6},{8,9},{9,8},{10,11... | collective-permute-start | bytes 1572872 | tf_op jit(solution)/shard_map/ppermute | solution.py:241
  75.2 1.5 %collective-permute-done.1.other_ref = bf16[2,2,512,128]{3,2,1,0:T(8,128)(2,1)S(1)} collective-permute-done((bf16[2,2,512,128]{3,2,1,0:T(8,128)(2,1)S(1)}, bf16[2,2,512,128]{3,2,1,0:T(8,128)(2,1)S(1)}, u32[]{:S(2)}, u32[]{:S(2)}) %collective-permute-start.1) | collective-permute-done | bytes 524320 | tf_op jit(solution)/shard_map/ppermute | solution.py:241
  76.7 3.2 %shard_map.83 = (bf16[2,128,512]{2,1,0:T(8,128)(2,1)}, bf16[128,4,128]{2,1,0:T(4,128)(2,1)S(1)}) custom-call(s32[1]{0:T(128)} %bitcast.tile_ref, bf16[2,2,512,128]{3,2,1,0:T(8,128)(2,1)S(1)} %shard_map.82.own_ref, bf16[2,2,512,128]{3,2,1,0:T(8,128)(2,1)S(1)} %collective-permute-done.1.other_ref, bf16[512,512]{1,0:T(8,128)(2,1)S(1)} %copy-done.1, ...), custom_call_target="tpu_custom_call" | custom-call | flops 1620000000 | bytes 4600000 | tf_op jit(solution)/shard_map/pallas_call | solution.py:242
  79.9 17.7 %all_to_all.20 = bf16[128,4,128]{2,1,0:T(4,128)(2,1)S(1)} all-to-all(bf16[128,4,128]{2,1,0:T(4,128)(2,1)S(1)} %get-tuple-element.15), channel_id=1, replica_groups=mesh['y4'=2,'y2'=2,'y1'=2,'w'=2,'z4'=2,'z2'=2,'z1'=2,'h'=2,'c'=2] {'z1',..., dimensions={0} | all-to-all | bytes 262144 | tf_op jit(solution)/shard_map/all_to_all | solution.py:172
  97.6 0.7 convert_reduce_fusion
Async XLA Ops:
  0.6 14.8 %copy-start.2 = (bf16[2,128,4,128]{3,2,1,0:T(4,128)(2,1)S(1)}, bf16[2,128,4,128]{3,2,1,0:T(4,128)(2,1)}, u32[]{:S(2)}) copy-start(bf16[2,128,4,128]{3,2,1,0:T(4,128)(2,1)} %param.6) | copy-start | bytes 786436
  0.6 0.9 copy-start.3
  2.3 21.7 %all-to-all-start = ((bf16[32,4,512]{2,1,0:T(4,128)(2,1)}), bf16[32,4,512]{2,1,0:T(4,128)(2,1)S(1)}, u32[]{:S(2)}, u32[]{:S(2)}) async-start(bf16[32,4,512]{2,1,0:T(4,128)(2,1)} %shard_map.77), calls=%async_computation | async-start | bytes 262144 | tf_op jit(solution)/shard_map/all_to_all | solution.py:172
  15.5 19.7 %collective-permute-start = (bf16[2,64,8,128]{3,2,1,0:T(8,128)(2,1)S(1)}, bf16[2,64,8,128]{3,2,1,0:T(8,128)(2,1)S(1)}, u32[]{:S(2)}, u32[]{:S(2)}) collective-permute-start(bf16[2,64,8,128]{3,2,1,0:T(8,128)(2,1)S(1)} %bitcast.14), channel_id=1, source_target_pairs={{0,2},{2,0},{1,3},{3,1},{4,6},{6,4},{5,7},{7,5},{8,10},{10,8},{9,1... | collective-permute-start | bytes 786440 | tf_op jit(solution)/shard_map/ppermute | solution.py:190
  24.6 20.2 %all-to-all-start.1 = ((bf16[16,8,128]{2,1,0:T(8,128)(2,1)}), bf16[16,8,128]{2,1,0:T(8,128)(2,1)S(1)}, u32[]{:S(2)}, u32[]{:S(2)}) async-start(bf16[16,8,128]{2,1,0:T(8,128)(2,1)} %shard_map.78), calls=%async_computation.1 | async-start | bytes 65536 | tf_op jit(solution)/shard_map/all_to_all | solution.py:172
  35.1 0.7 copy-start.4
  46.7 23.6 %all-to-all-start.2 = ((bf16[128,8,256]{2,1,0:T(8,128)(2,1)}), bf16[128,8,256]{2,1,0:T(8,128)(2,1)S(1)}, u32[]{:S(2)}, u32[]{:S(2)}) async-start(bf16[128,8,256]{2,1,0:T(8,128)(2,1)} %shard_map.80), calls=%async_computation.2 | async-start | bytes 1048576 | tf_op jit(solution)/shard_map/all_to_all | solution.py:172
  52.9 17.5 %copy-start = (bf16[512,512]{1,0:T(8,128)(2,1)S(1)}, bf16[512,512]{1,0:T(8,128)(2,1)}, u32[]{:S(2)}) copy-start(bf16[512,512]{1,0:T(8,128)(2,1)} %constant.68.clone.sin_ref) | copy-start | bytes 1572868
  52.9 17.4 %copy-start.1 = (bf16[512,512]{1,0:T(8,128)(2,1)S(1)}, bf16[512,512]{1,0:T(8,128)(2,1)}, u32[]{:S(2)}) copy-start(bf16[512,512]{1,0:T(8,128)(2,1)} %constant.67.clone.cos_ref) | copy-start | bytes 1572868
  71.1 5.6 %collective-permute-start.1 = (bf16[2,2,512,128]{3,2,1,0:T(8,128)(2,1)S(1)}, bf16[2,2,512,128]{3,2,1,0:T(8,128)(2,1)S(1)}, u32[]{:S(2)}, u32[]{:S(2)}) collective-permute-start(bf16[2,2,512,128]{3,2,1,0:T(8,128)(2,1)S(1)} %shard_map.82.own_ref), channel_id=1, source_target_pairs={{0,1},{1,0},{2,3},{3,2},{4,5},{5,4},{6,7},{7,6},{8,9},{9,8},{10,11... | collective-permute-start | bytes 1572872 | tf_op jit(solution)/shard_map/ppermute | solution.py:241

commit v7 on v6

--- a/solution.py
+++ b/solution.py
@@ -15,12 +15,6 @@
 size = 512
 tile_size = 128
 freq = ("y4", "y2", "y1", "w", "z4", "z2", "z1")
-mixed = ("z1", "y1", "w", "z2", "y2", "z4", "y4")
-
-
-def place_of(slot):
-    bits = {axis: slot >> (len(freq) - 1 - at) & 1 for at, axis in enumerate(freq)}
-    return sum(bits[axis] << (len(mixed) - 1 - at) for at, axis in enumerate(mixed))
 
 
 def dft_table(length):
@@ -94,30 +88,36 @@
         factor_ref[pair] = jnp.where(first, low, high)
 
 
-def lens_kernel(place_ref, slow_ref, own_ref, other_ref, factor_ref, out_ref):
+def lens_kernel(place_ref, slow_ref, own_ref, other_ref, factor_ref, out_ref, rows, sems):
     slow = slow_ref[place_ref[0]].astype(jnp.float32) - 1.0
     halves = (jnp.concatenate([slow[:4]] * 2, axis=0), jnp.concatenate([slow[4:]] * 2, axis=0))
     low = place_ref[1] == 0
     depths = (jnp.where(low, halves[0], halves[1]), jnp.where(low, halves[1], halves[0]))
-    for pair in range(slots // 2):
-        factor = factor_ref[pair]
-        for block, (ref, depth) in enumerate(zip((own_ref, other_ref), depths)):
-            phase = factor * depth
-            square = phase * phase
-            lens_cos = series(square, 0, 8)
-            lens_sin = phase * series(square, 1, 9)
-            wave_real = ref[0, pair].astype(jnp.float32)
-            wave_imag = ref[1, pair].astype(jnp.float32)
-            real = wave_real * lens_cos - wave_imag * lens_sin
-            imag = wave_real * lens_sin + wave_imag * lens_cos
-            lanes = slice(block * tile_size, (block + 1) * tile_size)
-            out_ref[place_of(2 * pair), :, lanes] = jnp.concatenate([real[:4], imag[:4]], axis=0).astype(jnp.bfloat16)
-            out_ref[place_of(2 * pair + 1), :, lanes] = jnp.concatenate([real[4:], imag[4:]], axis=0).astype(jnp.bfloat16)
+    copies = []
+    for quarter in range(4):
+        for pair in range(quarter * slots // 8, (quarter + 1) * slots // 8):
+            factor = factor_ref[pair]
+            for block, (ref, depth) in enumerate(zip((own_ref, other_ref), depths)):
+                phase = factor * depth
+                square = phase * phase
+                lens_cos = series(square, 0, 8)
+                lens_sin = phase * series(square, 1, 9)
+                wave_real = ref[0, pair].astype(jnp.float32)
+                wave_imag = ref[1, pair].astype(jnp.float32)
+                real = wave_real * lens_cos - wave_imag * lens_sin
+                imag = wave_real * lens_sin + wave_imag * lens_cos
+                both = jnp.concatenate([real[:4], imag[:4], real[4:], imag[4:]], axis=0).astype(jnp.bfloat16)
+                rows[16 * pair : 16 * pair + 16, block * tile_size : (block + 1) * tile_size] = both
+        part = pl.ds(quarter * 2 * slots, 2 * slots)
+        copies.append(pltpu.make_async_copy(rows.at[part], out_ref.at[part], sems.at[quarter]))
+        copies[-1].start()
+    for copy in copies:
+        copy.wait()
 
 
 def column_kernel(cos_ref, sin_ref, wave_ref, out_ref, both):
     for at in range(0, size // 4, 4):
-        tiles = [wave_ref[place_of(at + k)].astype(jnp.float32) for k in range(4)]
+        tiles = [wave_ref[at + k].astype(jnp.float32) for k in range(4)]
         for part in range(2):
             rows = jnp.concatenate([tile[4 * part : 4 * part + 4] for tile in tiles], axis=0)
             both[4 * at : 4 * at + 16, part * 2 * tile_size : (part + 1) * 2 * tile_size] = rows.astype(jnp.bfloat16)
@@ -131,7 +131,7 @@
         out_ref[block, 1] = imag[:, lanes]
 
 
-def step_kernel(tile_ref, own_ref, other_ref, cos_ref, sin_ref, shift_ref, wave_ref, image_ref, field, back):
+def step_kernel(tile_ref, own_ref, other_ref, cos_ref, sin_ref, shift_ref, wave_ref, image_ref, field, back, waves, sem):
     tile = tile_ref[0]
     for flip in range(4):
         block = (own_ref, other_ref)[flip % 2]
@@ -152,16 +152,19 @@
         from_imag = dot(inverse, shifted_imag)
         back[:tile_size, part] = (from_real[:tile_size] - from_imag[tile_size:]).astype(jnp.bfloat16)
         back[tile_size:, part] = (from_imag[:tile_size] + from_real[tile_size:]).astype(jnp.bfloat16)
+    reals = []
     for at in range(0, size, width):
         part = slice(at, at + width)
         by_cos = dot(back[...], cos_ref[:, part])
         by_sin = dot(back[...], sin_ref[:, part])
-        field_real = by_cos[:tile_size] - by_sin[tile_size:]
-        wave_ref[0, :, part] = field_real.astype(jnp.bfloat16)
-        wave_ref[1, :, part] = (by_cos[tile_size:] + by_sin[:tile_size]).astype(jnp.bfloat16)
-        image = (field_real * (1.0 / math.sqrt(slots))).T.astype(jnp.bfloat16)
-        for slot in range(at // 4, (at + width) // 4):
-            image_ref[place_of(slot)] = image[4 * slot - at : 4 * slot - at + 4]
+        reals.append(by_cos[:tile_size] - by_sin[tile_size:])
+        waves[0, :, part] = reals[-1].astype(jnp.bfloat16)
+        waves[1, :, part] = (by_cos[tile_size:] + by_sin[:tile_size]).astype(jnp.bfloat16)
+    copy = pltpu.make_async_copy(waves, wave_ref, sem)
+    copy.start()
+    for at in range(0, size, width):
+        image_ref[at : at + width, :] = (reals[at // width] * (1.0 / math.sqrt(slots))).T.astype(jnp.bfloat16)
+    copy.wait()
 
 
 def whole(memory=pltpu.VMEM):
@@ -209,13 +212,14 @@
     place = owner // 32 * 4 + lax.axis_index(("y4", "y2")).astype(jnp.int32)
     lensed = pl.pallas_call(
         lens_kernel,
-        out_shape=jax.ShapeDtypeStruct((slots, 8, 2 * tile_size), jnp.bfloat16),
+        out_shape=jax.ShapeDtypeStruct((8 * slots, 2 * tile_size), jnp.bfloat16),
         in_specs=[whole(pltpu.SMEM)] + [whole()] * 4,
-        out_specs=whole(),
+        out_specs=whole(pl.ANY),
+        scratch_shapes=[pltpu.VMEM((8 * slots, 2 * tile_size), jnp.bfloat16), pltpu.SemaphoreType.DMA((4,))],
         compiler_params=pltpu.CompilerParams(vmem_limit_bytes=8 << 20),
         cost_estimate=pl.CostEstimate(flops=6_000_000, bytes_accessed=1_300_000, transcendentals=0),
     )(jnp.stack([place, side]), pieces, own, other, factors)
-    columns = exchange(lensed, mixed)
+    columns = exchange(lensed.reshape(slots, 8, 2 * tile_size), freq)
 
     table_cos, table_sin = dft_table(size)
     shift = pl.pallas_call(
@@ -243,18 +247,20 @@
         step_kernel,
         out_shape=(
             jax.ShapeDtypeStruct((2, tile_size, size), jnp.bfloat16),
-            jax.ShapeDtypeStruct((slots, size // slots, tile_size), jnp.bfloat16),
+            jax.ShapeDtypeStruct((size, tile_size), jnp.bfloat16),
         ),
         in_specs=[whole(pltpu.SMEM)] + [whole()] * 5,
-        out_specs=(whole(), whole()),
+        out_specs=(whole(pl.ANY), whole()),
         scratch_shapes=[
             pltpu.VMEM((2, size, size), jnp.bfloat16),
             pltpu.VMEM((2 * tile_size, size), jnp.bfloat16),
+            pltpu.VMEM((2, tile_size, size), jnp.bfloat16),
+            pltpu.SemaphoreType.DMA,
         ],
         compiler_params=pltpu.CompilerParams(vmem_limit_bytes=20 << 20),
         cost_estimate=pl.CostEstimate(flops=1_620_000_000, bytes_accessed=4_600_000, transcendentals=0),
     )(tile[None], own, beside, table_cos, table_sin, shift)
-    parts = exchange(parts, mixed)
+    parts = exchange(parts.reshape(slots, size // slots, tile_size), freq)
     image = jnp.sum(parts.astype(jnp.float32), axis=0).T
     return (wave_next[:, None], image)
 

time: 99.1 us -> 99.7 us (level)
  no operation moved by 1% of the time
where the time goes in v7:
time: 99.7 us; the launch traced here: 99.3 us
  starting transfers between devices  38.8 us (39%)
  waiting for transfers between devices  28.6 us (29%)
  blocking collectives  17.6 us (18%)
  Pallas kernels  10.5 us (11%)
  local copies, waits for them, and re-layouts  1.53 us (2%)
  between operations  1.46 us (1%)
    all_to_all x3, starting transfers between devices, exchange(): return lax.all_to_all(x, axes, split_axis=0, concat_axis=0, tiled=True)  29.9 us
    all_to_all x3, waiting for transfers between devices, exchange(): return lax.all_to_all(x, axes, split_axis=0, concat_axis=0, tiled=True)  27.1 us
    all_to_all x1, blocking collectives, exchange(): return lax.all_to_all(x, axes, split_axis=0, concat_axis=0, tiled=True)  17.6 us
    ppermute x1, starting transfers between devices, local(): beside = lax.ppermute(own, 'c', swap)  4.54 us
    ppermute x1, starting transfers between devices, local(): other = lax.ppermute(wavefield, 'h', swap)  4.36 us
    pallas_call x1, Pallas kernels, local(): pl.pallas_call(step_kernel, out_shape=(jax.ShapeDtypeStruct((2, tile_size...  3.23 us
    pallas_call x1, Pallas kernels, local(): pl.pallas_call(shift_kernel, out_shape=jax.ShapeDtypeStruct((2, size, siz...  2.74 us
  transfers between devices with their start and end apart: 5, of which 4 were waited for; matrix products, arithmetic and copies ran while one was open for 0% of the time, Pallas kernels for 4%

profile of v7, /device:TPU:1, one launch (start us, length us, event | category | flops | bytes accessed | tf_op | source)
XLA Modules:
  0.0 99.3 jit_solution(897361459724775518)
XLA Ops:
  0.6 0.0 copy-start.2
  0.6 0.0 copy-start.3
  0.6 0.9 copy-done.3
  1.6 0.7 shard_map.77
  2.3 13.2 %all-to-all-start = ((bf16[32,4,512]{2,1,0:T(4,128)(2,1)}), bf16[32,4,512]{2,1,0:T(4,128)(2,1)S(1)}, u32[]{:S(2)}, u32[]{:S(2)}) async-start(bf16[32,4,512]{2,1,0:T(4,128)(2,1)} %shard_map.77), calls=%async_computation | async-start | bytes 262144 | tf_op jit(solution)/shard_map/all_to_all | solution.py:175
  15.5 0.0 copy-done.2
  15.5 4.4 %collective-permute-start = (bf16[2,64,8,128]{3,2,1,0:T(8,128)(2,1)S(1)}, bf16[2,64,8,128]{3,2,1,0:T(8,128)(2,1)S(1)}, u32[]{:S(2)}, u32[]{:S(2)}) collective-permute-start(bf16[2,64,8,128]{3,2,1,0:T(8,128)(2,1)S(1)} %bitcast.16), channel_id=1, source_target_pairs={{0,2},{2,0},{1,3},{3,1},{4,6},{6,4},{5,7},{7,5},{8,10},{10,8},{9,1... | collective-permute-start | bytes 786440 | tf_op jit(solution)/shard_map/ppermute | solution.py:193
  20.5 3.4 %all-to-all-done.rows_ref = bf16[32,4,512]{2,1,0:T(4,128)(2,1)S(1)} async-done(((bf16[32,4,512]{2,1,0:T(4,128)(2,1)}), bf16[32,4,512]{2,1,0:T(4,128)(2,1)S(1)}, u32[]{:S(2)}, u32[]{:S(2)}) %all-to-all-start) | async-done | bytes 131104 | tf_op jit(solution)/shard_map/all_to_all | solution.py:175
  24.0 0.6 shard_map.78
  24.6 10.5 %all-to-all-start.1 = ((bf16[16,8,128]{2,1,0:T(8,128)(2,1)}), bf16[16,8,128]{2,1,0:T(8,128)(2,1)S(1)}, u32[]{:S(2)}, u32[]{:S(2)}) async-start(bf16[16,8,128]{2,1,0:T(8,128)(2,1)} %shard_map.78), calls=%async_computation.1 | async-start | bytes 65536 | tf_op jit(solution)/shard_map/all_to_all | solution.py:175
  35.1 0.0 copy-start.4
  35.1 0.1 pad_add_fusion.place_ref
  35.2 0.0 collective-permute-done.other_ref
  35.2 0.6 copy-done.4
  35.7 0.8 shard_map.79
  36.5 8.3 %all-to-all-done.1.slow_ref = bf16[16,8,128]{2,1,0:T(8,128)(2,1)S(1)} async-done(((bf16[16,8,128]{2,1,0:T(8,128)(2,1)}), bf16[16,8,128]{2,1,0:T(8,128)(2,1)S(1)}, u32[]{:S(2)}, u32[]{:S(2)}) %all-to-all-start.1) | async-done | bytes 32800 | tf_op jit(solution)/shard_map/all_to_all | solution.py:175
  44.8 1.8 %shard_map.80 = bf16[1024,256]{1,0:T(8,128)(2,1)} custom-call(s32[2]{0:T(128)S(1)} %pad_add_fusion.place_ref, bf16[16,8,128]{2,1,0:T(8,128)(2,1)S(1)} %all-to-all-done.1.slow_ref, bf16[2,64,8,128]{3,2,1,0:T(8,128)(2,1)S(1)} %get-tuple-element.9.own_ref, bf16[2,64,8,128]{3,2,1,0:T(8,128)(2,1)S(1)} %get-tuple-element.10.other_ref, ...), custom_call_target="tpu_custom_call" | custom-call | flops 6000000 | bytes 1300000 | tf_op jit(solution)/shard_map/pallas_call | solution.py:213
  46.6 6.2 %all-to-all-start.2 = ((bf16[128,8,256]{2,1,0:T(8,128)(2,1)}), bf16[128,8,256]{2,1,0:T(8,128)(2,1)S(1)}, u32[]{:S(2)}, u32[]{:S(2)}) async-start(bf16[128,8,256]{2,1,0:T(8,128)(2,1)} %bitcast.5), calls=%async_computation.2 | async-start | bytes 1048576 | tf_op jit(solution)/shard_map/all_to_all | solution.py:175
  52.8 0.0 copy-start
  52.8 0.0 copy-start.1
  52.8 2.7 %shard_map.81.shift_ref = bf16[2,512,512]{2,1,0:T(8,128)(2,1)S(1)} custom-call(s32[1]{0:T(128)} %bitcast.6.slot_ref, s32[128]{0:T(128)S(1)} %copy-done.4), custom_call_target="tpu_custom_call" | custom-call | flops 10000000 | bytes 2100000 | tf_op jit(solution)/shard_map/pallas_call | solution.py:225
  55.6 15.4 %all-to-all-done.2.wave_ref = bf16[128,8,256]{2,1,0:T(8,128)(2,1)S(1)} async-done(((bf16[128,8,256]{2,1,0:T(8,128)(2,1)}), bf16[128,8,256]{2,1,0:T(8,128)(2,1)S(1)}, u32[]{:S(2)}, u32[]{:S(2)}) %all-to-all-start.2) | async-done | bytes 524320 | tf_op jit(solution)/shard_map/all_to_all | solution.py:175
  71.0 0.0 copy-done
  71.0 0.0 copy-done.1
  71.0 0.7 shard_map.82.own_ref
  71.7 4.5 %collective-permute-start.1 = (bf16[2,2,512,128]{3,2,1,0:T(8,128)(2,1)S(1)}, bf16[2,2,512,128]{3,2,1,0:T(8,128)(2,1)S(1)}, u32[]{:S(2)}, u32[]{:S(2)}) collective-permute-start(bf16[2,2,512,128]{3,2,1,0:T(8,128)(2,1)S(1)} %shard_map.82.own_ref), channel_id=1, source_target_pairs={{0,1},{1,0},{2,3},{3,2},{4,5},{5,4},{6,7},{7,6},{8,9},{9,8},{10,11... | collective-permute-start | bytes 1572872 | tf_op jit(solution)/shard_map/ppermute | solution.py:245
  76.2 1.5 %collective-permute-done.1.other_ref = bf16[2,2,512,128]{3,2,1,0:T(8,128)(2,1)S(1)} collective-permute-done((bf16[2,2,512,128]{3,2,1,0:T(8,128)(2,1)S(1)}, bf16[2,2,512,128]{3,2,1,0:T(8,128)(2,1)S(1)}, u32[]{:S(2)}, u32[]{:S(2)}) %collective-permute-start.1) | collective-permute-done | bytes 524320 | tf_op jit(solution)/shard_map/ppermute | solution.py:245
  77.8 3.2 %shard_map.83 = (bf16[2,128,512]{2,1,0:T(8,128)(2,1)}, bf16[512,128]{1,0:T(8,128)(2,1)S(1)}) custom-call(s32[1]{0:T(128)} %bitcast.tile_ref, bf16[2,2,512,128]{3,2,1,0:T(8,128)(2,1)S(1)} %shard_map.82.own_ref, bf16[2,2,512,128]{3,2,1,0:T(8,128)(2,1)S(1)} %collective-permute-done.1.other_ref, bf16[512,512]{1,0:T(8,128)(2,1)S(1)} %copy-done.1, ...), custom_call_target="tpu_custom_call" | custom-call | flops 1620000000 | bytes 4600000 | tf_op jit(solution)/shard_map/pallas_call | solution.py:246
  81.0 17.6 %all_to_all.20 = bf16[128,4,128]{2,1,0:T(4,128)(2,1)S(1)} all-to-all(bf16[128,4,128]{2,1,0:T(4,128)(2,1)S(1)} %bitcast.18), channel_id=1, replica_groups=mesh['y4'=2,'y2'=2,'y1'=2,'w'=2,'z4'=2,'z2'=2,'z1'=2,'h'=2,'c'=2] {'y4',..., dimensions={0} | all-to-all | bytes 262144 | tf_op jit(solution)/shard_map/all_to_all | solution.py:175
  98.6 0.7 convert_reduce_fusion
Async XLA Ops:
  0.6 14.8 %copy-start.2 = (bf16[2,128,4,128]{3,2,1,0:T(4,128)(2,1)S(1)}, bf16[2,128,4,128]{3,2,1,0:T(4,128)(2,1)}, u32[]{:S(2)}) copy-start(bf16[2,128,4,128]{3,2,1,0:T(4,128)(2,1)} %param.6) | copy-start | bytes 786436
  0.6 0.9 copy-start.3
  2.3 21.7 %all-to-all-start = ((bf16[32,4,512]{2,1,0:T(4,128)(2,1)}), bf16[32,4,512]{2,1,0:T(4,128)(2,1)S(1)}, u32[]{:S(2)}, u32[]{:S(2)}) async-start(bf16[32,4,512]{2,1,0:T(4,128)(2,1)} %shard_map.77), calls=%async_computation | async-start | bytes 262144 | tf_op jit(solution)/shard_map/all_to_all | solution.py:175
  15.5 19.7 %collective-permute-start = (bf16[2,64,8,128]{3,2,1,0:T(8,128)(2,1)S(1)}, bf16[2,64,8,128]{3,2,1,0:T(8,128)(2,1)S(1)}, u32[]{:S(2)}, u32[]{:S(2)}) collective-permute-start(bf16[2,64,8,128]{3,2,1,0:T(8,128)(2,1)S(1)} %bitcast.16), channel_id=1, source_target_pairs={{0,2},{2,0},{1,3},{3,1},{4,6},{6,4},{5,7},{7,5},{8,10},{10,8},{9,1... | collective-permute-start | bytes 786440 | tf_op jit(solution)/shard_map/ppermute | solution.py:193
  24.6 20.2 %all-to-all-start.1 = ((bf16[16,8,128]{2,1,0:T(8,128)(2,1)}), bf16[16,8,128]{2,1,0:T(8,128)(2,1)S(1)}, u32[]{:S(2)}, u32[]{:S(2)}) async-start(bf16[16,8,128]{2,1,0:T(8,128)(2,1)} %shard_map.78), calls=%async_computation.1 | async-start | bytes 65536 | tf_op jit(solution)/shard_map/all_to_all | solution.py:175
  35.1 0.7 copy-start.4
  46.6 24.3 %all-to-all-start.2 = ((bf16[128,8,256]{2,1,0:T(8,128)(2,1)}), bf16[128,8,256]{2,1,0:T(8,128)(2,1)S(1)}, u32[]{:S(2)}, u32[]{:S(2)}) async-start(bf16[128,8,256]{2,1,0:T(8,128)(2,1)} %bitcast.5), calls=%async_computation.2 | async-start | bytes 1048576 | tf_op jit(solution)/shard_map/all_to_all | solution.py:175
  52.8 18.1 %copy-start = (bf16[512,512]{1,0:T(8,128)(2,1)S(1)}, bf16[512,512]{1,0:T(8,128)(2,1)}, u32[]{:S(2)}) copy-start(bf16[512,512]{1,0:T(8,128)(2,1)} %constant.68.clone.sin_ref) | copy-start | bytes 1572868
  52.8 18.1 %copy-start.1 = (bf16[512,512]{1,0:T(8,128)(2,1)S(1)}, bf16[512,512]{1,0:T(8,128)(2,1)}, u32[]{:S(2)}) copy-start(bf16[512,512]{1,0:T(8,128)(2,1)} %constant.67.clone.cos_ref) | copy-start | bytes 1572868
  71.7 6.1 %collective-permute-start.1 = (bf16[2,2,512,128]{3,2,1,0:T(8,128)(2,1)S(1)}, bf16[2,2,512,128]{3,2,1,0:T(8,128)(2,1)S(1)}, u32[]{:S(2)}, u32[]{:S(2)}) collective-permute-start(bf16[2,2,512,128]{3,2,1,0:T(8,128)(2,1)S(1)} %shard_map.82.own_ref), channel_id=1, source_target_pairs={{0,1},{1,0},{2,3},{3,2},{4,5},{5,4},{6,7},{7,6},{8,9},{9,8},{10,11... | collective-permute-start | bytes 1572872 | tf_op jit(solution)/shard_map/ppermute | solution.py:245

commit v8 on v6

--- a/solution.py
+++ b/solution.py
@@ -131,19 +131,38 @@
         out_ref[block, 1] = imag[:, lanes]
 
 
-def step_kernel(tile_ref, own_ref, other_ref, cos_ref, sin_ref, shift_ref, wave_ref, image_ref, field, back):
+def half_transform(tile, flips, block_ref, cos_ref, sin_ref, field, use):
+    starts = [pl.multiple_of((tile ^ flip) * tile_size, tile_size) for flip in flips]
+    for at in range(2):
+        field[:, :, at * tile_size : (at + 1) * tile_size] = block_ref[at]
+    cos_rows, sin_rows = (
+        jnp.concatenate([ref[pl.ds(start, tile_size), :] for start in starts], axis=0) for ref in (cos_ref, sin_ref)
+    )
+    width = 256
+    for at in range(0, size, width):
+        part = slice(at, at + width)
+        real = dot(field[0], cos_rows[:, part]) + dot(field[1], sin_rows[:, part])
+        imag = dot(field[1], cos_rows[:, part]) - dot(field[0], sin_rows[:, part])
+        use(part, real, imag)
+
+
+def near_kernel(tile_ref, own_ref, cos_ref, sin_ref, out_ref, field):
+    def use(part, real, imag):
+        out_ref[0, :, part] = real
+        out_ref[1, :, part] = imag
+
+    half_transform(tile_ref[0], (0, 2), own_ref, cos_ref, sin_ref, field, use)
+
+
+def step_kernel(tile_ref, near_ref, other_ref, cos_ref, sin_ref, shift_ref, wave_ref, image_ref, field, back):
     tile = tile_ref[0]
-    for flip in range(4):
-        block = (own_ref, other_ref)[flip % 2]
-        start = pl.multiple_of((tile ^ flip) * tile_size, tile_size)
-        field[:, :, pl.ds(start, tile_size)] = block[flip // 2]
     rows = pl.ds(pl.multiple_of(tile * tile_size, tile_size), tile_size)
     inverse = jnp.concatenate([cos_ref[rows, :], sin_ref[rows, :]], axis=0)
     width = 256
-    for at in range(0, size, width):
-        part = slice(at, at + width)
-        spec_real = dot(field[0], cos_ref[:, part]) + dot(field[1], sin_ref[:, part])
-        spec_imag = dot(field[1], cos_ref[:, part]) - dot(field[0], sin_ref[:, part])
+
+    def use(part, real, imag):
+        spec_real = real + near_ref[0, :, part]
+        spec_imag = imag + near_ref[1, :, part]
         shift_real = shift_ref[0, :, part].astype(jnp.float32)
         shift_imag = shift_ref[1, :, part].astype(jnp.float32)
         shifted_real = (spec_real * shift_real - spec_imag * shift_imag).astype(jnp.bfloat16)
@@ -152,6 +171,8 @@
         from_imag = dot(inverse, shifted_imag)
         back[:tile_size, part] = (from_real[:tile_size] - from_imag[tile_size:]).astype(jnp.bfloat16)
         back[tile_size:, part] = (from_imag[:tile_size] + from_real[tile_size:]).astype(jnp.bfloat16)
+
+    half_transform(tile, (1, 3), other_ref, cos_ref, sin_ref, field, use)
     for at in range(0, size, width):
         part = slice(at, at + width)
         by_cos = dot(back[...], cos_ref[:, part])
@@ -239,6 +260,15 @@
         cost_estimate=pl.CostEstimate(flops=540_000_000, bytes_accessed=2_100_000, transcendentals=0),
     )(table_cos, table_sin, columns)
     beside = lax.ppermute(own, "c", swap)
+    near = pl.pallas_call(
+        near_kernel,
+        out_shape=jax.ShapeDtypeStruct((2, size, size), jnp.float32),
+        in_specs=[whole(pltpu.SMEM)] + [whole()] * 3,
+        out_specs=whole(),
+        scratch_shapes=[pltpu.VMEM((2, size, 2 * tile_size), jnp.bfloat16)],
+        compiler_params=pltpu.CompilerParams(vmem_limit_bytes=12 << 20),
+        cost_estimate=pl.CostEstimate(flops=540_000_000, bytes_accessed=3_600_000, transcendentals=0),
+    )(tile[None], own, table_cos, table_sin)
     wave_next, parts = pl.pallas_call(
         step_kernel,
         out_shape=(
@@ -248,12 +278,12 @@
         in_specs=[whole(pltpu.SMEM)] + [whole()] * 5,
         out_specs=(whole(), whole()),
         scratch_shapes=[
-            pltpu.VMEM((2, size, size), jnp.bfloat16),
+            pltpu.VMEM((2, size, 2 * tile_size), jnp.bfloat16),
             pltpu.VMEM((2 * tile_size, size), jnp.bfloat16),
         ],
         compiler_params=pltpu.CompilerParams(vmem_limit_bytes=20 << 20),
-        cost_estimate=pl.CostEstimate(flops=1_620_000_000, bytes_accessed=4_600_000, transcendentals=0),
-    )(tile[None], own, beside, table_cos, table_sin, shift)
+        cost_estimate=pl.CostEstimate(flops=1_080_000_000, bytes_accessed=5_600_000, transcendentals=0),
+    )(tile[None], near, beside, table_cos, table_sin, shift)
     parts = exchange(parts, mixed)
     image = jnp.sum(parts.astype(jnp.float32), axis=0).T
     return (wave_next[:, None], image)

time: 99.1 us -> 98.5 us (level)
  waiting for transfers between devices: 28 us -> 26.2 us
    all_to_all x3, waiting for transfers between devices: 26.4 us -> 25.4 us  [exchange(): return lax.all_to_all(x, axes, split_axis=0, concat_axis=0, tiled=True)]
    unnamed x10 -> x12, local copies, waits for them, and re-layouts: 1.53 us -> 2.52 us
  transfers between devices with their start and end apart: 5 -> 5, of which waited for: 4 -> 4; matrix products, arithmetic and copies ran while one was open for 0% -> 0% of each run, Pallas kernels for 4% -> 5%
where the time goes in v8:
time: 98.5 us; the launch traced here: 97.8 us
  starting transfers between devices  38.3 us (39%)
  waiting for transfers between devices  26.2 us (27%)
  blocking collectives  17.7 us (18%)
  Pallas kernels  10.8 us (11%)
  local copies, waits for them, and re-layouts  2.52 us (3%)
  between operations  1.44 us (1%)
    all_to_all x3, starting transfers between devices, exchange(): return lax.all_to_all(x, axes, split_axis=0, concat_axis=0, tiled=True)  29.8 us
    all_to_all x3, waiting for transfers between devices, exchange(): return lax.all_to_all(x, axes, split_axis=0, concat_axis=0, tiled=True)  25.4 us
    all_to_all x1, blocking collectives, exchange(): return lax.all_to_all(x, axes, split_axis=0, concat_axis=0, tiled=True)  17.7 us
    ppermute x1, starting transfers between devices, local(): other = lax.ppermute(wavefield, 'h', swap)  4.36 us
    ppermute x1, starting transfers between devices, local(): beside = lax.ppermute(own, 'c', swap)  4.1 us
    pallas_call x1, Pallas kernels, local(): pl.pallas_call(shift_kernel, out_shape=jax.ShapeDtypeStruct((2, size, siz...  2.74 us
    pallas_call x1, Pallas kernels, local(): pl.pallas_call(step_kernel, out_shape=(jax.ShapeDtypeStruct((2, tile_size...  2.67 us
    unnamed x12, local copies, waits for them, and re-layouts  2.52 us
  transfers between devices with their start and end apart: 5, of which 4 were waited for; matrix products, arithmetic and copies ran while one was open for 0% of the time, Pallas kernels for 5%

profile of v8, /device:TPU:1, one launch (start us, length us, event | category | flops | bytes accessed | tf_op | source)
XLA Modules:
  0.0 97.8 jit_solution(16448972960137731915)
XLA Ops:
  0.6 0.0 copy-start.3
  0.6 0.9 copy-done.3
  1.5 0.0 copy-start.5
  1.5 0.7 shard_map.77
  2.2 13.2 %all-to-all-start = ((bf16[32,4,512]{2,1,0:T(4,128)(2,1)}), bf16[32,4,512]{2,1,0:T(4,128)(2,1)S(1)}, u32[]{:S(2)}, u32[]{:S(2)}) async-start(bf16[32,4,512]{2,1,0:T(4,128)(2,1)} %shard_map.77), calls=%async_computation | async-start | bytes 262144 | tf_op jit(solution)/shard_map/all_to_all | solution.py:193
  15.4 4.4 %collective-permute-start = (bf16[2,64,8,128]{3,2,1,0:T(8,128)(2,1)}, bf16[2,64,8,128]{3,2,1,0:T(8,128)(2,1)S(1)}, u32[]{:S(2)}, u32[]{:S(2)}) collective-permute-start(bf16[2,64,8,128]{3,2,1,0:T(8,128)(2,1)} %bitcast.14), channel_id=1, source_target_pairs={{0,2},{2,0},{1,3},{3,1},{4,6},{6,4},{5,7},{7,5},{8,10},{10,8},{9,1... | collective-permute-start | bytes 786440 | tf_op jit(solution)/shard_map/ppermute | solution.py:211
  20.5 0.0 copy-start
  20.5 0.0 copy-start.1
  20.5 3.4 %all-to-all-done.rows_ref = bf16[32,4,512]{2,1,0:T(4,128)(2,1)S(1)} async-done(((bf16[32,4,512]{2,1,0:T(4,128)(2,1)}), bf16[32,4,512]{2,1,0:T(4,128)(2,1)S(1)}, u32[]{:S(2)}, u32[]{:S(2)}) %all-to-all-start) | async-done | bytes 131104 | tf_op jit(solution)/shard_map/all_to_all | solution.py:193
  23.9 0.6 shard_map.78
  24.5 10.5 %all-to-all-start.1 = ((bf16[16,8,128]{2,1,0:T(8,128)(2,1)}), bf16[16,8,128]{2,1,0:T(8,128)(2,1)S(1)}, u32[]{:S(2)}, u32[]{:S(2)}) async-start(bf16[16,8,128]{2,1,0:T(8,128)(2,1)} %shard_map.78), calls=%async_computation.1 | async-start | bytes 65536 | tf_op jit(solution)/shard_map/all_to_all | solution.py:193
  35.0 0.1 pad_add_fusion.place_ref
  35.1 0.0 collective-permute-done.other_ref
  35.1 0.0 copy-start.2
  35.1 0.9 copy-done.2
  36.1 0.7 copy-done.4
  36.7 0.8 shard_map.79
  37.5 7.3 %all-to-all-done.1.slow_ref = bf16[16,8,128]{2,1,0:T(8,128)(2,1)S(1)} async-done(((bf16[16,8,128]{2,1,0:T(8,128)(2,1)}), bf16[16,8,128]{2,1,0:T(8,128)(2,1)S(1)}, u32[]{:S(2)}, u32[]{:S(2)}) %all-to-all-start.1) | async-done | bytes 32800 | tf_op jit(solution)/shard_map/all_to_all | solution.py:193
  44.7 1.9 %shard_map.80 = bf16[128,8,256]{2,1,0:T(8,128)(2,1)} custom-call(s32[2]{0:T(128)S(1)} %pad_add_fusion.place_ref, bf16[16,8,128]{2,1,0:T(8,128)(2,1)S(1)} %all-to-all-done.1.slow_ref, bf16[2,64,8,128]{3,2,1,0:T(8,128)(2,1)S(1)} %get-tuple-element.9.own_ref, bf16[2,64,8,128]{3,2,1,0:T(8,128)(2,1)S(1)} %get-tuple-element.10.other_ref, ...), custom_call_target="tpu_custom_call" | custom-call | flops 6000000 | bytes 1300000 | tf_op jit(solution)/shard_map/pallas_call | solution.py:231
  46.7 6.2 %all-to-all-start.2 = ((bf16[128,8,256]{2,1,0:T(8,128)(2,1)}), bf16[128,8,256]{2,1,0:T(8,128)(2,1)S(1)}, u32[]{:S(2)}, u32[]{:S(2)}) async-start(bf16[128,8,256]{2,1,0:T(8,128)(2,1)} %shard_map.80), calls=%async_computation.2 | async-start | bytes 1048576 | tf_op jit(solution)/shard_map/all_to_all | solution.py:193
  52.9 0.0 copy-done.5
  52.9 2.7 %shard_map.81.shift_ref = bf16[2,512,512]{2,1,0:T(8,128)(2,1)S(1)} custom-call(s32[1]{0:T(128)} %bitcast.5.slot_ref, s32[128]{0:T(128)S(1)} %copy-done.5), custom_call_target="tpu_custom_call" | custom-call | flops 10000000 | bytes 2100000 | tf_op jit(solution)/shard_map/pallas_call | solution.py:242
  55.6 14.7 %all-to-all-done.2.wave_ref = bf16[128,8,256]{2,1,0:T(8,128)(2,1)S(1)} async-done(((bf16[128,8,256]{2,1,0:T(8,128)(2,1)}), bf16[128,8,256]{2,1,0:T(8,128)(2,1)S(1)}, u32[]{:S(2)}, u32[]{:S(2)}) %all-to-all-start.2) | async-done | bytes 524320 | tf_op jit(solution)/shard_map/all_to_all | solution.py:193
  70.3 0.0 copy-done
  70.3 0.0 copy-done.1
  70.3 0.7 shard_map.82.own_ref
  71.0 4.1 %collective-permute-start.1 = (bf16[2,2,512,128]{3,2,1,0:T(8,128)(2,1)S(1)}, bf16[2,2,512,128]{3,2,1,0:T(8,128)(2,1)S(1)}, u32[]{:S(2)}, u32[]{:S(2)}) collective-permute-start(bf16[2,2,512,128]{3,2,1,0:T(8,128)(2,1)S(1)} %shard_map.82.own_ref), channel_id=1, source_target_pairs={{0,1},{1,0},{2,3},{3,2},{4,5},{5,4},{6,7},{7,6},{8,9},{9,8},{10,11... | collective-permute-start | bytes 1572872 | tf_op jit(solution)/shard_map/ppermute | solution.py:262
  75.2 0.7 shard_map.83.near_ref
  75.9 0.8 collective-permute-done.1.other_ref
  76.7 2.7 %shard_map.84 = (bf16[2,128,512]{2,1,0:T(8,128)(2,1)}, bf16[128,4,128]{2,1,0:T(4,128)(2,1)S(1)}) custom-call(s32[1]{0:T(128)} %bitcast.tile_ref, f32[2,512,512]{2,1,0:T(8,128)S(1)} %shard_map.83.near_ref, bf16[2,2,512,128]{3,2,1,0:T(8,128)(2,1)S(1)} %collective-permute-done.1.other_ref, bf16[512,512]{1,0:T(8,128)(2,1)S(1)} %copy-done.1, ...), custom_call_target="tpu_custom_call" | custom-call | flops 1080000000 | bytes 5600000 | tf_op jit(solution)/shard_map/pallas_call | solution.py:272
  79.3 17.7 %all_to_all.20 = bf16[128,4,128]{2,1,0:T(4,128)(2,1)S(1)} all-to-all(bf16[128,4,128]{2,1,0:T(4,128)(2,1)S(1)} %get-tuple-element.15), channel_id=1, replica_groups=mesh['y4'=2,'y2'=2,'y1'=2,'w'=2,'z4'=2,'z2'=2,'z1'=2,'h'=2,'c'=2] {'z1',..., dimensions={0} | all-to-all | bytes 262144 | tf_op jit(solution)/shard_map/all_to_all | solution.py:193
  97.0 0.7 convert_reduce_fusion
  (1 shorter events, 0.0 us)
Async XLA Ops:
  0.6 0.9 copy-start.3
  1.5 51.3 %copy-start.5 = (s32[128]{0:T(128)S(1)}, s32[128]{0:T(128)}, u32[]{:S(2)}) copy-start(s32[128]{0:T(128)} %ids_ref.3) | copy-start | bytes 1540
  2.2 21.7 %all-to-all-start = ((bf16[32,4,512]{2,1,0:T(4,128)(2,1)}), bf16[32,4,512]{2,1,0:T(4,128)(2,1)S(1)}, u32[]{:S(2)}, u32[]{:S(2)}) async-start(bf16[32,4,512]{2,1,0:T(4,128)(2,1)} %shard_map.77), calls=%async_computation | async-start | bytes 262144 | tf_op jit(solution)/shard_map/all_to_all | solution.py:193
  15.4 19.7 %collective-permute-start = (bf16[2,64,8,128]{3,2,1,0:T(8,128)(2,1)}, bf16[2,64,8,128]{3,2,1,0:T(8,128)(2,1)S(1)}, u32[]{:S(2)}, u32[]{:S(2)}) collective-permute-start(bf16[2,64,8,128]{3,2,1,0:T(8,128)(2,1)} %bitcast.14), channel_id=1, source_target_pairs={{0,2},{2,0},{1,3},{3,1},{4,6},{6,4},{5,7},{7,5},{8,10},{10,8},{9,1... | collective-permute-start | bytes 786440 | tf_op jit(solution)/shard_map/ppermute | solution.py:211
  20.5 49.9 %copy-start = (bf16[512,512]{1,0:T(8,128)(2,1)S(1)}, bf16[512,512]{1,0:T(8,128)(2,1)}, u32[]{:S(2)}) copy-start(bf16[512,512]{1,0:T(8,128)(2,1)} %constant.68.clone.sin_ref) | copy-start | bytes 1572868
  20.5 49.8 %copy-start.1 = (bf16[512,512]{1,0:T(8,128)(2,1)S(1)}, bf16[512,512]{1,0:T(8,128)(2,1)}, u32[]{:S(2)}) copy-start(bf16[512,512]{1,0:T(8,128)(2,1)} %constant.67.clone.cos_ref) | copy-start | bytes 1572868
  24.5 20.2 %all-to-all-start.1 = ((bf16[16,8,128]{2,1,0:T(8,128)(2,1)}), bf16[16,8,128]{2,1,0:T(8,128)(2,1)S(1)}, u32[]{:S(2)}, u32[]{:S(2)}) async-start(bf16[16,8,128]{2,1,0:T(8,128)(2,1)} %shard_map.78), calls=%async_computation.1 | async-start | bytes 65536 | tf_op jit(solution)/shard_map/all_to_all | solution.py:193
  35.1 1.0 copy-start.2
  36.0 0.7 copy-start.4
  46.7 23.6 %all-to-all-start.2 = ((bf16[128,8,256]{2,1,0:T(8,128)(2,1)}), bf16[128,8,256]{2,1,0:T(8,128)(2,1)S(1)}, u32[]{:S(2)}, u32[]{:S(2)}) async-start(bf16[128,8,256]{2,1,0:T(8,128)(2,1)} %shard_map.80), calls=%async_computation.2 | async-start | bytes 1048576 | tf_op jit(solution)/shard_map/all_to_all | solution.py:193
  71.0 5.6 %collective-permute-start.1 = (bf16[2,2,512,128]{3,2,1,0:T(8,128)(2,1)S(1)}, bf16[2,2,512,128]{3,2,1,0:T(8,128)(2,1)S(1)}, u32[]{:S(2)}, u32[]{:S(2)}) collective-permute-start(bf16[2,2,512,128]{3,2,1,0:T(8,128)(2,1)S(1)} %shard_map.82.own_ref), channel_id=1, source_target_pairs={{0,1},{1,0},{2,3},{3,2},{4,5},{5,4},{6,7},{7,6},{8,9},{9,8},{10,11... | collective-permute-start | bytes 1572872 | tf_op jit(solution)/shard_map/ppermute | solution.py:262

commit v9 on v7

--- a/solution.py
+++ b/solution.py
@@ -131,19 +131,38 @@
         out_ref[block, 1] = imag[:, lanes]
 
 
-def step_kernel(tile_ref, own_ref, other_ref, cos_ref, sin_ref, shift_ref, wave_ref, image_ref, field, back, waves, sem):
+def half_transform(tile, flips, block_ref, cos_ref, sin_ref, field, use):
+    starts = [pl.multiple_of((tile ^ flip) * tile_size, tile_size) for flip in flips]
+    for at in range(2):
+        field[:, :, at * tile_size : (at + 1) * tile_size] = block_ref[at]
+    cos_rows, sin_rows = (
+        jnp.concatenate([ref[pl.ds(start, tile_size), :] for start in starts], axis=0) for ref in (cos_ref, sin_ref)
+    )
+    width = 256
+    for at in range(0, size, width):
+        part = slice(at, at + width)
+        real = dot(field[0], cos_rows[:, part]) + dot(field[1], sin_rows[:, part])
+        imag = dot(field[1], cos_rows[:, part]) - dot(field[0], sin_rows[:, part])
+        use(part, real, imag)
+
+
+def near_kernel(tile_ref, own_ref, cos_ref, sin_ref, out_ref, field):
+    def use(part, real, imag):
+        out_ref[0, :, part] = real
+        out_ref[1, :, part] = imag
+
+    half_transform(tile_ref[0], (0, 2), own_ref, cos_ref, sin_ref, field, use)
+
+
+def step_kernel(tile_ref, near_ref, other_ref, cos_ref, sin_ref, shift_ref, wave_ref, image_ref, field, back, waves, sem):
     tile = tile_ref[0]
-    for flip in range(4):
-        block = (own_ref, other_ref)[flip % 2]
-        start = pl.multiple_of((tile ^ flip) * tile_size, tile_size)
-        field[:, :, pl.ds(start, tile_size)] = block[flip // 2]
     rows = pl.ds(pl.multiple_of(tile * tile_size, tile_size), tile_size)
     inverse = jnp.concatenate([cos_ref[rows, :], sin_ref[rows, :]], axis=0)
     width = 256
-    for at in range(0, size, width):
-        part = slice(at, at + width)
-        spec_real = dot(field[0], cos_ref[:, part]) + dot(field[1], sin_ref[:, part])
-        spec_imag = dot(field[1], cos_ref[:, part]) - dot(field[0], sin_ref[:, part])
+
+    def use(part, real, imag):
+        spec_real = real + near_ref[0, :, part]
+        spec_imag = imag + near_ref[1, :, part]
         shift_real = shift_ref[0, :, part].astype(jnp.float32)
         shift_imag = shift_ref[1, :, part].astype(jnp.float32)
         shifted_real = (spec_real * shift_real - spec_imag * shift_imag).astype(jnp.bfloat16)
@@ -152,6 +171,8 @@
         from_imag = dot(inverse, shifted_imag)
         back[:tile_size, part] = (from_real[:tile_size] - from_imag[tile_size:]).astype(jnp.bfloat16)
         back[tile_size:, part] = (from_imag[:tile_size] + from_real[tile_size:]).astype(jnp.bfloat16)
+
+    half_transform(tile, (1, 3), other_ref, cos_ref, sin_ref, field, use)
     reals = []
     for at in range(0, size, width):
         part = slice(at, at + width)
@@ -243,6 +264,15 @@
         cost_estimate=pl.CostEstimate(flops=540_000_000, bytes_accessed=2_100_000, transcendentals=0),
     )(table_cos, table_sin, columns)
     beside = lax.ppermute(own, "c", swap)
+    near = pl.pallas_call(
+        near_kernel,
+        out_shape=jax.ShapeDtypeStruct((2, size, size), jnp.float32),
+        in_specs=[whole(pltpu.SMEM)] + [whole()] * 3,
+        out_specs=whole(),
+        scratch_shapes=[pltpu.VMEM((2, size, 2 * tile_size), jnp.bfloat16)],
+        compiler_params=pltpu.CompilerParams(vmem_limit_bytes=12 << 20),
+        cost_estimate=pl.CostEstimate(flops=540_000_000, bytes_accessed=3_600_000, transcendentals=0),
+    )(tile[None], own, table_cos, table_sin)
     wave_next, parts = pl.pallas_call(
         step_kernel,
         out_shape=(
@@ -252,14 +282,14 @@
         in_specs=[whole(pltpu.SMEM)] + [whole()] * 5,
         out_specs=(whole(pl.ANY), whole()),
         scratch_shapes=[
-            pltpu.VMEM((2, size, size), jnp.bfloat16),
+            pltpu.VMEM((2, size, 2 * tile_size), jnp.bfloat16),
             pltpu.VMEM((2 * tile_size, size), jnp.bfloat16),
             pltpu.VMEM((2, tile_size, size), jnp.bfloat16),
             pltpu.SemaphoreType.DMA,
         ],
         compiler_params=pltpu.CompilerParams(vmem_limit_bytes=20 << 20),
-        cost_estimate=pl.CostEstimate(flops=1_620_000_000, bytes_accessed=4_600_000, transcendentals=0),
-    )(tile[None], own, beside, table_cos, table_sin, shift)
+        cost_estimate=pl.CostEstimate(flops=1_080_000_000, bytes_accessed=5_600_000, transcendentals=0),
+    )(tile[None], near, beside, table_cos, table_sin, shift)
     parts = exchange(parts.reshape(slots, size // slots, tile_size), freq)
     image = jnp.sum(parts.astype(jnp.float32), axis=0).T
     return (wave_next[:, None], image)

time: 99.7 us -> 99.1 us (level)
  waiting for transfers between devices: 28.6 us -> 26.9 us
    all_to_all x3, waiting for transfers between devices: 27.1 us -> 26.1 us  [exchange(): return lax.all_to_all(x, axes, split_axis=0, concat_axis=0, tiled=True)]
    unnamed x10 -> x12, local copies, waits for them, and re-layouts: 1.53 us -> 2.52 us
  transfers between devices with their start and end apart: 5 -> 5, of which waited for: 4 -> 4; matrix products, arithmetic and copies ran while one was open for 0% -> 0% of each run, Pallas kernels for 4% -> 5%
where the time goes in v9:
time: 99.1 us; the launch traced here: 98.7 us
  starting transfers between devices  38.8 us (39%)
  waiting for transfers between devices  26.9 us (27%)
  blocking collectives  17.6 us (18%)
  Pallas kernels  10.7 us (11%)
  local copies, waits for them, and re-layouts  2.52 us (3%)
  between operations  1.46 us (1%)
    all_to_all x3, starting transfers between devices, exchange(): return lax.all_to_all(x, axes, split_axis=0, concat_axis=0, tiled=True)  29.9 us
    all_to_all x3, waiting for transfers between devices, exchange(): return lax.all_to_all(x, axes, split_axis=0, concat_axis=0, tiled=True)  26.1 us
    all_to_all x1, blocking collectives, exchange(): return lax.all_to_all(x, axes, split_axis=0, concat_axis=0, tiled=True)  17.6 us
    ppermute x1, starting transfers between devices, local(): beside = lax.ppermute(own, 'c', swap)  4.54 us
    ppermute x1, starting transfers between devices, local(): other = lax.ppermute(wavefield, 'h', swap)  4.36 us
    pallas_call x1, Pallas kernels, local(): pl.pallas_call(shift_kernel, out_shape=jax.ShapeDtypeStruct((2, size, siz...  2.74 us
    pallas_call x1, Pallas kernels, local(): pl.pallas_call(step_kernel, out_shape=(jax.ShapeDtypeStruct((2, tile_size...  2.67 us
    unnamed x12, local copies, waits for them, and re-layouts  2.52 us
  transfers between devices with their start and end apart: 5, of which 4 were waited for; matrix products, arithmetic and copies ran while one was open for 0% of the time, Pallas kernels for 5%

profile of v9, /device:TPU:1, one launch (start us, length us, event | category | flops | bytes accessed | tf_op | source)
XLA Modules:
  0.0 98.7 jit_solution(7615519475780048881)
XLA Ops:
  0.6 0.0 copy-start.3
  0.6 0.9 copy-done.3
  1.5 0.0 copy-start.5
  1.5 0.7 shard_map.77
  2.2 13.2 %all-to-all-start = ((bf16[32,4,512]{2,1,0:T(4,128)(2,1)}), bf16[32,4,512]{2,1,0:T(4,128)(2,1)S(1)}, u32[]{:S(2)}, u32[]{:S(2)}) async-start(bf16[32,4,512]{2,1,0:T(4,128)(2,1)} %shard_map.77), calls=%async_computation | async-start | bytes 262144 | tf_op jit(solution)/shard_map/all_to_all | solution.py:196
  15.4 4.4 %collective-permute-start = (bf16[2,64,8,128]{3,2,1,0:T(8,128)(2,1)}, bf16[2,64,8,128]{3,2,1,0:T(8,128)(2,1)S(1)}, u32[]{:S(2)}, u32[]{:S(2)}) collective-permute-start(bf16[2,64,8,128]{3,2,1,0:T(8,128)(2,1)} %bitcast.16), channel_id=1, source_target_pairs={{0,2},{2,0},{1,3},{3,1},{4,6},{6,4},{5,7},{7,5},{8,10},{10,8},{9,1... | collective-permute-start | bytes 786440 | tf_op jit(solution)/shard_map/ppermute | solution.py:214
  20.5 0.0 copy-start
  20.5 0.0 copy-start.1
  20.5 3.4 %all-to-all-done.rows_ref = bf16[32,4,512]{2,1,0:T(4,128)(2,1)S(1)} async-done(((bf16[32,4,512]{2,1,0:T(4,128)(2,1)}), bf16[32,4,512]{2,1,0:T(4,128)(2,1)S(1)}, u32[]{:S(2)}, u32[]{:S(2)}) %all-to-all-start) | async-done | bytes 131104 | tf_op jit(solution)/shard_map/all_to_all | solution.py:196
  23.9 0.6 shard_map.78
  24.5 10.5 %all-to-all-start.1 = ((bf16[16,8,128]{2,1,0:T(8,128)(2,1)}), bf16[16,8,128]{2,1,0:T(8,128)(2,1)S(1)}, u32[]{:S(2)}, u32[]{:S(2)}) async-start(bf16[16,8,128]{2,1,0:T(8,128)(2,1)} %shard_map.78), calls=%async_computation.1 | async-start | bytes 65536 | tf_op jit(solution)/shard_map/all_to_all | solution.py:196
  35.0 0.1 pad_add_fusion.place_ref
  35.1 0.0 collective-permute-done.other_ref
  35.1 0.0 copy-start.2
  35.1 0.9 copy-done.2
  36.1 0.7 copy-done.4
  36.7 0.8 shard_map.79
  37.5 7.3 %all-to-all-done.1.slow_ref = bf16[16,8,128]{2,1,0:T(8,128)(2,1)S(1)} async-done(((bf16[16,8,128]{2,1,0:T(8,128)(2,1)}), bf16[16,8,128]{2,1,0:T(8,128)(2,1)S(1)}, u32[]{:S(2)}, u32[]{:S(2)}) %all-to-all-start.1) | async-done | bytes 32800 | tf_op jit(solution)/shard_map/all_to_all | solution.py:196
  44.7 1.8 %shard_map.80 = bf16[1024,256]{1,0:T(8,128)(2,1)} custom-call(s32[2]{0:T(128)S(1)} %pad_add_fusion.place_ref, bf16[16,8,128]{2,1,0:T(8,128)(2,1)S(1)} %all-to-all-done.1.slow_ref, bf16[2,64,8,128]{3,2,1,0:T(8,128)(2,1)S(1)} %get-tuple-element.9.own_ref, bf16[2,64,8,128]{3,2,1,0:T(8,128)(2,1)S(1)} %get-tuple-element.10.other_ref, ...), custom_call_target="tpu_custom_call" | custom-call | flops 6000000 | bytes 1300000 | tf_op jit(solution)/shard_map/pallas_call | solution.py:234
  46.6 6.2 %all-to-all-start.2 = ((bf16[128,8,256]{2,1,0:T(8,128)(2,1)}), bf16[128,8,256]{2,1,0:T(8,128)(2,1)S(1)}, u32[]{:S(2)}, u32[]{:S(2)}) async-start(bf16[128,8,256]{2,1,0:T(8,128)(2,1)} %bitcast.5), calls=%async_computation.2 | async-start | bytes 1048576 | tf_op jit(solution)/shard_map/all_to_all | solution.py:196
  52.8 0.0 copy-done.5
  52.8 2.7 %shard_map.81.shift_ref = bf16[2,512,512]{2,1,0:T(8,128)(2,1)S(1)} custom-call(s32[1]{0:T(128)} %bitcast.6.slot_ref, s32[128]{0:T(128)S(1)} %copy-done.5), custom_call_target="tpu_custom_call" | custom-call | flops 10000000 | bytes 2100000 | tf_op jit(solution)/shard_map/pallas_call | solution.py:246
  55.5 15.4 %all-to-all-done.2.wave_ref = bf16[128,8,256]{2,1,0:T(8,128)(2,1)S(1)} async-done(((bf16[128,8,256]{2,1,0:T(8,128)(2,1)}), bf16[128,8,256]{2,1,0:T(8,128)(2,1)S(1)}, u32[]{:S(2)}, u32[]{:S(2)}) %all-to-all-start.2) | async-done | bytes 524320 | tf_op jit(solution)/shard_map/all_to_all | solution.py:196
  70.9 0.0 copy-done
  70.9 0.0 copy-done.1
  70.9 0.7 shard_map.82.own_ref
  71.6 4.5 %collective-permute-start.1 = (bf16[2,2,512,128]{3,2,1,0:T(8,128)(2,1)S(1)}, bf16[2,2,512,128]{3,2,1,0:T(8,128)(2,1)S(1)}, u32[]{:S(2)}, u32[]{:S(2)}) collective-permute-start(bf16[2,2,512,128]{3,2,1,0:T(8,128)(2,1)S(1)} %shard_map.82.own_ref), channel_id=1, source_target_pairs={{0,1},{1,0},{2,3},{3,2},{4,5},{5,4},{6,7},{7,6},{8,9},{9,8},{10,11... | collective-permute-start | bytes 1572872 | tf_op jit(solution)/shard_map/ppermute | solution.py:266
  76.2 0.7 shard_map.83.near_ref
  76.9 0.8 collective-permute-done.1.other_ref
  77.7 2.7 %shard_map.84 = (bf16[2,128,512]{2,1,0:T(8,128)(2,1)}, bf16[512,128]{1,0:T(8,128)(2,1)S(1)}) custom-call(s32[1]{0:T(128)} %bitcast.tile_ref, f32[2,512,512]{2,1,0:T(8,128)S(1)} %shard_map.83.near_ref, bf16[2,2,512,128]{3,2,1,0:T(8,128)(2,1)S(1)} %collective-permute-done.1.other_ref, bf16[512,512]{1,0:T(8,128)(2,1)S(1)} %copy-done.1, ...), custom_call_target="tpu_custom_call" | custom-call | flops 1080000000 | bytes 5600000 | tf_op jit(solution)/shard_map/pallas_call | solution.py:276
  80.4 17.6 %all_to_all.20 = bf16[128,4,128]{2,1,0:T(4,128)(2,1)S(1)} all-to-all(bf16[128,4,128]{2,1,0:T(4,128)(2,1)S(1)} %bitcast.18), channel_id=1, replica_groups=mesh['y4'=2,'y2'=2,'y1'=2,'w'=2,'z4'=2,'z2'=2,'z1'=2,'h'=2,'c'=2] {'y4',..., dimensions={0} | all-to-all | bytes 262144 | tf_op jit(solution)/shard_map/all_to_all | solution.py:196
  98.0 0.7 convert_reduce_fusion
  (1 shorter events, 0.0 us)
Async XLA Ops:
  0.6 0.9 copy-start.3
  1.5 51.2 %copy-start.5 = (s32[128]{0:T(128)S(1)}, s32[128]{0:T(128)}, u32[]{:S(2)}) copy-start(s32[128]{0:T(128)} %ids_ref.3) | copy-start | bytes 1540
  2.2 21.7 %all-to-all-start = ((bf16[32,4,512]{2,1,0:T(4,128)(2,1)}), bf16[32,4,512]{2,1,0:T(4,128)(2,1)S(1)}, u32[]{:S(2)}, u32[]{:S(2)}) async-start(bf16[32,4,512]{2,1,0:T(4,128)(2,1)} %shard_map.77), calls=%async_computation | async-start | bytes 262144 | tf_op jit(solution)/shard_map/all_to_all | solution.py:196
  15.4 19.7 %collective-permute-start = (bf16[2,64,8,128]{3,2,1,0:T(8,128)(2,1)}, bf16[2,64,8,128]{3,2,1,0:T(8,128)(2,1)S(1)}, u32[]{:S(2)}, u32[]{:S(2)}) collective-permute-start(bf16[2,64,8,128]{3,2,1,0:T(8,128)(2,1)} %bitcast.16), channel_id=1, source_target_pairs={{0,2},{2,0},{1,3},{3,1},{4,6},{6,4},{5,7},{7,5},{8,10},{10,8},{9,1... | collective-permute-start | bytes 786440 | tf_op jit(solution)/shard_map/ppermute | solution.py:214
  20.5 50.5 %copy-start = (bf16[512,512]{1,0:T(8,128)(2,1)S(1)}, bf16[512,512]{1,0:T(8,128)(2,1)}, u32[]{:S(2)}) copy-start(bf16[512,512]{1,0:T(8,128)(2,1)} %constant.68.clone.sin_ref) | copy-start | bytes 1572868
  20.5 50.4 %copy-start.1 = (bf16[512,512]{1,0:T(8,128)(2,1)S(1)}, bf16[512,512]{1,0:T(8,128)(2,1)}, u32[]{:S(2)}) copy-start(bf16[512,512]{1,0:T(8,128)(2,1)} %constant.67.clone.cos_ref) | copy-start | bytes 1572868
  24.5 20.2 %all-to-all-start.1 = ((bf16[16,8,128]{2,1,0:T(8,128)(2,1)}), bf16[16,8,128]{2,1,0:T(8,128)(2,1)S(1)}, u32[]{:S(2)}, u32[]{:S(2)}) async-start(bf16[16,8,128]{2,1,0:T(8,128)(2,1)} %shard_map.78), calls=%async_computation.1 | async-start | bytes 65536 | tf_op jit(solution)/shard_map/all_to_all | solution.py:196
  35.1 1.0 copy-start.2
  36.0 0.7 copy-start.4
  46.6 24.4 %all-to-all-start.2 = ((bf16[128,8,256]{2,1,0:T(8,128)(2,1)}), bf16[128,8,256]{2,1,0:T(8,128)(2,1)S(1)}, u32[]{:S(2)}, u32[]{:S(2)}) async-start(bf16[128,8,256]{2,1,0:T(8,128)(2,1)} %bitcast.5), calls=%async_computation.2 | async-start | bytes 1048576 | tf_op jit(solution)/shard_map/all_to_all | solution.py:196
  71.6 6.1 %collective-permute-start.1 = (bf16[2,2,512,128]{3,2,1,0:T(8,128)(2,1)S(1)}, bf16[2,2,512,128]{3,2,1,0:T(8,128)(2,1)S(1)}, u32[]{:S(2)}, u32[]{:S(2)}) collective-permute-start(bf16[2,2,512,128]{3,2,1,0:T(8,128)(2,1)S(1)} %shard_map.82.own_ref), channel_id=1, source_target_pairs={{0,1},{1,0},{2,3},{3,2},{4,5},{5,4},{6,7},{7,6},{8,9},{9,8},{10,11... | collective-permute-start | bytes 1572872 | tf_op jit(solution)/shard_map/ppermute | solution.py:266

commit v10 on v8

--- a/solution.py
+++ b/solution.py
@@ -138,7 +138,7 @@
     cos_rows, sin_rows = (
         jnp.concatenate([ref[pl.ds(start, tile_size), :] for start in starts], axis=0) for ref in (cos_ref, sin_ref)
     )
-    width = 256
+    width = 512
     for at in range(0, size, width):
         part = slice(at, at + width)
         real = dot(field[0], cos_rows[:, part]) + dot(field[1], sin_rows[:, part])

time: 98.5 us -> 98.4 us (level)
  no operation moved by 1% of the time
where the time goes in v10:
time: 98.4 us; the launch traced here: 97.6 us
  starting transfers between devices  38.3 us (39%)
  waiting for transfers between devices  26.2 us (27%)
  blocking collectives  17.7 us (18%)
  Pallas kernels  10.7 us (11%)
  local copies, waits for them, and re-layouts  2.52 us (3%)
  between operations  1.44 us (1%)
    all_to_all x3, starting transfers between devices, exchange(): return lax.all_to_all(x, axes, split_axis=0, concat_axis=0, tiled=True)  29.8 us
    all_to_all x3, waiting for transfers between devices, exchange(): return lax.all_to_all(x, axes, split_axis=0, concat_axis=0, tiled=True)  25.4 us
    all_to_all x1, blocking collectives, exchange(): return lax.all_to_all(x, axes, split_axis=0, concat_axis=0, tiled=True)  17.7 us
    ppermute x1, starting transfers between devices, local(): other = lax.ppermute(wavefield, 'h', swap)  4.36 us
    ppermute x1, starting transfers between devices, local(): beside = lax.ppermute(own, 'c', swap)  4.1 us
    pallas_call x1, Pallas kernels, local(): pl.pallas_call(shift_kernel, out_shape=jax.ShapeDtypeStruct((2, size, siz...  2.74 us
    pallas_call x1, Pallas kernels, local(): pl.pallas_call(step_kernel, out_shape=(jax.ShapeDtypeStruct((2, tile_size...  2.55 us
    unnamed x12, local copies, waits for them, and re-layouts  2.52 us
  transfers between devices with their start and end apart: 5, of which 4 were waited for; matrix products, arithmetic and copies ran while one was open for 0% of the time, Pallas kernels for 5%

profile of v10, /device:TPU:1, one launch (start us, length us, event | category | flops | bytes accessed | tf_op | source)
XLA Modules:
  0.0 97.6 jit_solution(16687939729518827154)
XLA Ops:
  0.6 0.0 copy-start.3
  0.6 0.9 copy-done.3
  1.5 0.0 copy-start.5
  1.5 0.7 shard_map.77
  2.2 13.2 %all-to-all-start = ((bf16[32,4,512]{2,1,0:T(4,128)(2,1)}), bf16[32,4,512]{2,1,0:T(4,128)(2,1)S(1)}, u32[]{:S(2)}, u32[]{:S(2)}) async-start(bf16[32,4,512]{2,1,0:T(4,128)(2,1)} %shard_map.77), calls=%async_computation | async-start | bytes 262144 | tf_op jit(solution)/shard_map/all_to_all | solution.py:193
  15.4 4.4 %collective-permute-start = (bf16[2,64,8,128]{3,2,1,0:T(8,128)(2,1)}, bf16[2,64,8,128]{3,2,1,0:T(8,128)(2,1)S(1)}, u32[]{:S(2)}, u32[]{:S(2)}) collective-permute-start(bf16[2,64,8,128]{3,2,1,0:T(8,128)(2,1)} %bitcast.14), channel_id=1, source_target_pairs={{0,2},{2,0},{1,3},{3,1},{4,6},{6,4},{5,7},{7,5},{8,10},{10,8},{9,1... | collective-permute-start | bytes 786440 | tf_op jit(solution)/shard_map/ppermute | solution.py:211
  20.5 0.0 copy-start
  20.5 0.0 copy-start.1
  20.5 3.4 %all-to-all-done.rows_ref = bf16[32,4,512]{2,1,0:T(4,128)(2,1)S(1)} async-done(((bf16[32,4,512]{2,1,0:T(4,128)(2,1)}), bf16[32,4,512]{2,1,0:T(4,128)(2,1)S(1)}, u32[]{:S(2)}, u32[]{:S(2)}) %all-to-all-start) | async-done | bytes 131104 | tf_op jit(solution)/shard_map/all_to_all | solution.py:193
  23.9 0.6 shard_map.78
  24.5 10.5 %all-to-all-start.1 = ((bf16[16,8,128]{2,1,0:T(8,128)(2,1)}), bf16[16,8,128]{2,1,0:T(8,128)(2,1)S(1)}, u32[]{:S(2)}, u32[]{:S(2)}) async-start(bf16[16,8,128]{2,1,0:T(8,128)(2,1)} %shard_map.78), calls=%async_computation.1 | async-start | bytes 65536 | tf_op jit(solution)/shard_map/all_to_all | solution.py:193
  35.0 0.1 pad_add_fusion.place_ref
  35.1 0.0 collective-permute-done.other_ref
  35.1 0.0 copy-start.2
  35.1 0.9 copy-done.2
  36.1 0.7 copy-done.4
  36.7 0.8 shard_map.79
  37.5 7.3 %all-to-all-done.1.slow_ref = bf16[16,8,128]{2,1,0:T(8,128)(2,1)S(1)} async-done(((bf16[16,8,128]{2,1,0:T(8,128)(2,1)}), bf16[16,8,128]{2,1,0:T(8,128)(2,1)S(1)}, u32[]{:S(2)}, u32[]{:S(2)}) %all-to-all-start.1) | async-done | bytes 32800 | tf_op jit(solution)/shard_map/all_to_all | solution.py:193
  44.7 1.9 %shard_map.80 = bf16[128,8,256]{2,1,0:T(8,128)(2,1)} custom-call(s32[2]{0:T(128)S(1)} %pad_add_fusion.place_ref, bf16[16,8,128]{2,1,0:T(8,128)(2,1)S(1)} %all-to-all-done.1.slow_ref, bf16[2,64,8,128]{3,2,1,0:T(8,128)(2,1)S(1)} %get-tuple-element.9.own_ref, bf16[2,64,8,128]{3,2,1,0:T(8,128)(2,1)S(1)} %get-tuple-element.10.other_ref, ...), custom_call_target="tpu_custom_call" | custom-call | flops 6000000 | bytes 1300000 | tf_op jit(solution)/shard_map/pallas_call | solution.py:231
  46.7 6.2 %all-to-all-start.2 = ((bf16[128,8,256]{2,1,0:T(8,128)(2,1)}), bf16[128,8,256]{2,1,0:T(8,128)(2,1)S(1)}, u32[]{:S(2)}, u32[]{:S(2)}) async-start(bf16[128,8,256]{2,1,0:T(8,128)(2,1)} %shard_map.80), calls=%async_computation.2 | async-start | bytes 1048576 | tf_op jit(solution)/shard_map/all_to_all | solution.py:193
  52.9 0.0 copy-done.5
  52.9 2.7 %shard_map.81.shift_ref = bf16[2,512,512]{2,1,0:T(8,128)(2,1)S(1)} custom-call(s32[1]{0:T(128)} %bitcast.5.slot_ref, s32[128]{0:T(128)S(1)} %copy-done.5), custom_call_target="tpu_custom_call" | custom-call | flops 10000000 | bytes 2100000 | tf_op jit(solution)/shard_map/pallas_call | solution.py:242
  55.6 14.7 %all-to-all-done.2.wave_ref = bf16[128,8,256]{2,1,0:T(8,128)(2,1)S(1)} async-done(((bf16[128,8,256]{2,1,0:T(8,128)(2,1)}), bf16[128,8,256]{2,1,0:T(8,128)(2,1)S(1)}, u32[]{:S(2)}, u32[]{:S(2)}) %all-to-all-start.2) | async-done | bytes 524320 | tf_op jit(solution)/shard_map/all_to_all | solution.py:193
  70.3 0.0 copy-done
  70.3 0.0 copy-done.1
  70.3 0.7 shard_map.82.own_ref
  71.0 4.1 %collective-permute-start.1 = (bf16[2,2,512,128]{3,2,1,0:T(8,128)(2,1)S(1)}, bf16[2,2,512,128]{3,2,1,0:T(8,128)(2,1)S(1)}, u32[]{:S(2)}, u32[]{:S(2)}) collective-permute-start(bf16[2,2,512,128]{3,2,1,0:T(8,128)(2,1)S(1)} %shard_map.82.own_ref), channel_id=1, source_target_pairs={{0,1},{1,0},{2,3},{3,2},{4,5},{5,4},{6,7},{7,6},{8,9},{9,8},{10,11... | collective-permute-start | bytes 1572872 | tf_op jit(solution)/shard_map/ppermute | solution.py:262
  75.2 0.7 shard_map.83.near_ref
  75.9 0.8 collective-permute-done.1.other_ref
  76.7 2.5 %shard_map.84 = (bf16[2,128,512]{2,1,0:T(8,128)(2,1)}, bf16[128,4,128]{2,1,0:T(4,128)(2,1)S(1)}) custom-call(s32[1]{0:T(128)} %bitcast.tile_ref, f32[2,512,512]{2,1,0:T(8,128)S(1)} %shard_map.83.near_ref, bf16[2,2,512,128]{3,2,1,0:T(8,128)(2,1)S(1)} %collective-permute-done.1.other_ref, bf16[512,512]{1,0:T(8,128)(2,1)S(1)} %copy-done.1, ...), custom_call_target="tpu_custom_call" | custom-call | flops 1080000000 | bytes 5600000 | tf_op jit(solution)/shard_map/pallas_call | solution.py:272
  79.2 17.7 %all_to_all.20 = bf16[128,4,128]{2,1,0:T(4,128)(2,1)S(1)} all-to-all(bf16[128,4,128]{2,1,0:T(4,128)(2,1)S(1)} %get-tuple-element.15), channel_id=1, replica_groups=mesh['y4'=2,'y2'=2,'y1'=2,'w'=2,'z4'=2,'z2'=2,'z1'=2,'h'=2,'c'=2] {'z1',..., dimensions={0} | all-to-all | bytes 262144 | tf_op jit(solution)/shard_map/all_to_all | solution.py:193
  96.9 0.7 convert_reduce_fusion
  (1 shorter events, 0.0 us)
Async XLA Ops:
  0.6 0.9 copy-start.3
  1.5 51.3 %copy-start.5 = (s32[128]{0:T(128)S(1)}, s32[128]{0:T(128)}, u32[]{:S(2)}) copy-start(s32[128]{0:T(128)} %ids_ref.3) | copy-start | bytes 1540
  2.2 21.7 %all-to-all-start = ((bf16[32,4,512]{2,1,0:T(4,128)(2,1)}), bf16[32,4,512]{2,1,0:T(4,128)(2,1)S(1)}, u32[]{:S(2)}, u32[]{:S(2)}) async-start(bf16[32,4,512]{2,1,0:T(4,128)(2,1)} %shard_map.77), calls=%async_computation | async-start | bytes 262144 | tf_op jit(solution)/shard_map/all_to_all | solution.py:193
  15.4 19.7 %collective-permute-start = (bf16[2,64,8,128]{3,2,1,0:T(8,128)(2,1)}, bf16[2,64,8,128]{3,2,1,0:T(8,128)(2,1)S(1)}, u32[]{:S(2)}, u32[]{:S(2)}) collective-permute-start(bf16[2,64,8,128]{3,2,1,0:T(8,128)(2,1)} %bitcast.14), channel_id=1, source_target_pairs={{0,2},{2,0},{1,3},{3,1},{4,6},{6,4},{5,7},{7,5},{8,10},{10,8},{9,1... | collective-permute-start | bytes 786440 | tf_op jit(solution)/shard_map/ppermute | solution.py:211
  20.5 49.9 %copy-start = (bf16[512,512]{1,0:T(8,128)(2,1)S(1)}, bf16[512,512]{1,0:T(8,128)(2,1)}, u32[]{:S(2)}) copy-start(bf16[512,512]{1,0:T(8,128)(2,1)} %constant.68.clone.sin_ref) | copy-start | bytes 1572868
  20.5 49.8 %copy-start.1 = (bf16[512,512]{1,0:T(8,128)(2,1)S(1)}, bf16[512,512]{1,0:T(8,128)(2,1)}, u32[]{:S(2)}) copy-start(bf16[512,512]{1,0:T(8,128)(2,1)} %constant.67.clone.cos_ref) | copy-start | bytes 1572868
  24.5 20.2 %all-to-all-start.1 = ((bf16[16,8,128]{2,1,0:T(8,128)(2,1)}), bf16[16,8,128]{2,1,0:T(8,128)(2,1)S(1)}, u32[]{:S(2)}, u32[]{:S(2)}) async-start(bf16[16,8,128]{2,1,0:T(8,128)(2,1)} %shard_map.78), calls=%async_computation.1 | async-start | bytes 65536 | tf_op jit(solution)/shard_map/all_to_all | solution.py:193
  35.1 1.0 copy-start.2
  36.0 0.7 copy-start.4
  46.7 23.6 %all-to-all-start.2 = ((bf16[128,8,256]{2,1,0:T(8,128)(2,1)}), bf16[128,8,256]{2,1,0:T(8,128)(2,1)S(1)}, u32[]{:S(2)}, u32[]{:S(2)}) async-start(bf16[128,8,256]{2,1,0:T(8,128)(2,1)} %shard_map.80), calls=%async_computation.2 | async-start | bytes 1048576 | tf_op jit(solution)/shard_map/all_to_all | solution.py:193
  71.0 5.6 %collective-permute-start.1 = (bf16[2,2,512,128]{3,2,1,0:T(8,128)(2,1)S(1)}, bf16[2,2,512,128]{3,2,1,0:T(8,128)(2,1)S(1)}, u32[]{:S(2)}, u32[]{:S(2)}) collective-permute-start(bf16[2,2,512,128]{3,2,1,0:T(8,128)(2,1)S(1)} %shard_map.82.own_ref), channel_id=1, source_target_pairs={{0,1},{1,0},{2,3},{3,2},{4,5},{5,4},{6,7},{7,6},{8,9},{9,8},{10,11... | collective-permute-start | bytes 1572872 | tf_op jit(solution)/shard_map/ppermute | solution.py:262
